TPU v7x, 256 devices: a whole 4x4x8 slice. The times are simulated.
256 devices in a mesh: gx: 32 (over x, y, core), gy: 8 (over z).
Axes of the slice: x: 4, y: 4, z: 8, core: 2. Of those that a mesh axis runs over, the one named last changes fastest.
Arguments:
- pressure: float32 [512, 512, 512], P('gx', 'gy'), may hold values from -3 to 3
- permeability: float32 [512, 512, 512], P('gx', 'gy'), may hold values from 0.1 to 1
- kernel: float32 [2, 12288, 12288], P(None, 'gx', 'gy'), may hold values from -0.4330127 to 0.4330127
- slip_rate: float32 [12288], P(('gx', 'gy')), may hold values from 0.1 to 1
- aging_state: float32 [12288], P(('gx', 'gy')), may hold values from 0.5 to 5
- normal_stress: float32 [12288], P(('gx', 'gy')), may hold values from 50 to 80
- shear_stress: float32 [12288], P(('gx', 'gy')), may hold values from 33 to 45
- direct_effect: float32 [12288], P(('gx', 'gy')), may hold values from 0.01 to 0.02
- evolution_effect: float32 [12288], P(('gx', 'gy')), may hold values from 0.01 to 0.03
- slip_distance: float32 [12288], P(('gx', 'gy')), may hold values from 0.2 to 1
- tri_owner: int32 [12288, 1], P(('gx', 'gy')), may hold values from 0 to 31; in each aligned block of 48 rows (0 to 47, 48 to 95, ...) at most 3 rows name the same one
- tri_cell: int32 [12288], P(('gx', 'gy')), may hold values from 0 to 524287
Outputs:
- pressure_next: float32 [512, 512, 512], P('gx', 'gy')
- state_next: float32 [12288], P(('gx', 'gy'))
- log_rate: float32 [12288], P(('gx', 'gy'))
Inputs may be any that keep to these rules, and one draw needn't show every extreme that they name: `tri_owner`: at most 3 of the 48 triangles of one device name one owner, and in every draw some owner is named by exactly 3 triangles of some device.
All inputs are finite; a program needn't handle non-finite values.
Results may differ from a plain program's by a relative error of at most 0.000092.
Values sent between devices are 32-bit elements; how exact they have to be, the bound alone decides.
No kernel may reach another device: no remote copies, remote signals or barrier semaphores. Data moves between devices by JAX's collectives and lax.ppermute only.
A program may use at most 64 MiB of HBM per device.

v0:
```python
import jax
import jax.numpy as jnp
from jax import lax
from jax.sharding import Mesh
from jax.sharding import PartitionSpec as P

SWEEPS = 3
GX_GY = ("gx_0", "gx_1", "gx_2", "gy")
GX = ("gx_0", "gx_1", "gx_2")


conductance = 0.15
step_time = 1.0
heal_time = 0.5
friction_ref = 0.6
neighbours = ((1, 0, 0), (-1, 0, 0), (0, 1, 0), (0, -1, 0), (0, 0, 1), (0, 0, -1))


def padded(value, sides, width):
    for axis, dim in sides:
        count, length = (lax.axis_size(axis), value.shape[dim])
        up = [(i, (i + 1) % count) for i in range(count - 1)]
        down = [(j, i) for i, j in up]
        last = lax.slice_in_dim(value, length - width, length, axis=dim)
        leading = lax.slice_in_dim(value, 0, width, axis=dim)
        before = lax.ppermute(last, axis, up)
        after = lax.ppermute(leading, axis, down)
        value = jnp.concatenate([before, value, after], axis=dim)
    return value


def joined_along(pieces, dim):
    pieces = jnp.moveaxis(pieces, 0, dim)
    shape = pieces.shape
    return pieces.reshape(*shape[:dim], shape[dim] * shape[dim + 1], *shape[dim + 2 :])


def all_blocks(value, axes, sequence):
    pieces = value
    for k in sequence:
        pieces = lax.all_gather(pieces, axes[k])
    done = sequence[::-1]
    back = [done.index(k) for k in range(len(axes))]
    pieces = pieces.transpose(*back, *range(len(axes), pieces.ndim))
    return pieces.reshape(-1, *value.shape)


def gather_axes(value, axes, sequence, dim):
    return joined_along(all_blocks(value, axes, sequence), dim)


def cut_along(value, dim, count):
    shape = value.shape
    pieces = value.reshape(*shape[:dim], count, shape[dim] // count, *shape[dim + 1 :])
    return jnp.moveaxis(pieces, dim, 0)


def sent_and_summed(value, axis, dim):
    pieces = cut_along(value, dim, lax.axis_size(axis))
    arrived = lax.all_to_all(pieces, axis, split_axis=0, concat_axis=0, tiled=True)
    return arrived.sum(axis=0)


def shifted(values, step_x, step_y, step_z):
    return values[
        1 + step_x : values.shape[0] - 1 + step_x,
        1 + step_y : values.shape[1] - 1 + step_y,
        1 + step_z : values.shape[2] - 1 + step_z,
    ]


def explicit_step(padded_p, padded_k):
    full_p = jnp.pad(padded_p, ((0, 0), (0, 0), (1, 1)))
    full_k = jnp.pad(padded_k, ((0, 0), (0, 0), (1, 1)))
    centre_p = shifted(full_p, 0, 0, 0)
    centre_k = shifted(full_k, 0, 0, 0)
    flux = jnp.zeros_like(centre_p)
    for offset in neighbours:
        other_p = shifted(full_p, offset[0], offset[1], offset[2])
        other_k = shifted(full_k, offset[0], offset[1], offset[2])
        flux = flux + jnp.sqrt(centre_k * other_k) * (other_p - centre_p)
    return centre_p + conductance * flux


def diffuse(pressure, permeability):
    padded_p, padded_k = (
        padded(pressure, ((GX, 0), ("gy", 1)), SWEEPS),
        padded(permeability, ((GX, 0), ("gy", 1)), SWEEPS),
    )
    for repeat in range(SWEEPS):
        padded_p = explicit_step(padded_p, padded_k)
        padded_k = padded_k[1:-1, 1:-1]
    return padded_p


def tractions(kernel, slip_rate):
    gathered = gather_axes(slip_rate, GX_GY, (0, 1, 3, 2), 0)
    column_count = kernel.shape[2]
    offset = lax.axis_index("gy") * column_count
    segment = lax.dynamic_slice_in_dim(gathered, offset, column_count, 0)
    partial_value = jnp.dot(
        kernel.reshape(-1, column_count), segment, precision=lax.Precision.HIGHEST
    ).reshape(2, kernel.shape[1])
    return sent_and_summed(partial_value, "gy", 1)


def fault_pressure_of(pressure_field, tri_owner, tri_cell):
    owners = tri_owner[:, 0]
    tri_count = owners.shape[0]
    groups = lax.axis_size(GX)
    capacity = max(2, 2 * tri_count // groups)
    same_owner = owners[:, None] == owners[None, :]
    indices = jnp.arange(tri_count, dtype=jnp.int32)
    earlier = indices[None, :] < indices[:, None]
    slot_rank = jnp.sum(jnp.logical_and(same_owner, earlier), axis=1)
    slot_index = owners * capacity + slot_rank
    matches = slot_index[:, None] == jnp.arange(groups * capacity, dtype=jnp.int32)[None, :]
    requests = jnp.sum(jnp.where(matches, tri_cell[:, None], 0), axis=0).reshape(groups, capacity)
    flat_field = pressure_field.reshape(-1)
    values = jnp.take(
        flat_field, lax.all_to_all(requests, GX, split_axis=0, concat_axis=0, tiled=True), axis=0
    )
    answers = lax.all_to_all(values, GX, split_axis=0, concat_axis=0, tiled=True)
    return jnp.sum(jnp.where(matches, answers.reshape(-1)[None, :], 0.0), axis=1)


def local(
    pressure,
    permeability,
    kernel,
    slip_rate,
    aging_state,
    normal_stress,
    shear_stress,
    direct_effect,
    evolution_effect,
    slip_distance,
    tri_owner,
    tri_cell,
):
    pressure_field = diffuse(pressure, permeability)
    rates = tractions(kernel, slip_rate)
    fault_pressure = fault_pressure_of(pressure_field, tri_owner, tri_cell)
    shear = shear_stress + step_time * rates[0]
    effective = normal_stress + step_time * rates[1] - fault_pressure
    ratio = slip_distance / slip_rate
    state_next = ratio + (aging_state - ratio) * jnp.exp(-heal_time / ratio)
    log_rate = (
        shear / effective - friction_ref - evolution_effect * jnp.log(state_next / slip_distance)
    ) / direct_effect
    return (pressure_field, state_next, log_rate)


def solution(mesh):
    split = Mesh(mesh.devices.reshape(4, 4, 2, mesh.shape["gy"]), ("gx_0", "gx_1", "gx_2", "gy"))
    placed = (
        P(GX, "gy", None),
        P(GX, "gy", None),
        P(None, GX, "gy"),
        P(GX_GY),
        P(GX_GY),
        P(GX_GY),
        P(GX_GY),
        P(GX_GY),
        P(GX_GY),
        P(GX_GY),
        P(GX_GY, None),
        P(GX_GY),
    )
    return jax.shard_map(
        local,
        mesh=split,
        in_specs=placed,
        out_specs=(P(GX, "gy", None), P(GX_GY), P(GX_GY)),
        check_vma=False,
    )
```

profile of v0, /device:TPU:1, one launch (start us, length us, event | category | flops | bytes accessed | tf_op | source)
XLA Modules:
  0.0 173.3 jit_solution(11511444369471891663)
XLA Ops:
  0.6 0.0 copy-start.21
  0.7 2.1 %fusion.86 = (f32[3,64,512]{2,1,0:T(8,128)}, f32[3,64,512]{2,1,0:T(8,128)}) fusion(f32[16,64,512]{2,1,0:T(8,128)} %param.13), kind=kLoop, calls=%fused_computation.150 | loop fusion | bytes 1572864 | tf_op jit(solution)/shard_map/slice | solution.py:25
  2.8 4.6 %collective-permute-start.4 = (f32[3,64,512]{2,1,0:T(8,128)}, f32[3,64,512]{2,1,0:T(8,128)S(1)}, u32[]{:S(2)}, u32[]{:S(2)}) collective-permute-start(f32[3,64,512]{2,1,0:T(8,128)} %get-tuple-element.16), channel_id=1, source_target_pairs={{0,8},{8,16},{16,24},{24,32},{32,40},{40,48},{48,56},{56,64},{64,7... | collective-permute-start | bytes 1179656 | tf_op jit(solution)/shard_map/ppermute | solution.py:26
  7.3 1.9 %collective-permute-start.5 = (f32[3,64,512]{2,1,0:T(8,128)}, f32[3,64,512]{2,1,0:T(8,128)S(1)}, u32[]{:S(2)}, u32[]{:S(2)}) collective-permute-start(f32[3,64,512]{2,1,0:T(8,128)} %get-tuple-element.15), channel_id=1, source_target_pairs={{8,0},{16,8},{24,16},{32,24},{40,32},{48,40},{56,48},{64,56},{72,6... | collective-permute-start | bytes 1179656 | tf_op jit(solution)/shard_map/ppermute | solution.py:27
  9.3 2.1 %fusion.85 = (f32[3,64,512]{2,1,0:T(8,128)}, f32[3,64,512]{2,1,0:T(8,128)}) fusion(f32[16,64,512]{2,1,0:T(8,128)} %param.12), kind=kLoop, calls=%fused_computation.149 | loop fusion | bytes 1572864 | tf_op jit(solution)/shard_map/slice | solution.py:25
  11.3 3.6 %collective-permute-start = (f32[3,64,512]{2,1,0:T(8,128)}, f32[3,64,512]{2,1,0:T(8,128)}, u32[]{:S(2)}, u32[]{:S(2)}) collective-permute-start(f32[3,64,512]{2,1,0:T(8,128)} %get-tuple-element.14), channel_id=1, source_target_pairs={{0,8},{8,16},{16,24},{24,32},{32,40},{40,48},{48,56},{56,64},{64,7... | collective-permute-start | bytes 1179656 | tf_op jit(solution)/shard_map/ppermute | solution.py:26
  15.0 1.9 %collective-permute-start.1 = (f32[3,64,512]{2,1,0:T(8,128)}, f32[3,64,512]{2,1,0:T(8,128)S(1)}, u32[]{:S(2)}, u32[]{:S(2)}) collective-permute-start(f32[3,64,512]{2,1,0:T(8,128)} %get-tuple-element.13), channel_id=1, source_target_pairs={{8,0},{16,8},{24,16},{32,24},{40,32},{48,40},{56,48},{64,56},{72,6... | collective-permute-start | bytes 1179656 | tf_op jit(solution)/shard_map/ppermute | solution.py:27
  16.9 0.2 convert_reduce_fusion
  17.1 0.1 select_reduce_fusion.1
  17.2 0.7 all_to_all.16
  17.9 9.2 %all-to-all-start.1 = ((s32[32,1,3]{2,1,0:T(1,128)}), s32[32,1,3]{2,1,0:T(1,128)S(1)}, u32[]{:S(2)}, u32[]{:S(2)}) async-start(s32[32,1,3]{2,1,0:T(1,128)} %bitcast.13), calls=%async_computation.1 | async-start | bytes 32768 | tf_op jit(solution)/shard_map/all_to_all | solution.py:121
  27.2 0.6 dynamic-slice
  28.4 0.2 dynamic-update-slice
  28.7 8.6 %all-reduce.6 = f32[192]{0:T(256)S(1)} all-reduce(f32[192]{0:T(256)S(1)} %dynamic-update-slice), channel_id=2, replica_groups=mesh['gx_0'=4,'gx_1'=4,'gx_2'=2,'gy'=8] {'gx_0'}, use_global_device_ids=true, to_apply=%add.6 | all-reduce | flops 192 | bytes 1536
  37.3 0.1 reshape.76
  37.4 8.4 %all-gather.4 = f32[4,4,48]{2,1,0:T(4,128)S(1)} all-gather(f32[1,4,48]{2,1,0:T(4,128)S(1)} %reshape.76), channel_id=3, replica_groups=mesh['gx_0'=4,'gx_1'=4,'gx_2'=2,'gy'=8] {'gx_1'}, dimensions={0}, use_global_device_ids=true | all-gather | bytes 3840 | tf_op jit(solution)/shard_map/all_gather | solution.py:41
  45.8 22.1 %all-gather.2 = f32[32,4,48]{2,1,0:T(4,128)S(1)} all-gather(f32[4,4,48]{2,1,0:T(4,128)S(1)} %all-gather.4), channel_id=4, replica_groups=mesh['gx_0'=4,'gx_1'=4,'gx_2'=2,'gy'=8] {'gy'}, dimensions={0}, use_global_device_ids=true | all-gather | bytes 27648 | tf_op jit(solution)/shard_map/all_gather | solution.py:41
  67.9 12.6 %all-gather.3 = f32[16,4,4,48]{3,1,0,2:T(4,128)S(1)} all-gather(f32[8,4,4,48]{3,1,0,2:T(4,128)S(1)} %bitcast.55), channel_id=5, replica_groups=mesh['gx_0'=4,'gx_1'=4,'gx_2'=2,'gy'=8] {'gx_2'}, dimensions={0}, use_global_device_ids=true | all-gather | bytes 73728 | tf_op jit(solution)/shard_map/all_gather | solution.py:41
  80.5 0.1 reshape_reshape.4
  80.6 0.1 dynamic_slice.3
  80.7 8.7 %fusion.78 = f32[1,2,8,48]{3,0,2,1:T(1,128)S(1)} fusion(f32[2,8,48,1536]{3,2,1,0:T(8,128)} %bitcast.52, f32[1536,1,1,1]{0,1,2,3:T(1,128)S(1)} %reshape.82), kind=kOutput, calls=%fused_computation.135 | convolution fusion | flops 14155776 | bytes 4727808 | tf_op jit(solution)/shard_map/dot_general | solution.py:101
  89.5 0.6 copy.46
  90.1 4.6 %all-to-all-start = ((f32[8,2,48]{2,1,0:T(2,128)}), f32[8,2,48]{2,1,0:T(2,128)S(1)}, u32[]{:S(2)}, u32[]{:S(2)}) async-start(f32[8,2,48]{2,1,0:T(2,128)} %bitcast.49), calls=%async_computation | async-start | bytes 16384 | tf_op jit(solution)/shard_map/all_to_all | solution.py:60
  94.6 0.1 copy.37
  94.7 0.1 copy.38
  94.8 0.1 reshape.61
  95.0 0.0 copy-start.5
  95.0 0.2 constant_dynamic-update-slice_fusion.4
  95.2 0.0 copy-start.10
  95.3 0.4 copy-done.8
  95.7 0.1 fusion.84
  95.8 3.5 %collective-permute-start.6 = (f32[22,3,512]{2,1,0:T(4,128)S(1)}, f32[22,3,512]{2,1,0:T(4,128)S(1)}, u32[]{:S(2)}, u32[]{:S(2)}) collective-permute-start(f32[22,3,512]{2,1,0:T(4,128)S(1)} %get-tuple-element.11), channel_id=1, source_target_pairs={{0,1},{1,2},{2,3},{3,4},{4,5},{5,6},{6,7},{8,9},{9,10},{10,11},{11... | collective-permute-start | bytes 405512 | tf_op jit(solution)/shard_map/ppermute | solution.py:26
  99.3 1.3 collective-permute-start.7
  100.6 1.0 constant_dynamic-update-slice_fusion.2
  101.7 0.2 constant_dynamic-update-slice_fusion.1
  101.9 0.1 fusion.83
  102.0 4.0 %collective-permute-start.2 = (f32[22,3,512]{2,1,0:T(4,128)S(1)}, f32[22,3,512]{2,1,0:T(4,128)S(1)}, u32[]{:S(2)}, u32[]{:S(2)}) collective-permute-start(f32[22,3,512]{2,1,0:T(4,128)S(1)} %get-tuple-element.9), channel_id=1, source_target_pairs={{0,1},{1,2},{2,3},{3,4},{4,5},{5,6},{6,7},{8,9},{9,10},{10,11},{11... | collective-permute-start | bytes 405512 | tf_op jit(solution)/shard_map/ppermute | solution.py:26
  106.0 1.5 collective-permute-start.3
  107.5 0.5 pad_maximum_fusion.1
  108.0 0.2 copy-done.6
  108.2 0.2 collective-permute-done.2
  108.4 3.8 %collective-permute-done.3 = f32[22,3,512]{2,1,0:T(4,128)S(1)} collective-permute-done((f32[22,3,512]{2,1,0:T(4,128)S(1)}, f32[22,3,512]{2,1,0:T(4,128)S(1)}, u32[]{:S(2)}, u32[]{:S(2)}) %collective-permute-start.3) | collective-permute-done | bytes 135200 | tf_op jit(solution)/shard_map/ppermute | solution.py:27
  112.2 0.4 pad_maximum_fusion
  112.7 11.8 %fusion.6 = (f32[20,68,512]{2,1,0:T(8,128)}, f32[20,68,512]{2,1,0:T(8,128)}) fusion(f32[22,70,512]{2,1,0:T(8,128)S(1)} %pad_maximum_fusion.1, f32[22,70,512]{2,1,0:T(8,128)S(1)} %pad_maximum_fusion), kind=kLoop, calls=%fused_computation.25 | loop fusion | flops 17408000 | bytes 41549824 | tf_op jit(solution)/shard_map/add | solution.py:82
  124.5 0.0 copy-start.11
  124.5 18.3 %fusion.31 = (f32[18,66,512]{2,1,0:T(8,128)S(1)}, f32[18,66,512]{2,1,0:T(8,128)S(1)}) fusion(f32[22,3,512]{2,1,0:T(4,128)S(1)} %collective-permute-done.6, f32[22,64,512]{2,1,0:T(8,128)} %copy-done, f32[22,3,512]{2,1,0:T(4,128)} %copy-done.6, f32[20,68,512]{2,1,0:T(8,128)} %get-tuple-element.8, f32[20,68,512]{2,1,0:T(8,128)} %get-tuple-element.7, ...), kind=kLoop, calls=%fused_computation.58 | loop fusion | flops 16422912 | bytes 34533376 | tf_op jit(solution)/shard_map/add | solution.py:82
  142.9 10.9 %fusion.56 = f32[16,64,512]{2,1,0:T(8,128)S(1)} fusion(f32[16,64,512]{2,1,0:T(8,128)S(1)} %copy-done.3, f32[18,66,512]{2,1,0:T(8,128)S(1)} %get-tuple-element.6, f32[18,66,512]{2,1,0:T(8,128)S(1)} %get-tuple-element.5, f32[22,64,512]{2,1,0:T(8,128)S(1)} %copy-done.1, f32[22,3,512]{2,1,0:T(4,128)S(1)} %collective-permute-done.6, ...), kind=kLoop, calls=%fused_computation.89 | loop fusion | flops 15204352 | bytes 24018944 | tf_op jit(solution)/shard_map/add | solution.py:82
  153.7 0.0 copy-start.4
  153.7 1.3 copy-done.4
  155.1 0.5 copy.42
  155.6 0.0 copy-start.12
  155.6 0.0 copy-start.13
  155.6 0.0 copy-start.14
  155.6 0.0 copy-start.16
  155.7 1.1 gather_fusion
  156.8 0.1 gather.7
  156.9 0.6 and_select_fusion
  157.6 6.7 %all-to-all-start.2 = ((f32[32,1,3]{2,1,0:T(1,128)}), f32[32,1,3]{2,1,0:T(1,128)S(1)}, u32[]{:S(2)}, u32[]{:S(2)}) async-start(f32[32,1,3]{2,1,0:T(1,128)} %bitcast.18), calls=%async_computation.2 | async-start | bytes 32768 | tf_op jit(solution)/shard_map/all_to_all | solution.py:123
  164.3 6.9 %all-to-all-done.2 = f32[32,1,3]{2,1,0:T(1,128)S(1)} async-done(((f32[32,1,3]{2,1,0:T(1,128)}), f32[32,1,3]{2,1,0:T(1,128)S(1)}, u32[]{:S(2)}, u32[]{:S(2)}) %all-to-all-start.2) | async-done | bytes 416 | tf_op jit(solution)/shard_map/all_to_all | solution.py:123
  171.2 0.5 broadcast.56
  171.7 0.7 reduce.3
  172.4 0.1 broadcast_in_dim.40
  172.5 0.2 select_reduce_fusion
  172.7 0.5 subtract_divide_fusion
  (51 shorter events, 0.2 us)
Async XLA Ops:
  0.6 26.5 %copy-start.21 = (u32[256]{0:T(256)S(1)}, u32[256]{0:T(256)}, u32[]{:S(2)}) copy-start(u32[256]{0:T(256)} %constant.64) | copy-start | bytes 3076
  0.6 16.3 %copy-start.19 = (s32[48,1]{0,1:T(1,128)S(1)}, s32[48,1]{0,1:T(1,128)}, u32[]{:S(2)}) copy-start(s32[48,1]{0,1:T(1,128)} %param.22) | copy-start | bytes 580
  0.7 16.5 %copy-start.20 = (s32[48]{0:T(128)S(1)}, s32[48]{0:T(128)}, u32[]{:S(2)}) copy-start(s32[48]{0:T(128)} %param.23) | copy-start | bytes 580
  0.7 27.8 %copy-start.15 = (f32[48]{0:T(128)S(1)}, f32[48]{0:T(128)}, u32[]{:S(2)}) copy-start(f32[48]{0:T(128)} %param.15) | copy-start | bytes 580
  2.8 92.2 %collective-permute-start.4 = (f32[3,64,512]{2,1,0:T(8,128)}, f32[3,64,512]{2,1,0:T(8,128)S(1)}, u32[]{:S(2)}, u32[]{:S(2)}) collective-permute-start(f32[3,64,512]{2,1,0:T(8,128)} %get-tuple-element.16), channel_id=1, source_target_pairs={{0,8},{8,16},{16,24},{24,32},{32,40},{40,48},{48,56},{56,64},{64,7... | collective-permute-start | bytes 1179656 | tf_op jit(solution)/shard_map/ppermute | solution.py:26
  7.3 87.9 %collective-permute-start.5 = (f32[3,64,512]{2,1,0:T(8,128)}, f32[3,64,512]{2,1,0:T(8,128)S(1)}, u32[]{:S(2)}, u32[]{:S(2)}) collective-permute-start(f32[3,64,512]{2,1,0:T(8,128)} %get-tuple-element.15), channel_id=1, source_target_pairs={{8,0},{16,8},{24,16},{32,24},{40,32},{48,40},{56,48},{64,56},{72,6... | collective-permute-start | bytes 1179656 | tf_op jit(solution)/shard_map/ppermute | solution.py:27
  11.3 89.3 %collective-permute-start = (f32[3,64,512]{2,1,0:T(8,128)}, f32[3,64,512]{2,1,0:T(8,128)}, u32[]{:S(2)}, u32[]{:S(2)}) collective-permute-start(f32[3,64,512]{2,1,0:T(8,128)} %get-tuple-element.14), channel_id=1, source_target_pairs={{0,8},{8,16},{16,24},{24,32},{32,40},{40,48},{48,56},{56,64},{64,7... | collective-permute-start | bytes 1179656 | tf_op jit(solution)/shard_map/ppermute | solution.py:26
  15.0 86.9 %collective-permute-start.1 = (f32[3,64,512]{2,1,0:T(8,128)}, f32[3,64,512]{2,1,0:T(8,128)S(1)}, u32[]{:S(2)}, u32[]{:S(2)}) collective-permute-start(f32[3,64,512]{2,1,0:T(8,128)} %get-tuple-element.13), channel_id=1, source_target_pairs={{8,0},{16,8},{24,16},{32,24},{40,32},{48,40},{56,48},{64,56},{72,6... | collective-permute-start | bytes 1179656 | tf_op jit(solution)/shard_map/ppermute | solution.py:27
  17.9 72.1 %all-to-all-start.1 = ((s32[32,1,3]{2,1,0:T(1,128)}), s32[32,1,3]{2,1,0:T(1,128)S(1)}, u32[]{:S(2)}, u32[]{:S(2)}) async-start(s32[32,1,3]{2,1,0:T(1,128)} %bitcast.13), calls=%async_computation.1 | async-start | bytes 32768 | tf_op jit(solution)/shard_map/all_to_all | solution.py:121
  80.7 14.3 %copy-start.2 = (f32[16,64,512]{2,1,0:T(8,128)S(1)}, f32[16,64,512]{2,1,0:T(8,128)}, u32[]{:S(2)}) copy-start(f32[16,64,512]{2,1,0:T(8,128)} %param.13) | copy-start | bytes 6291460
  90.1 67.5 %all-to-all-start = ((f32[8,2,48]{2,1,0:T(2,128)}), f32[8,2,48]{2,1,0:T(2,128)S(1)}, u32[]{:S(2)}, u32[]{:S(2)}) async-start(f32[8,2,48]{2,1,0:T(2,128)} %bitcast.49), calls=%async_computation | async-start | bytes 16384 | tf_op jit(solution)/shard_map/all_to_all | solution.py:60
  94.9 0.8 copy-start.8
  95.0 6.6 %copy-start.5 = (f32[16,64,512]{2,1,0:T(8,128)S(1)}, f32[16,64,512]{2,1,0:T(8,128)}, u32[]{:S(2)}) copy-start(f32[16,64,512]{2,1,0:T(8,128)} %param.12) | copy-start | bytes 6291460
  95.2 6.6 %copy-start.10 = (f32[3,64,512]{2,1,0:T(8,128)}, f32[3,64,512]{2,1,0:T(8,128)S(1)}, u32[]{:S(2)}) copy-start(f32[3,64,512]{2,1,0:T(8,128)S(1)} %collective-permute-done.5) | copy-start | bytes 1179652
  95.7 11.8 %copy-start = (f32[22,64,512]{2,1,0:T(8,128)}, f32[22,64,512]{2,1,0:T(8,128)S(1)}, u32[]{:S(2)}) copy-start(f32[22,64,512]{2,1,0:T(8,128)S(1)} %constant_dynamic-update-slice_fusion.3) | copy-start | bytes 8650756
  95.8 11.7 %collective-permute-start.6 = (f32[22,3,512]{2,1,0:T(4,128)S(1)}, f32[22,3,512]{2,1,0:T(4,128)S(1)}, u32[]{:S(2)}, u32[]{:S(2)}) collective-permute-start(f32[22,3,512]{2,1,0:T(4,128)S(1)} %get-tuple-element.11), channel_id=1, source_target_pairs={{0,1},{1,2},{2,3},{3,4},{4,5},{5,6},{6,7},{8,9},{9,10},{10,11},{11... | collective-permute-start | bytes 405512 | tf_op jit(solution)/shard_map/ppermute | solution.py:26
  99.3 8.2 %collective-permute-start.7 = (f32[22,3,512]{2,1,0:T(4,128)S(1)}, f32[22,3,512]{2,1,0:T(4,128)S(1)}, u32[]{:S(2)}, u32[]{:S(2)}) collective-permute-start(f32[22,3,512]{2,1,0:T(4,128)S(1)} %get-tuple-element.12), channel_id=1, source_target_pairs={{1,0},{2,1},{3,2},{4,3},{5,4},{6,5},{7,6},{9,8},{10,9},{11,10},{12... | collective-permute-start | bytes 405512 | tf_op jit(solution)/shard_map/ppermute | solution.py:27
  102.0 6.4 %collective-permute-start.2 = (f32[22,3,512]{2,1,0:T(4,128)S(1)}, f32[22,3,512]{2,1,0:T(4,128)S(1)}, u32[]{:S(2)}, u32[]{:S(2)}) collective-permute-start(f32[22,3,512]{2,1,0:T(4,128)S(1)} %get-tuple-element.9), channel_id=1, source_target_pairs={{0,1},{1,2},{2,3},{3,4},{4,5},{5,6},{6,7},{8,9},{9,10},{10,11},{11... | collective-permute-start | bytes 405512 | tf_op jit(solution)/shard_map/ppermute | solution.py:26
  106.0 6.2 %collective-permute-start.3 = (f32[22,3,512]{2,1,0:T(4,128)S(1)}, f32[22,3,512]{2,1,0:T(4,128)S(1)}, u32[]{:S(2)}, u32[]{:S(2)}) collective-permute-start(f32[22,3,512]{2,1,0:T(4,128)S(1)} %get-tuple-element.10), channel_id=1, source_target_pairs={{1,0},{2,1},{3,2},{4,3},{5,4},{6,5},{7,6},{9,8},{10,9},{11,10},{12... | collective-permute-start | bytes 405512 | tf_op jit(solution)/shard_map/ppermute | solution.py:27
  107.5 0.7 copy-start.6
  124.5 18.3 %copy-start.1 = (f32[22,64,512]{2,1,0:T(8,128)S(1)}, f32[22,64,512]{2,1,0:T(8,128)}, u32[]{:S(2)}) copy-start(f32[22,64,512]{2,1,0:T(8,128)} %copy-done) | copy-start | bytes 8650756
  124.5 18.3 %copy-start.3 = (f32[16,64,512]{2,1,0:T(8,128)S(1)}, f32[16,64,512]{2,1,0:T(8,128)}, u32[]{:S(2)}) copy-start(f32[16,64,512]{2,1,0:T(8,128)} %param.13) | copy-start | bytes 6291460
  124.5 18.4 %copy-start.7 = (f32[22,3,512]{2,1,0:T(4,128)S(1)}, f32[22,3,512]{2,1,0:T(4,128)}, u32[]{:S(2)}) copy-start(f32[22,3,512]{2,1,0:T(4,128)} %copy-done.6) | copy-start | bytes 405508
  124.5 18.4 %copy-start.9 = (f32[3,64,512]{2,1,0:T(8,128)S(1)}, f32[3,64,512]{2,1,0:T(8,128)}, u32[]{:S(2)}) copy-start(f32[3,64,512]{2,1,0:T(8,128)} %copy-done.8) | copy-start | bytes 1179652
  124.5 18.4 %copy-start.11 = (f32[3,64,512]{2,1,0:T(8,128)S(1)}, f32[3,64,512]{2,1,0:T(8,128)}, u32[]{:S(2)}) copy-start(f32[3,64,512]{2,1,0:T(8,128)} %copy-done.10) | copy-start | bytes 1179652
  153.7 1.3 copy-start.4
  155.6 17.1 %copy-start.12 = (f32[48]{0:T(128)S(1)}, f32[48]{0:T(128)}, u32[]{:S(2)}) copy-start(f32[48]{0:T(128)} %param.19) | copy-start | bytes 580
  155.6 17.1 %copy-start.13 = (f32[48]{0:T(128)S(1)}, f32[48]{0:T(128)}, u32[]{:S(2)}) copy-start(f32[48]{0:T(128)} %param.20) | copy-start | bytes 580
  155.6 17.1 %copy-start.14 = (f32[48]{0:T(128)S(1)}, f32[48]{0:T(128)}, u32[]{:S(2)}) copy-start(f32[48]{0:T(128)} %param.17) | copy-start | bytes 580
  155.6 17.1 %copy-start.16 = (f32[48]{0:T(128)S(1)}, f32[48]{0:T(128)}, u32[]{:S(2)}) copy-start(f32[48]{0:T(128)} %param.18) | copy-start | bytes 580
  155.6 17.1 %copy-start.17 = (f32[48]{0:T(128)S(1)}, f32[48]{0:T(128)}, u32[]{:S(2)}) copy-start(f32[48]{0:T(128)} %param.21) | copy-start | bytes 580
  155.7 17.1 %copy-start.18 = (f32[48]{0:T(128)S(1)}, f32[48]{0:T(128)}, u32[]{:S(2)}) copy-start(f32[48]{0:T(128)} %param.16) | copy-start | bytes 580
  157.6 13.6 %all-to-all-start.2 = ((f32[32,1,3]{2,1,0:T(1,128)}), f32[32,1,3]{2,1,0:T(1,128)S(1)}, u32[]{:S(2)}, u32[]{:S(2)}) async-start(f32[32,1,3]{2,1,0:T(1,128)} %bitcast.18), calls=%async_computation.2 | async-start | bytes 32768 | tf_op jit(solution)/shard_map/all_to_all | solution.py:123
where the time goes:
time: 175 us; the launch traced here: 173 us
  blocking collectives  51.7 us (30%)
  other arithmetic  44.2 us (25%)
  starting transfers between devices  42.8 us (24%)
  local copies, waits for them, and re-layouts  12.9 us (7%)
  waiting for transfers between devices  11 us (6%)
  matrix products  8.75 us (5%)
  between operations  1.86 us (1%)
    all_gather x3, blocking collectives, all_blocks(): pieces = lax.all_gather(pieces, axes[k])  43.1 us
    add x3, other arithmetic, explicit_step(): return centre_p + conductance * flux  41 us
    ppermute x4, starting transfers between devices, padded(): before = lax.ppermute(last, axis, up)  15.7 us
    all_to_all x1, starting transfers between devices, fault_pressure_of(): lax.all_to_all(requests, GX, split_axis=0, concat_axis=0, tiled=True)  9.22 us
    dot_general x1, matrix products, tractions(): jnp.dot(kernel.reshape(-1, column_count), segment, precision=lax.Precisio...  8.75 us
    unnamed x1, blocking collectives  8.6 us
    all_to_all x1, waiting for transfers between devices, fault_pressure_of(): lax.all_to_all(values, GX, split_axis=0, concat_axis=0, tiled=True)  6.92 us
    all_to_all x1, starting transfers between devices, fault_pressure_of(): lax.all_to_all(values, GX, split_axis=0, concat_axis=0, tiled=True)  6.69 us
  transfers between devices with their start and end apart: 11, of which 3 were waited for; matrix products, arithmetic and copies ran while one was open for 34% of the time, Pallas kernels for 0%

commit v1 on v0

v1 whole, which is shorter than its diff:
```python
import jax
import jax.numpy as jnp
from jax import lax
from jax.experimental import pallas as pl
from jax.experimental.pallas import tpu as pltpu
from jax.sharding import PartitionSpec as P

NGX, NGY = 32, 8
CX, CY, NZ, TRI = 16, 64, 512, 48
HALO = 3
ROWS = 80
LANES = 128
CHUNKS = NZ // LANES
conductance = 0.15
step_time = 1.0
heal_time = 0.5
friction_ref = 0.6
F32 = jnp.float32
VMEM = pltpu.VMEM
ANY = pl.ANY

X_MOVE = (2, 1, 2, 1, 0, 3, 0, 3)
Y_MOVE = (1, 1, 0, 0, 0, 0, 1, 1)
X_CODE = sum(v << (2 * i) for i, v in enumerate(X_MOVE))
Y_CODE = sum(v << i for i, v in enumerate(Y_MOVE))


def landing(group, other):
    delta = (other - group) & 7
    x = ((group >> 1) + ((X_CODE >> (2 * delta)) & 3)) & 3
    y = (group & 1) ^ ((Y_CODE >> delta) & 1)
    return 2 * x + y


SLIP_MOVES = [
    ((4 * g + r) * NGY + j, (4 * landing(g, j) + r) * NGY + g) for g in range(8) for r in range(4) for j in range(NGY)
]
X_UP = [(i, i + 1) for i in range(NGX - 1)]
X_DOWN = [(j, i) for i, j in X_UP]
Y_UP = [(i, i + 1) for i in range(NGY - 1)]
Y_DOWN = [(j, i) for i, j in Y_UP]


def spec(space=VMEM):
    return pl.BlockSpec(memory_space=space)


def shape(*dims, dtype=F32):
    return jax.ShapeDtypeStruct(dims, dtype)


def pack_kernel(p, k, x_up, x_down, y_up, y_down, tiles, sems):
    copies = [
        pltpu.make_async_copy(src, dst, sems.at[n])
        for n, (src, dst) in enumerate(
            (
                (p.at[:, pl.ds(CY - 8, 8), :], tiles.at[0]),
                (k.at[:, pl.ds(CY - 8, 8), :], tiles.at[1]),
                (p.at[:, pl.ds(0, 8), :], tiles.at[2]),
                (k.at[:, pl.ds(0, 8), :], tiles.at[3]),
                (p.at[pl.ds(CX - HALO, HALO)], x_up.at[pl.ds(0, HALO)]),
                (k.at[pl.ds(CX - HALO, HALO)], x_up.at[pl.ds(HALO, HALO)]),
                (p.at[pl.ds(0, HALO)], x_down.at[pl.ds(0, HALO)]),
                (k.at[pl.ds(0, HALO)], x_down.at[pl.ds(HALO, HALO)]),
            )
        )
    ]
    for copy in copies:
        copy.start()
    for copy in copies[:4]:
        copy.wait()
    row = lax.broadcasted_iota(jnp.int32, (8, NZ), 0)

    def plane(x, carry):
        y_up[x] = jnp.where(row >= 5, tiles[0, x], pltpu.roll(tiles[1, x], 3, 0))
        y_down[x] = jnp.where(row < 3, tiles[2, x], pltpu.roll(tiles[3, x], 5, 0))
        return carry

    lax.fori_loop(0, CX, plane, 0)
    for copy in copies[4:]:
        copy.wait()


def pack(p, k):
    return pl.pallas_call(
        pack_kernel,
        out_shape=(
            shape(2 * HALO, CY, NZ),
            shape(2 * HALO, CY, NZ),
            shape(CX, 8, NZ),
            shape(CX, 8, NZ),
        ),
        in_specs=[spec(ANY)] * 2,
        out_specs=(spec(ANY), spec(ANY), spec(), spec()),
        scratch_shapes=[VMEM((4, CX, 8, NZ), F32), pltpu.SemaphoreType.DMA((8,))],
        compiler_params=pltpu.CompilerParams(vmem_limit_bytes=8 << 20),
        name="pack",
    )(p, k)


def rank_row(owner_row, owner_column):
    same = owner_column == owner_row
    first = lax.broadcasted_iota(jnp.int32, (TRI, TRI), 0)
    second = lax.broadcasted_iota(jnp.int32, (TRI, TRI), 1)
    hits = jnp.where(jnp.logical_and(same, first < second), 1.0, 0.0)
    return jnp.sum(hits, axis=0, keepdims=True)


def request_kernel(owner_row, owner_column, cell_row, out):
    owners = owner_row[...]
    rank = rank_row(owners, owner_column[...])
    cells = cell_row[...].astype(F32)
    lane = lax.broadcasted_iota(jnp.int32, (NGX, LANES), 1)
    named = lax.broadcasted_iota(jnp.int32, (NGX, TRI), 0) == owners
    value = jnp.zeros((NGX, LANES), F32)
    for c in range(3):
        asked = jnp.where(jnp.logical_and(named, rank == float(c)), cells, 0.0)
        value = jnp.where(lane == TRI + c, jnp.sum(asked, axis=1, keepdims=True), value)
    out[...] = value


def requests_of(owner_row, owner_column, cell_row):
    return pl.pallas_call(
        request_kernel,
        out_shape=shape(NGX, LANES),
        in_specs=[spec()] * 3,
        out_specs=spec(),
        name="requests",
    )(owner_row, owner_column, cell_row)


def rates_kernel(arrived, kernel, out, cells, acc):
    gy = lax.axis_index("gy")
    lane = lax.broadcasted_iota(jnp.int32, (1, LANES), 1)
    chunks = [jnp.zeros((1, LANES), F32) for _ in range(12)]
    for j in range(NGY):
        spot = landing(gy, j)
        for r in range(4):
            start = (r * NGY + j) * TRI
            chunk, offset = divmod(start, LANES)
            row = pltpu.roll(arrived[pl.ds(4 * spot + r, 1), :], offset, 1)
            inside = jnp.logical_and(lane >= offset, lane < offset + TRI)
            chunks[chunk] = jnp.where(inside, row, chunks[chunk])
            if offset + TRI > LANES:
                chunks[chunk + 1] = jnp.where(lane < offset + TRI - LANES, row, chunks[chunk + 1])
    cells[...] = pltpu.roll(arrived[...], LANES - TRI, 1).astype(jnp.int32)
    wide = [jnp.broadcast_to(c, (8, LANES)) for c in chunks]

    for part in range(2):

        def tile(t, carry):
            rows = pl.ds(pl.multiple_of(t * 8, 8), 8)
            terms = [kernel[part, rows, pl.ds(LANES * c, LANES)] * wide[c] for c in range(12)]
            while len(terms) > 1:
                terms = [a + b for a, b in zip(terms[::2], terms[1::2])] + terms[len(terms) // 2 * 2 :]
            dest = (t // 6) * 96 + part * TRI + (t % 6) * 8
            acc[pl.ds(pl.multiple_of(dest, 8), 8), :] = terms[0]
            return carry

        lax.fori_loop(0, 48, tile, 0, unroll=4)
    row8 = lax.broadcasted_iota(jnp.int32, (8, LANES), 0)
    total = jnp.zeros((8, 2 * TRI), F32)
    for j in range(NGY):
        total = total + lax.dot_general(
            jnp.where(row8 == j, 1.0, 0.0),
            acc[pl.ds(2 * TRI * j, 2 * TRI), :],
            (((1,), (1,)), ((), ())),
            precision=lax.Precision.HIGHEST,
            preferred_element_type=F32,
        )
    out[...] = jnp.zeros((8, LANES), F32)
    out[:, 0 : 2 * TRI] = total


def partial_rates(arrived, kernel):
    return pl.pallas_call(
        rates_kernel,
        out_shape=(shape(NGY, LANES), shape(NGX, LANES, dtype=jnp.int32)),
        in_specs=[spec()] * 2,
        out_specs=(spec(), spec()),
        scratch_shapes=[VMEM((768, LANES), F32)],
        compiler_params=pltpu.CompilerParams(vmem_limit_bytes=16 << 20),
        name="rates",
    )(arrived, kernel)


def around(ref, x, before, after, row, lane):
    rows = pl.ds(row, 8)
    centre = [ref[x * CHUNKS + i, rows, :] for i in range(CHUNKS)]
    left = [pltpu.roll(v, 1, 1) for v in centre]
    right = [pltpu.roll(v, LANES - 1, 1) for v in centre]
    sums = []
    for i in range(CHUNKS):
        below = left[i - 1] if i else 0.0
        above = right[i + 1] if i + 1 < CHUNKS else 0.0
        z = jnp.where(lane == 0, below, left[i]) + jnp.where(lane == LANES - 1, above, right[i])
        y = ref[x * CHUNKS + i, pl.ds(row - 1, 8), :] + ref[x * CHUNKS + i, pl.ds(row + 1, 8), :]
        xs = ref[before * CHUNKS + i, rows, :] + ref[after * CHUNKS + i, rows, :]
        sums.append((xs + y) + z)
    return centre, sums


def stretch(first, last):
    return range(first, last, 8)


def inner_kernel(p, k, y_up, y_down, out, s_edge, q_edge, a_edge, q1_edge, q2_edge, s, q, a, q1, q2, field, sem):
    lane = lax.broadcasted_iota(jnp.int32, (8, LANES), 1)
    row = lax.broadcasted_iota(jnp.int32, (8, LANES), 0)

    def convert(x, carry):
        for i in range(CHUNKS):
            lanes = pl.ds(LANES * i, LANES)
            low, high = y_up[x, :, lanes], y_down[x, :, lanes]
            root = jnp.sqrt(jnp.where(row >= 5, pltpu.roll(low, 5, 0), 0.0))
            s[x * CHUNKS + i, 0:8, :] = root
            q[x * CHUNKS + i, 0:8, :] = root * low
            root = jnp.sqrt(jnp.where(row < 3, pltpu.roll(high, 3, 0), 0.0))
            s[x * CHUNKS + i, 72:80, :] = root
            q[x * CHUNKS + i, 72:80, :] = root * high
            for t in range(CY // 8):
                root = jnp.sqrt(k[x, 8 * t : 8 * t + 8, lanes])
                s[x * CHUNKS + i, 8 * t + 8 : 8 * t + 16, :] = root
                q[x * CHUNKS + i, 8 * t + 8 : 8 * t + 16, :] = root * p[x, 8 * t : 8 * t + 8, lanes]
        return carry

    lax.fori_loop(0, CX, convert, 0)

    def first(x, carry):
        for r in stretch(6, 74):
            root, sums = around(s, x, x - 1, x + 1, r, lane)
            centre, total = around(q, x, x - 1, x + 1, r, lane)
            for i in range(CHUNKS):
                scaled = conductance * root[i]
                keep = 1.0 - scaled * sums[i]
                a[x * CHUNKS + i, pl.ds(r, 8), :] = keep
                q1[x * CHUNKS + i, pl.ds(r, 8), :] = keep * centre[i] + (scaled * root[i]) * total[i]
        return carry

    lax.fori_loop(1, CX - 1, first, 0)

    def second(x, carry):
        for r in stretch(7, 73):
            centre, total = around(q1, x, x - 1, x + 1, r, lane)
            for i in range(CHUNKS):
                root = s[x * CHUNKS + i, pl.ds(r, 8), :]
                keep = a[x * CHUNKS + i, pl.ds(r, 8), :]
                q2[x * CHUNKS + i, pl.ds(r, 8), :] = keep * centre[i] + (conductance * root * root) * total[i]
        return carry

    lax.fori_loop(2, CX - 2, second, 0)

    def third(x, carry):
        for r in stretch(8, 72):
            centre, total = around(q2, x, x - 1, x + 1, r, lane)
            for i in range(CHUNKS):
                root = s[x * CHUNKS + i, pl.ds(r, 8), :]
                keep = a[x * CHUNKS + i, pl.ds(r, 8), :]
                field[x - HALO, pl.ds(r - 8, 8), pl.ds(LANES * i, LANES)] = (
                    keep * centre[i] / root + (conductance * root) * total[i]
                )
        return carry

    lax.fori_loop(HALO, CX - HALO, third, 0)
    copy = pltpu.make_async_copy(field, out.at[pl.ds(HALO, CX - 2 * HALO)], sem)
    copy.start()
    for source, edge, depths in (
        (s, s_edge, (0, 1, 2)),
        (q, q_edge, (0, 1)),
        (a, a_edge, (1, 2)),
        (q1, q1_edge, (1, 2)),
        (q2, q2_edge, (2, 3)),
    ):
        for n, depth in enumerate(depths):
            for side, x in enumerate((depth, CX - 1 - depth)):
                edge[side, pl.ds(n * CHUNKS, CHUNKS)] = source[pl.ds(x * CHUNKS, CHUNKS)]
    copy.wait()


def block(planes):
    return VMEM((planes * CHUNKS, ROWS, LANES), F32)


def inner(p, k, y_up, y_down):
    return pl.pallas_call(
        inner_kernel,
        out_shape=(shape(CX, CY, NZ),) + tuple(shape(2, n * CHUNKS, ROWS, LANES) for n in (3, 2, 2, 2, 2)),
        in_specs=[spec()] * 4,
        out_specs=(spec(ANY),) + (spec(),) * 5,
        scratch_shapes=[block(CX) for _ in range(5)]
        + [VMEM((CX - 2 * HALO, CY, NZ), F32), pltpu.SemaphoreType.DMA(())],
        compiler_params=pltpu.CompilerParams(vmem_limit_bytes=40 << 20),
        cost_estimate=pl.CostEstimate(flops=40_000_000, bytes_accessed=12_000_000, transcendentals=0),
        name="inner",
    )(p, k, y_up, y_down)


def outer_kernel(
    field, s_edge, q_edge, a_edge, q1_edge, q2_edge, x_up, x_down, c_up, c_down, cells, out, answers, s, q, a, q1, q2, full, asked, sems
):
    del field
    ask = pltpu.make_async_copy(cells, asked, sems.at[0])
    ask.start()
    fill = pltpu.make_async_copy(
        out.at[pl.ds(HALO, CX - 2 * HALO)], full.at[pl.ds(HALO, CX - 2 * HALO)], sems.at[1]
    )
    fill.start()
    lane = lax.broadcasted_iota(jnp.int32, (8, LANES), 1)
    row = lax.broadcasted_iota(jnp.int32, (8, LANES), 0)
    zero = jnp.zeros((8, LANES), F32)
    stores = []
    for side, (wide, corner) in enumerate(((x_up, c_up), (x_down, c_down))):
        for target, edge, start in ((s, s_edge, 3), (q, q_edge, 3), (a, a_edge, 4), (q1, q1_edge, 4), (q2, q2_edge, 5)):
            count = edge.shape[1]
            target[pl.ds(start * CHUNKS, count)] = edge[side]
        for d in range(HALO):
            plane = d if side == 0 else HALO - 1 - d
            for i in range(CHUNKS):
                lanes = pl.ds(LANES * i, LANES)
                n = d * CHUNKS + i
                if d == 0:
                    for ref in (s, q):
                        ref[n, 0:8, :] = zero
                        ref[n, 72:80, :] = zero
                else:
                    c = d - 1 if side == 0 else 2 - d
                    low, high = corner[c, :, lanes], corner[2 + c, :, lanes]
                    root = jnp.sqrt(jnp.where(row >= 5, pltpu.roll(low, 5, 0), 0.0))
                    s[n, 0:8, :] = root
                    q[n, 0:8, :] = root * low
                    root = jnp.sqrt(jnp.where(row < 3, pltpu.roll(high, 3, 0), 0.0))
                    s[n, 72:80, :] = root
                    q[n, 72:80, :] = root * high
                for t in range(CY // 8):
                    root = jnp.sqrt(wide[HALO + plane, 8 * t : 8 * t + 8, lanes])
                    s[n, 8 * t + 8 : 8 * t + 16, :] = root
                    q[n, 8 * t + 8 : 8 * t + 16, :] = root * wide[plane, 8 * t : 8 * t + 8, lanes]

        def first(x, carry):
            for r in stretch(6, 74):
                root, sums = around(s, x, x - 1, x + 1, r, lane)
                centre, total = around(q, x, x - 1, x + 1, r, lane)
                for i in range(CHUNKS):
                    scaled = conductance * root[i]
                    keep = 1.0 - scaled * sums[i]
                    a[x * CHUNKS + i, pl.ds(r, 8), :] = keep
                    q1[x * CHUNKS + i, pl.ds(r, 8), :] = keep * centre[i] + (scaled * root[i]) * total[i]
            return carry

        lax.fori_loop(1, 4, first, 0)

        def second(x, carry):
            for r in stretch(7, 73):
                centre, total = around(q1, x, x - 1, x + 1, r, lane)
                for i in range(CHUNKS):
                    root = s[x * CHUNKS + i, pl.ds(r, 8), :]
                    keep = a[x * CHUNKS + i, pl.ds(r, 8), :]
                    q2[x * CHUNKS + i, pl.ds(r, 8), :] = keep * centre[i] + (conductance * root * root) * total[i]
            return carry

        lax.fori_loop(2, 5, second, 0)

        def third(x, carry):
            position = x - 3 if side == 0 else CX + 2 - x
            for r in stretch(8, 72):
                centre, total = around(q2, x, x - 1, x + 1, r, lane)
                for i in range(CHUNKS):
                    root = s[x * CHUNKS + i, pl.ds(r, 8), :]
                    keep = a[x * CHUNKS + i, pl.ds(r, 8), :]
                    full[position, pl.ds(r - 8, 8), pl.ds(LANES * i, LANES)] = (
                        keep * centre[i] / root + (conductance * root) * total[i]
                    )
            return carry

        lax.fori_loop(3, 6, third, 0)
        planes = pl.ds(0 if side == 0 else CX - HALO, HALO)
        store = pltpu.make_async_copy(full.at[planes], out.at[planes], sems.at[2 + side])
        store.start()
        stores.append(store)
    ask.wait()
    fill.wait()

    def answer(d, carry):
        value = zero
        for c in range(3):
            cell = asked[d, c]
            x, y, z = cell >> 15, (cell >> 9) & 63, cell & 511
            lanes = pl.ds(pl.multiple_of((z >> 7) * LANES, LANES), LANES)
            tile = full[x, pl.ds(pl.multiple_of((y >> 3) * 8, 8), 8), lanes]
            tile = pltpu.roll(tile, (LANES + c - (z & 127)) & 127, 1)
            value = jnp.where(jnp.logical_and(row == (y & 7), lane == c), tile, value)
        answers[pl.ds(d, 1), :] = jnp.sum(value, axis=0, keepdims=True)
        return carry

    lax.fori_loop(0, NGX, answer, 0, unroll=4)
    for store in stores:
        store.wait()


def outer(field, edges, x_up, x_down, c_up, c_down, cells):
    return pl.pallas_call(
        outer_kernel,
        out_shape=(shape(CX, CY, NZ), shape(NGX, LANES)),
        in_specs=[spec(ANY)] + [spec()] * 9 + [spec(ANY)],
        out_specs=(spec(ANY), spec()),
        scratch_shapes=[block(6), block(5), block(6), block(6), block(7)]
        + [
            VMEM((CX, CY, NZ), F32),
            pltpu.SMEM((NGX, LANES), jnp.int32),
            pltpu.SemaphoreType.DMA((4,)),
        ],
        input_output_aliases={0: 0},
        compiler_params=pltpu.CompilerParams(vmem_limit_bytes=32 << 20),
        name="outer",
    )(field, *edges, x_up, x_down, c_up, c_down, cells)


def friction_kernel(
    rates, answers, slip, aging, normal, shear, direct, evolution, distance, owner_row, owner_column, state_out, rate_out
):
    owners = owner_row[...]
    rank = rank_row(owners, owner_column[...])
    got = answers[...]
    named = lax.broadcasted_iota(jnp.int32, (NGX, TRI), 0) == owners
    held = jnp.zeros((NGX, TRI), F32)
    for c in range(3):
        held = jnp.where(jnp.logical_and(named, rank == float(c)), got[:, c : c + 1], held)
    pressure = jnp.sum(held, axis=0, keepdims=True)
    both = jnp.sum(rates[...], axis=0, keepdims=True)
    first, second = both[:, 0:TRI], both[:, TRI : 2 * TRI]
    effective = normal[...] + step_time * second - pressure
    ratio = distance[...] / slip[...]
    state = ratio + (aging[...] - ratio) * jnp.exp(-heal_time / ratio)
    state_out[...] = state
    rate_out[...] = (
        (shear[...] + step_time * first) / effective - friction_ref - evolution[...] * jnp.log(state / distance[...])
    ) / direct[...]


def friction(*values):
    return pl.pallas_call(
        friction_kernel,
        out_shape=(shape(1, TRI), shape(1, TRI)),
        in_specs=[spec()] * len(values),
        out_specs=(spec(), spec()),
        name="friction",
    )(*values)


def exchanged(value, axis):
    return lax.all_to_all(value, axis, split_axis=0, concat_axis=0, tiled=True)


def local(
    pressure,
    permeability,
    kernel,
    slip_rate,
    aging_state,
    normal_stress,
    shear_stress,
    direct_effect,
    evolution_effect,
    slip_distance,
    tri_owner,
    tri_cell,
):
    owner_row, cell_row = tri_owner.reshape(1, TRI), tri_cell.reshape(1, TRI)
    moved = lax.ppermute(slip_rate, ("gx", "gy"), SLIP_MOVES)
    x_up, x_down, y_up, y_down = pack(pressure, permeability)
    x_up, x_down = lax.ppermute(x_up, "gx", X_UP), lax.ppermute(x_down, "gx", X_DOWN)
    y_up, y_down = lax.ppermute(y_up, "gy", Y_UP), lax.ppermute(y_down, "gy", Y_DOWN)
    wanted = requests_of(owner_row, tri_owner, cell_row)
    lane = lax.broadcasted_iota(jnp.int32, (NGX, LANES), 1)
    row = jnp.pad(moved, (0, LANES - TRI)).reshape(1, LANES)
    arrived = exchanged(jnp.where(lane < TRI, row, wanted), "gx")
    partial_sums, cells = partial_rates(arrived, kernel)
    rates = exchanged(partial_sums, "gy")
    c_up = lax.ppermute(jnp.concatenate([y_up[CX - 2 :], y_down[CX - 2 :]]), "gx", X_UP)
    c_down = lax.ppermute(jnp.concatenate([y_up[:2], y_down[:2]]), "gx", X_DOWN)
    field, *edges = inner(pressure, permeability, y_up, y_down)
    field, answers = outer(field, edges, x_up, x_down, c_up, c_down, cells)
    answers = exchanged(answers, "gx")
    flat = [
        v.reshape(1, TRI)
        for v in (slip_rate, aging_state, normal_stress, shear_stress, direct_effect, evolution_effect, slip_distance)
    ]
    state_next, log_rate = friction(rates, answers, *flat, owner_row, tri_owner)
    return field, state_next.reshape(TRI), log_rate.reshape(TRI)


def solution(mesh):
    both = P(("gx", "gy"))
    placed = (
        P("gx", "gy", None),
        P("gx", "gy", None),
        P(None, "gx", "gy"),
        *([both] * 7),
        P(("gx", "gy"), None),
        both,
    )
    return jax.shard_map(
        local,
        mesh=mesh,
        in_specs=placed,
        out_specs=(P("gx", "gy", None), both, both),
        check_vma=False,
    )
```

time: 175 us -> 90.3 us (0.52)
  other arithmetic: 44.2 us -> 1.99 us
  blocking collectives: 51.7 us -> 28.6 us
  Pallas kernels: 0 us -> 20.1 us
  starting transfers between devices: 42.8 us -> 29.7 us
  waiting for transfers between devices: 11 us -> 0.02 us
  matrix products: 8.75 us -> 0 us
  local copies, waits for them, and re-layouts: 12.9 us -> 8.42 us
    all_gather x3 -> x0, blocking collectives: 43.1 us -> none  [all_blocks(): pieces = lax.all_gather(pieces, axes[k])]
    add x3 -> x0, other arithmetic: 41 us -> none  [explicit_step(): return centre_p + conductance * flux]
    all_to_all x0 -> x2, blocking collectives: none -> 28.6 us  [exchanged(): return lax.all_to_all(value, axis, split_axis=0, concat_axis=0, tiled=True)]
    pallas_call x0 -> x6, Pallas kernels: none -> 20.1 us  [the longest x1 8.22 us: inner(): pl.pallas_call(inner_kernel, out_shape=(shape(CX, CY, NZ),) + tuple((shap...]
    all_to_all x3 -> x1, starting transfers between devices: 20.5 us -> 7.45 us  [exchanged(): return lax.all_to_all(value, axis, split_axis=0, concat_axis=0, tiled=True)]
    dot_general x1 -> x0, matrix products: 8.75 us -> none  [tractions(): jnp.dot(kernel.reshape(-1, column_count), segment, precision=lax.Precisio...]
    unnamed x1 -> x0, blocking collectives: 8.6 us -> none
    all_to_all x3 -> x1, waiting for transfers between devices: 6.93 us -> 0.01 us  [exchanged(): return lax.all_to_all(value, axis, split_axis=0, concat_axis=0, tiled=True)]
  transfers between devices with their start and end apart: 11 -> 8, of which waited for: 3 -> 0; matrix products, arithmetic and copies ran while one was open for 34% -> 3% of each run, Pallas kernels for 0% -> 19%
where the time goes in v1:
time: 90.3 us; the launch traced here: 89.6 us
  starting transfers between devices  29.7 us (33%)
  blocking collectives  28.6 us (32%)
  Pallas kernels  20.1 us (22%)
  local copies, waits for them, and re-layouts  8.42 us (9%)
  other arithmetic  1.99 us (2%)
    all_to_all x2, blocking collectives, exchanged(): return lax.all_to_all(value, axis, split_axis=0, concat_axis=0, tiled=True)  28.6 us
    unnamed x17, local copies, waits for them, and re-layouts  8.4 us
    pallas_call x1, Pallas kernels, inner(): pl.pallas_call(inner_kernel, out_shape=(shape(CX, CY, NZ),) + tuple((shap...  8.22 us
    all_to_all x1, starting transfers between devices, exchanged(): return lax.all_to_all(value, axis, split_axis=0, concat_axis=0, tiled=True)  7.45 us
    pallas_call x1, Pallas kernels, outer(): pl.pallas_call(outer_kernel, out_shape=(shape(CX, CY, NZ), shape(NGX, LAN...  5.88 us
    ppermute x1, starting transfers between devices, local(): moved = lax.ppermute(slip_rate, ('gx', 'gy'), SLIP_MOVES)  5.45 us
    ppermute x1, starting transfers between devices, local(): lax.ppermute(y_up, 'gy', Y_UP)  4.39 us
    ppermute x1, starting transfers between devices, local(): lax.ppermute(jnp.concatenate([y_up[CX - 2:], y_down[CX - 2:]]), 'gx', X_UP)  3.85 us
  transfers between devices with their start and end apart: 8, of which 0 were waited for; matrix products, arithmetic and copies ran while one was open for 3% of the time, Pallas kernels for 19%

profile of v1, /device:TPU:1, one launch (start us, length us, event | category | flops | bytes accessed | tf_op | source)
XLA Modules:
  0.0 89.6 jit_solution(16312264126808016513)
XLA Ops:
  0.6 0.0 copy-start
  0.6 1.6 %copy-done = f32[16,64,512]{2,1,0:T(8,128)S(1)} copy-done((f32[16,64,512]{2,1,0:T(8,128)S(1)}, f32[16,64,512]{2,1,0:T(8,128)}, u32[]{:S(2)}) %copy-start) | copy-done | bytes 2097176
  2.2 0.0 copy-start.2
  2.2 1.6 %copy-done.2 = f32[16,64,512]{2,1,0:T(8,128)S(1)} copy-done((f32[16,64,512]{2,1,0:T(8,128)S(1)}, f32[16,64,512]{2,1,0:T(8,128)}, u32[]{:S(2)}) %copy-start.2) | copy-done | bytes 2097176
  3.8 0.0 copy-start.7
  3.8 0.0 copy-start.6
  3.8 1.3 %pack.1 = (f32[6,64,512]{2,1,0:T(8,128)}, f32[6,64,512]{2,1,0:T(8,128)}, f32[16,8,512]{2,1,0:T(8,128)S(1)}, f32[16,8,512]{2,1,0:T(8,128)S(1)}) custom-call(f32[16,64,512]{2,1,0:T(8,128)S(1)} %copy-done, f32[16,64,512]{2,1,0:T(8,128)S(1)} %copy-done.2), custom_call_target="tpu_custom_call" | custom-call | tf_op jit(solution)/shard_map/pack/pallas_call | solution.py:85
  5.1 4.4 %collective-permute-start = (f32[16,8,512]{2,1,0:T(8,128)S(1)}, f32[16,8,512]{2,1,0:T(8,128)S(1)}, u32[]{:S(2)}, u32[]{:S(2)}) collective-permute-start(f32[16,8,512]{2,1,0:T(8,128)S(1)} %get-tuple-element.19), channel_id=1, source_target_pairs={{0,1},{1,2},{2,3},{3,4},{4,5},{5,6},{6,7},{8,9},{9,10},{10,11},{11... | collective-permute-start | bytes 786440 | tf_op jit(solution)/shard_map/ppermute | solution.py:472
  9.5 0.0 copy-done.7
  9.5 5.5 %collective-permute-start.6 = (f32[48]{0:T(128)S(1)}, f32[48]{0:T(128)S(1)}, u32[]{:S(2)}, u32[]{:S(2)}) collective-permute-start(f32[48]{0:T(128)S(1)} %copy-done.7), channel_id=1, source_target_pairs={{0,160},{1,96},{2,128},{3,64},{4,0},{5,192},{6,32},{7,224},{8,168}... | collective-permute-start | bytes 584 | tf_op jit(solution)/shard_map/ppermute | solution.py:469
  15.0 1.3 %collective-permute-start.1 = (f32[16,8,512]{2,1,0:T(8,128)S(1)}, f32[16,8,512]{2,1,0:T(8,128)S(1)}, u32[]{:S(2)}, u32[]{:S(2)}) collective-permute-start(f32[16,8,512]{2,1,0:T(8,128)S(1)} %get-tuple-element.20), channel_id=1, source_target_pairs={{1,0},{2,1},{3,2},{4,3},{5,4},{6,5},{7,6},{9,8},{10,9},{11,10},{12... | collective-permute-start | bytes 786440 | tf_op jit(solution)/shard_map/ppermute | solution.py:472
  16.3 3.4 %collective-permute-start.2 = (f32[6,64,512]{2,1,0:T(8,128)}, f32[6,64,512]{2,1,0:T(8,128)S(1)}, u32[]{:S(2)}, u32[]{:S(2)}) collective-permute-start(f32[6,64,512]{2,1,0:T(8,128)} %get-tuple-element.27), channel_id=1, source_target_pairs={{0,8},{8,16},{16,24},{24,32},{32,40},{40,48},{48,56},{56,64},{64,7... | collective-permute-start | bytes 2359304 | tf_op jit(solution)/shard_map/ppermute | solution.py:471
  19.7 1.9 %collective-permute-start.3 = (f32[6,64,512]{2,1,0:T(8,128)}, f32[6,64,512]{2,1,0:T(8,128)}, u32[]{:S(2)}, u32[]{:S(2)}) collective-permute-start(f32[6,64,512]{2,1,0:T(8,128)} %get-tuple-element.28), channel_id=1, source_target_pairs={{8,0},{16,8},{24,16},{32,24},{40,32},{48,40},{56,48},{64,56},{72,6... | collective-permute-start | bytes 2359304 | tf_op jit(solution)/shard_map/ppermute | solution.py:471
  21.6 0.0 copy-done.6
  21.7 0.7 copy.18.owner_column
  22.4 1.5 %requests.1 = f32[32,128]{1,0:T(8,128)} custom-call(s32[1,48]{1,0:T(1,128)} %bitcast.28, s32[48,1]{1,0:T(8,128)} %copy.18.owner_column, s32[1,48]{1,0:T(1,128)} %bitcast.30), custom_call_target="tpu_custom_call" | custom-call | tf_op jit(solution)/shard_map/requests/pallas_call | solution.py:123
  23.9 0.0 collective-permute-done.6
  23.9 0.0 collective-permute-done.y_up
  23.9 0.0 collective-permute-done.1.y_down
  23.9 0.6 pad_maximum_fusion
  24.5 3.9 %collective-permute-start.4 = (f32[4,8,512]{2,1,0:T(8,128)}, f32[4,8,512]{2,1,0:T(8,128)S(1)}, u32[]{:S(2)}, u32[]{:S(2)}) collective-permute-start(f32[4,8,512]{2,1,0:T(8,128)} %pad_maximum_fusion), channel_id=1, source_target_pairs={{0,8},{8,16},{16,24},{24,32},{32,40},{40,48},{48,56},{56,64},{64,7... | collective-permute-start | bytes 196616 | tf_op jit(solution)/shard_map/ppermute | solution.py:479
  28.4 0.6 pad_maximum_fusion.1
  29.0 1.9 %collective-permute-start.5 = (f32[4,8,512]{2,1,0:T(8,128)}, f32[4,8,512]{2,1,0:T(8,128)S(1)}, u32[]{:S(2)}, u32[]{:S(2)}) collective-permute-start(f32[4,8,512]{2,1,0:T(8,128)} %pad_maximum_fusion.1), channel_id=1, source_target_pairs={{8,0},{16,8},{24,16},{32,24},{40,32},{48,40},{56,48},{64,56},{72,6... | collective-permute-start | bytes 196616 | tf_op jit(solution)/shard_map/ppermute | solution.py:480
  31.0 0.7 broadcast_select_fusion
  31.7 17.3 %all_to_all.33 = f32[32,1,128]{2,1,0:T(1,128)S(1)} all-to-all(f32[32,1,128]{2,1,0:T(1,128)S(1)} %bitcast.27), channel_id=1, replica_groups=mesh['gx'=32,'gy'=8] {'gx'}, dimensions={0} | all-to-all | bytes 32768 | tf_op jit(solution)/shard_map/all_to_all | solution.py:451
  48.9 0.0 copy-start.4
  48.9 2.3 %copy-done.4 = f32[2,384,1536]{2,1,0:T(8,128)S(1)} copy-done((f32[2,384,1536]{2,1,0:T(8,128)S(1)}, f32[2,384,1536]{2,1,0:T(8,128)}, u32[]{:S(2)}) %copy-start.4) | copy-done | bytes 4718616
  51.3 0.0 copy-start.1
  51.3 1.7 %rates.1 = (f32[8,128]{1,0:T(8,128)S(1)}, s32[32,128]{1,0:T(8,128)S(1)}) custom-call(f32[32,128]{1,0:T(8,128)S(1)} %bitcast.23, f32[2,384,1536]{2,1,0:T(8,128)S(1)} %copy-done.4), custom_call_target="tpu_custom_call" | custom-call | tf_op jit(solution)/shard_map/rates/pallas_call | solution.py:176
  53.0 0.0 copy-start.5
  53.0 0.6 copy-done.5
  53.6 7.5 %all-to-all-start.1 = ((f32[8,1,128]{2,1,0:T(1,128)}), f32[8,1,128]{2,1,0:T(1,128)}, u32[]{:S(2)}, u32[]{:S(2)}) async-start(f32[8,1,128]{2,1,0:T(1,128)} %bitcast.25), calls=%async_computation.1 | async-start | bytes 8192 | tf_op jit(solution)/shard_map/all_to_all | solution.py:451
  61.0 0.0 copy-done.1
  61.0 0.0 copy-start.3
  61.0 1.6 %copy-done.3 = f32[16,64,512]{2,1,0:T(8,128)S(1)} copy-done((f32[16,64,512]{2,1,0:T(8,128)S(1)}, f32[16,64,512]{2,1,0:T(8,128)}, u32[]{:S(2)}) %copy-start.3) | copy-done | bytes 2097176
  62.6 8.2 %inner.1 = (f32[16,64,512]{2,1,0:T(8,128)}, f32[2,12,80,128]{3,2,1,0:T(8,128)S(1)}, f32[2,8,80,128]{3,2,1,0:T(8,128)S(1)}, f32[2,8,80,128]{3,2,1,0:T(8,128)S(1)}...) custom-call(f32[16,64,512]{2,1,0:T(8,128)S(1)} %copy-done.1, f32[16,64,512]{2,1,0:T(8,128)S(1)} %copy-done.3, ...), custom_call_target="tpu_custom_call" | custom-call | flops 40000000 | bytes 12000000 | tf_op jit(solution)/shard_map/inner/pallas_call | solution.py:285
  70.8 0.0 collective-permute-done.4.c_up
  70.9 0.0 collective-permute-done.5.c_down
  70.9 0.0 collective-permute-done.2.x_up
  70.9 0.0 collective-permute-done.3.x_down
  70.9 5.9 %outer.1 = (f32[16,64,512]{2,1,0:T(8,128)}, f32[32,128]{1,0:T(8,128)S(1)}) custom-call(f32[16,64,512]{2,1,0:T(8,128)} %get-tuple-element.21.field, f32[2,12,80,128]{3,2,1,0:T(8,128)S(1)} %get-tuple-element.22.s_edge, f32[2,8,80,128]{3,2,1,0:T(8,128)S(1)} %get-tuple-element.23.q_edge, ...), custom_call_target="tpu_custom_call", output_to_operand_aliasing={{0}: (0, {})} | custom-call | tf_op jit(solution)/shard_map/outer/pallas_call | solution.py:401
  76.8 0.0 all-to-all-done.1
  76.8 11.3 %all_to_all.34 = f32[32,1,128]{2,1,0:T(1,128)} all-to-all(f32[32,1,128]{2,1,0:T(1,128)S(1)} %bitcast.24), channel_id=1, replica_groups=mesh['gx'=32,'gy'=8] {'gx'}, dimensions={0} | all-to-all | bytes 32768 | tf_op jit(solution)/shard_map/all_to_all | solution.py:451
  88.1 1.5 %friction.1 = (f32[1,48]{1,0:T(1,128)}, f32[1,48]{1,0:T(1,128)}) custom-call(f32[8,128]{1,0:T(8,128)} %bitcast.7.rates, f32[32,128]{1,0:T(8,128)} %bitcast.26, f32[1,48]{1,0:T(1,128)} %bitcast.31, f32[1,48]{1,0:T(1,128)} %bitcast.32, f32[1,48]{1,0:T(1,128)} %bitcast.33, f32[1,48]{1,0:T(1,128)} %bitcast.34, f32[1,48]{1,0:T(1,128)} %bitcast.35, ...), custom_call_target="tpu_custom_call" | custom-call | tf_op jit(solution)/shard_map/friction/pallas_call | solution.py:441
  (4 shorter events, 0.0 us)
Async XLA Ops:
  0.6 1.6 %copy-start = (f32[16,64,512]{2,1,0:T(8,128)S(1)}, f32[16,64,512]{2,1,0:T(8,128)}, u32[]{:S(2)}) copy-start(f32[16,64,512]{2,1,0:T(8,128)} %p.3) | copy-start | bytes 6291460
  2.2 1.6 %copy-start.2 = (f32[16,64,512]{2,1,0:T(8,128)S(1)}, f32[16,64,512]{2,1,0:T(8,128)}, u32[]{:S(2)}) copy-start(f32[16,64,512]{2,1,0:T(8,128)} %k.3) | copy-start | bytes 6291460
  3.8 5.7 %copy-start.7 = (f32[48]{0:T(128)S(1)}, f32[48]{0:T(128)}, u32[]{:S(2)}) copy-start(f32[48]{0:T(128)} %param.15) | copy-start | bytes 580
  3.8 17.8 %copy-start.6 = (s32[48,1]{0,1:T(1,128)S(1)}, s32[48,1]{0,1:T(1,128)}, u32[]{:S(2)}) copy-start(s32[48,1]{0,1:T(1,128)} %param.22) | copy-start | bytes 580
  5.1 18.7 %collective-permute-start = (f32[16,8,512]{2,1,0:T(8,128)S(1)}, f32[16,8,512]{2,1,0:T(8,128)S(1)}, u32[]{:S(2)}, u32[]{:S(2)}) collective-permute-start(f32[16,8,512]{2,1,0:T(8,128)S(1)} %get-tuple-element.19), channel_id=1, source_target_pairs={{0,1},{1,2},{2,3},{3,4},{4,5},{5,6},{6,7},{8,9},{9,10},{10,11},{11... | collective-permute-start | bytes 786440 | tf_op jit(solution)/shard_map/ppermute | solution.py:472
  9.5 14.3 %collective-permute-start.6 = (f32[48]{0:T(128)S(1)}, f32[48]{0:T(128)S(1)}, u32[]{:S(2)}, u32[]{:S(2)}) collective-permute-start(f32[48]{0:T(128)S(1)} %copy-done.7), channel_id=1, source_target_pairs={{0,160},{1,96},{2,128},{3,64},{4,0},{5,192},{6,32},{7,224},{8,168}... | collective-permute-start | bytes 584 | tf_op jit(solution)/shard_map/ppermute | solution.py:469
  15.0 8.9 %collective-permute-start.1 = (f32[16,8,512]{2,1,0:T(8,128)S(1)}, f32[16,8,512]{2,1,0:T(8,128)S(1)}, u32[]{:S(2)}, u32[]{:S(2)}) collective-permute-start(f32[16,8,512]{2,1,0:T(8,128)S(1)} %get-tuple-element.20), channel_id=1, source_target_pairs={{1,0},{2,1},{3,2},{4,3},{5,4},{6,5},{7,6},{9,8},{10,9},{11,10},{12... | collective-permute-start | bytes 786440 | tf_op jit(solution)/shard_map/ppermute | solution.py:472
  16.3 54.6 %collective-permute-start.2 = (f32[6,64,512]{2,1,0:T(8,128)}, f32[6,64,512]{2,1,0:T(8,128)S(1)}, u32[]{:S(2)}, u32[]{:S(2)}) collective-permute-start(f32[6,64,512]{2,1,0:T(8,128)} %get-tuple-element.27), channel_id=1, source_target_pairs={{0,8},{8,16},{16,24},{24,32},{32,40},{40,48},{48,56},{56,64},{64,7... | collective-permute-start | bytes 2359304 | tf_op jit(solution)/shard_map/ppermute | solution.py:471
  19.7 51.2 %collective-permute-start.3 = (f32[6,64,512]{2,1,0:T(8,128)}, f32[6,64,512]{2,1,0:T(8,128)}, u32[]{:S(2)}, u32[]{:S(2)}) collective-permute-start(f32[6,64,512]{2,1,0:T(8,128)} %get-tuple-element.28), channel_id=1, source_target_pairs={{8,0},{16,8},{24,16},{32,24},{40,32},{48,40},{56,48},{64,56},{72,6... | collective-permute-start | bytes 2359304 | tf_op jit(solution)/shard_map/ppermute | solution.py:471
  24.5 46.3 %collective-permute-start.4 = (f32[4,8,512]{2,1,0:T(8,128)}, f32[4,8,512]{2,1,0:T(8,128)S(1)}, u32[]{:S(2)}, u32[]{:S(2)}) collective-permute-start(f32[4,8,512]{2,1,0:T(8,128)} %pad_maximum_fusion), channel_id=1, source_target_pairs={{0,8},{8,16},{16,24},{24,32},{32,40},{40,48},{48,56},{56,64},{64,7... | collective-permute-start | bytes 196616 | tf_op jit(solution)/shard_map/ppermute | solution.py:479
  29.0 41.8 %collective-permute-start.5 = (f32[4,8,512]{2,1,0:T(8,128)}, f32[4,8,512]{2,1,0:T(8,128)S(1)}, u32[]{:S(2)}, u32[]{:S(2)}) collective-permute-start(f32[4,8,512]{2,1,0:T(8,128)} %pad_maximum_fusion.1), channel_id=1, source_target_pairs={{8,0},{16,8},{24,16},{32,24},{40,32},{48,40},{56,48},{64,56},{72,6... | collective-permute-start | bytes 196616 | tf_op jit(solution)/shard_map/ppermute | solution.py:480
  48.9 2.3 %copy-start.4 = (f32[2,384,1536]{2,1,0:T(8,128)S(1)}, f32[2,384,1536]{2,1,0:T(8,128)}, u32[]{:S(2)}) copy-start(f32[2,384,1536]{2,1,0:T(8,128)} %kernel.1) | copy-start | bytes 14155780
  51.3 9.7 %copy-start.1 = (f32[16,64,512]{2,1,0:T(8,128)S(1)}, f32[16,64,512]{2,1,0:T(8,128)}, u32[]{:S(2)}) copy-start(f32[16,64,512]{2,1,0:T(8,128)} %p.3) | copy-start | bytes 6291460
  53.0 0.6 copy-start.5
  53.6 23.2 %all-to-all-start.1 = ((f32[8,1,128]{2,1,0:T(1,128)}), f32[8,1,128]{2,1,0:T(1,128)}, u32[]{:S(2)}, u32[]{:S(2)}) async-start(f32[8,1,128]{2,1,0:T(1,128)} %bitcast.25), calls=%async_computation.1 | async-start | bytes 8192 | tf_op jit(solution)/shard_map/all_to_all | solution.py:451
  61.0 1.6 %copy-start.3 = (f32[16,64,512]{2,1,0:T(8,128)S(1)}, f32[16,64,512]{2,1,0:T(8,128)}, u32[]{:S(2)}) copy-start(f32[16,64,512]{2,1,0:T(8,128)} %k.3) | copy-start | bytes 6291460

commit v2 on v1

v2 whole, which is shorter than its diff:
```python
import jax
import jax.numpy as jnp
from jax import lax
from jax.experimental import pallas as pl
from jax.experimental.pallas import tpu as pltpu
from jax.sharding import PartitionSpec as P

NGX, NGY = 32, 8
CX, CY, NZ, TRI = 16, 64, 512, 48
HALO = 3
ROWS = 80
LANES = 128
CHUNKS = NZ // LANES
conductance = 0.15
step_time = 1.0
heal_time = 0.5
friction_ref = 0.6
F32 = jnp.float32
VMEM = pltpu.VMEM
ANY = pl.ANY

X_MOVE = (2, 1, 2, 1, 0, 3, 0, 3)
Y_MOVE = (1, 1, 0, 0, 0, 0, 1, 1)
X_CODE = sum(v << (2 * i) for i, v in enumerate(X_MOVE))
Y_CODE = sum(v << i for i, v in enumerate(Y_MOVE))


def landing(group, other):
    delta = (other - group) & 7
    x = ((group >> 1) + ((X_CODE >> (2 * delta)) & 3)) & 3
    y = (group & 1) ^ ((Y_CODE >> delta) & 1)
    return 2 * x + y


SLIP_MOVES = [
    ((4 * g + r) * NGY + j, (4 * landing(g, j) + r) * NGY + g) for g in range(8) for r in range(4) for j in range(NGY)
]
X_UP = [(i, i + 1) for i in range(NGX - 1)]
X_DOWN = [(j, i) for i, j in X_UP]
Y_UP = [(i, i + 1) for i in range(NGY - 1)]
Y_DOWN = [(j, i) for i, j in Y_UP]


def spec(space=VMEM):
    return pl.BlockSpec(memory_space=space)


def shape(*dims, dtype=F32):
    return jax.ShapeDtypeStruct(dims, dtype)


def far(value):
    return pltpu.with_memory_space_constraint(value, pltpu.HBM)


def all_far(*values):
    return tuple(far(v) for v in values)


def started(*copies):
    for copy in copies:
        copy.start()
    return copies


def waited(copies):
    for copy in copies:
        copy.wait()


HBM = pltpu.HBM
DMA = pltpu.SemaphoreType.DMA


def turned(row_value):
    row = lax.broadcasted_iota(jnp.int32, (TRI, TRI), 0)
    column = lax.broadcasted_iota(jnp.int32, (TRI, TRI), 1)
    return jnp.sum(jnp.where(row == column, row_value, 0.0), axis=1, keepdims=True)


def prepare_kernel(p, k, owner, cell, *refs):
    floats, (y_up, y_down, wanted, terms, tiles, whole, held, sems) = refs[:7], refs[7:]
    tops = started(
        pltpu.make_async_copy(p.at[:, pl.ds(CY - 8, 8), :], tiles.at[0], sems.at[0]),
        pltpu.make_async_copy(k.at[:, pl.ds(CY - 8, 8), :], tiles.at[1], sems.at[1]),
        pltpu.make_async_copy(p.at[:, pl.ds(0, 8), :], tiles.at[2], sems.at[2]),
        pltpu.make_async_copy(k.at[:, pl.ds(0, 8), :], tiles.at[3], sems.at[3]),
    )
    small = started(
        pltpu.make_async_copy(owner, whole.at[0], sems.at[4]),
        pltpu.make_async_copy(cell, whole.at[1], sems.at[5]),
        *[pltpu.make_async_copy(ref, held.at[n], sems.at[6 + n]) for n, ref in enumerate(floats)],
    )
    waited(small)
    slip, aging, normal, shear, direct, evolution, distance = (held[n] for n in range(7))
    owners = whole[0].astype(F32)
    first = lax.broadcasted_iota(jnp.int32, (TRI, TRI), 0)
    second = lax.broadcasted_iota(jnp.int32, (TRI, TRI), 1)
    same = jnp.logical_and(turned(owners) == owners, first < second)
    rank = jnp.sum(jnp.where(same, 1.0, 0.0), axis=0, keepdims=True)
    cells = whole[1].astype(F32)
    lane = lax.broadcasted_iota(jnp.int32, (NGX, LANES), 1)
    named = lax.broadcasted_iota(jnp.int32, (NGX, TRI), 0) == whole[0]
    value = jnp.zeros((NGX, LANES), F32)
    for c in range(3):
        asked = jnp.where(jnp.logical_and(named, rank == float(c)), cells, 0.0)
        value = jnp.where(lane == TRI + c, jnp.sum(asked, axis=1, keepdims=True), value)
    wanted[...] = value
    ratio = distance / slip
    state = ratio + (aging - ratio) * jnp.exp(-heal_time / ratio)
    terms[...] = jnp.zeros((8, LANES), F32)
    aged = evolution * jnp.log(state / distance)
    for n, term in enumerate((state, aged, normal, shear, direct, owners, rank)):
        terms[n : n + 1, 0:TRI] = term
    waited(tops)
    row = lax.broadcasted_iota(jnp.int32, (8, NZ), 0)

    def plane(x, carry):
        y_up[x] = jnp.where(row >= 5, tiles[0, x], pltpu.roll(tiles[1, x], 3, 0))
        y_down[x] = jnp.where(row < 3, tiles[2, x], pltpu.roll(tiles[3, x], 5, 0))
        return carry

    lax.fori_loop(0, CX, plane, 0)


def prepare(*values):
    return pl.pallas_call(
        prepare_kernel,
        out_shape=(
            shape(CX, 8, NZ),
            shape(CX, 8, NZ),
            shape(NGX, LANES),
            shape(8, LANES),
        ),
        in_specs=[spec(HBM)] * len(values),
        out_specs=(spec(),) * 4,
        scratch_shapes=[VMEM((4, CX, 8, NZ), F32), VMEM((2, 1, TRI), jnp.int32), VMEM((7, 1, TRI), F32), DMA((13,))],
        compiler_params=pltpu.CompilerParams(vmem_limit_bytes=4 << 20),
        name="prepare",
    )(*all_far(*values))


def halo_rows(low, high, row):
    p = jnp.where(row >= 5, low, jnp.where(row < 3, high, 0.0))
    k = jnp.where(row >= 5, pltpu.roll(low, 5, 0), jnp.where(row < 3, pltpu.roll(high, 3, 0), 0.0))
    return p, k


def sides_kernel(p, k, y_up, y_down, token, x_up, x_down, sems):
    del token
    copies = []
    for side, (target, start) in enumerate(((x_up, CX - HALO), (x_down, 0))):
        for n, source in enumerate((p, k)):
            copies.append(
                pltpu.make_async_copy(
                    source.at[pl.ds(start, HALO)], target.at[pl.ds(HALO * n, HALO), pl.ds(0, CY)], sems.at[2 * side + n]
                )
            )
    started(*copies)
    row = lax.broadcasted_iota(jnp.int32, (8, NZ), 0)
    for target, start in ((x_up, CX - HALO), (x_down, 0)):
        for n in range(HALO):
            halo_p, halo_k = halo_rows(y_up[start + n], y_down[start + n], row)
            target[n, CY : CY + 8, :] = halo_p
            target[HALO + n, CY : CY + 8, :] = halo_k
    waited(copies)


def sides(p, k, y_up, y_down, token):
    return pl.pallas_call(
        sides_kernel,
        out_shape=(shape(2 * HALO, CY + 8, NZ),) * 2,
        in_specs=[spec(HBM)] * 2 + [spec()] * 2 + [spec(ANY)],
        out_specs=(spec(),) * 2,
        scratch_shapes=[DMA((4,))],
        compiler_params=pltpu.CompilerParams(vmem_limit_bytes=4 << 20),
        name="sides",
    )(far(p), far(k), y_up, y_down, token)


def rates_kernel(arrived, kernel_far, token, out, cells, acc, kernel, sems):
    del token
    copies = started(
        *[
            pltpu.make_async_copy(
                kernel_far.at[n // 4, pl.ds(96 * (n % 4), 96)], kernel.at[n // 4, pl.ds(96 * (n % 4), 96)], sems.at[n]
            )
            for n in range(8)
        ]
    )
    gy = lax.axis_index("gy")
    lane = lax.broadcasted_iota(jnp.int32, (1, LANES), 1)
    chunks = [jnp.zeros((1, LANES), F32) for _ in range(12)]
    for j in range(NGY):
        spot = landing(gy, j)
        for r in range(4):
            start = (r * NGY + j) * TRI
            chunk, offset = divmod(start, LANES)
            row = pltpu.roll(arrived[pl.ds(4 * spot + r, 1), :], offset, 1)
            inside = jnp.logical_and(lane >= offset, lane < offset + TRI)
            chunks[chunk] = jnp.where(inside, row, chunks[chunk])
            if offset + TRI > LANES:
                chunks[chunk + 1] = jnp.where(lane < offset + TRI - LANES, row, chunks[chunk + 1])
    cells[...] = pltpu.roll(arrived[...], LANES - TRI, 1).astype(jnp.int32)
    wide = [jnp.broadcast_to(c, (8, LANES)) for c in chunks]

    for n in range(8):
        part = n // 4
        copies[n].wait()

        def tile(t, carry):
            rows = pl.ds(pl.multiple_of(t * 8, 8), 8)
            terms = [kernel[part, rows, pl.ds(LANES * c, LANES)] * wide[c] for c in range(12)]
            while len(terms) > 1:
                terms = [a + b for a, b in zip(terms[::2], terms[1::2])] + terms[len(terms) // 2 * 2 :]
            dest = (t // 6) * 96 + part * TRI + (t % 6) * 8
            acc[pl.ds(pl.multiple_of(dest, 8), 8), :] = terms[0]
            return carry

        lax.fori_loop(12 * (n % 4), 12 * (n % 4) + 12, tile, 0, unroll=4)
    row8 = lax.broadcasted_iota(jnp.int32, (8, LANES), 0)
    total = jnp.zeros((8, 2 * TRI), F32)
    for j in range(NGY):
        total = total + lax.dot_general(
            jnp.where(row8 == j, 1.0, 0.0),
            acc[pl.ds(2 * TRI * j, 2 * TRI), :],
            (((1,), (1,)), ((), ())),
            precision=lax.Precision.HIGHEST,
            preferred_element_type=F32,
        )
    out[...] = jnp.zeros((8, LANES), F32)
    out[:, 0 : 2 * TRI] = total


def partial_rates(arrived, kernel, token):
    return pl.pallas_call(
        rates_kernel,
        out_shape=(shape(NGY, LANES), shape(NGX, LANES, dtype=jnp.int32)),
        in_specs=[spec(), spec(HBM), spec(ANY)],
        out_specs=(spec(), spec()),
        scratch_shapes=[VMEM((768, LANES), F32), VMEM(kernel.shape, F32), DMA((8,))],
        compiler_params=pltpu.CompilerParams(vmem_limit_bytes=8 << 20),
        name="rates",
    )(arrived, far(kernel), token)


def around(ref, x, before, after, row, lane):
    rows = pl.ds(row, 8)
    centre = [ref[x * CHUNKS + i, rows, :] for i in range(CHUNKS)]
    left = [pltpu.roll(v, 1, 1) for v in centre]
    right = [pltpu.roll(v, LANES - 1, 1) for v in centre]
    sums = []
    for i in range(CHUNKS):
        below = left[i - 1] if i else 0.0
        above = right[i + 1] if i + 1 < CHUNKS else 0.0
        z = jnp.where(lane == 0, below, left[i]) + jnp.where(lane == LANES - 1, above, right[i])
        y = ref[x * CHUNKS + i, pl.ds(row - 1, 8), :] + ref[x * CHUNKS + i, pl.ds(row + 1, 8), :]
        xs = ref[before * CHUNKS + i, rows, :] + ref[after * CHUNKS + i, rows, :]
        sums.append((xs + y) + z)
    return centre, sums


def stretch(first, last):
    return range(first, last, 8)


EDGES = ((3, 3), (2, 3), (2, 4), (2, 4), (2, 5))


def edge_copies(which, source, edge, sems):
    count, depth = EDGES[which]
    copies = []
    for n in range(count):
        inside = depth - HALO + n
        for side, x in enumerate((inside, CX - 1 - inside)):
            copies.append(
                pltpu.make_async_copy(
                    source.at[pl.ds(x * CHUNKS, CHUNKS)], edge.at[side, pl.ds(n * CHUNKS, CHUNKS)], sems.at[2 * n + side]
                )
            )
    return started(*copies)


def inner_kernel(
    p_far, k_far, y_up, y_down, token, out, s_edge, q_edge, a_edge, q1_edge, q2_edge, s, q, a, q1, q2, p, k, field, sems, edge_sems
):
    del token
    loads = [
        started(
            pltpu.make_async_copy(p_far.at[pl.ds(4 * n, 4)], p.at[pl.ds(4 * n, 4)], sems.at[2 * n]),
            pltpu.make_async_copy(k_far.at[pl.ds(4 * n, 4)], k.at[pl.ds(4 * n, 4)], sems.at[2 * n + 1]),
        )
        for n in range(4)
    ]
    edges = []
    lane = lax.broadcasted_iota(jnp.int32, (8, LANES), 1)
    row = lax.broadcasted_iota(jnp.int32, (8, LANES), 0)

    def convert(x, carry):
        for i in range(CHUNKS):
            lanes = pl.ds(LANES * i, LANES)
            n = x * CHUNKS + i
            halo_p, halo_k = halo_rows(y_up[x, :, lanes], y_down[x, :, lanes], row)
            root = jnp.sqrt(halo_k)
            scaled = root * halo_p
            for place in (0, CY + 8):
                s[n, place : place + 8, :] = root
                q[n, place : place + 8, :] = scaled
            for t in range(CY // 8):
                root = jnp.sqrt(k[x, 8 * t : 8 * t + 8, lanes])
                s[n, 8 * t + 8 : 8 * t + 16, :] = root
                q[n, 8 * t + 8 : 8 * t + 16, :] = root * p[x, 8 * t : 8 * t + 8, lanes]
        return carry

    for n in range(4):
        waited(loads[n])
        lax.fori_loop(4 * n, 4 * n + 4, convert, 0)
    edges += edge_copies(0, s, s_edge, edge_sems.at[0])
    edges += edge_copies(1, q, q_edge, edge_sems.at[1])

    def first(x, carry):
        for r in stretch(6, 74):
            root, sums = around(s, x, x - 1, x + 1, r, lane)
            centre, total = around(q, x, x - 1, x + 1, r, lane)
            for i in range(CHUNKS):
                scaled = conductance * root[i]
                keep = 1.0 - scaled * sums[i]
                a[x * CHUNKS + i, pl.ds(r, 8), :] = keep
                q1[x * CHUNKS + i, pl.ds(r, 8), :] = keep * centre[i] + (scaled * root[i]) * total[i]
        return carry

    lax.fori_loop(1, CX - 1, first, 0)
    edges += edge_copies(2, a, a_edge, edge_sems.at[2])
    edges += edge_copies(3, q1, q1_edge, edge_sems.at[3])

    def second(x, carry):
        for r in stretch(7, 73):
            centre, total = around(q1, x, x - 1, x + 1, r, lane)
            for i in range(CHUNKS):
                root = s[x * CHUNKS + i, pl.ds(r, 8), :]
                keep = a[x * CHUNKS + i, pl.ds(r, 8), :]
                q2[x * CHUNKS + i, pl.ds(r, 8), :] = keep * centre[i] + (conductance * root * root) * total[i]
        return carry

    lax.fori_loop(2, CX - 2, second, 0)
    edges += edge_copies(4, q2, q2_edge, edge_sems.at[4])

    def third(x, carry):
        for r in stretch(8, 72):
            centre, total = around(q2, x, x - 1, x + 1, r, lane)
            for i in range(CHUNKS):
                root = s[x * CHUNKS + i, pl.ds(r, 8), :]
                keep = a[x * CHUNKS + i, pl.ds(r, 8), :]
                field[x - HALO, pl.ds(r - 8, 8), pl.ds(LANES * i, LANES)] = (
                    keep * centre[i] / root + (conductance * root) * total[i]
                )
        return carry

    for n in range(2):
        start = HALO + 5 * n
        lax.fori_loop(start, start + 5, third, 0)
        edges += started(
            pltpu.make_async_copy(field.at[pl.ds(5 * n, 5)], out.at[pl.ds(start, 5)], sems.at[8 + n])
        )
    waited(edges)


def block(planes):
    return VMEM((planes * CHUNKS, ROWS, LANES), F32)


def inner(p, k, y_up, y_down, token):
    return pl.pallas_call(
        inner_kernel,
        out_shape=(shape(CX, CY, NZ),) + tuple(shape(2, n * CHUNKS, ROWS, LANES) for n, _ in EDGES),
        in_specs=[spec(HBM)] * 2 + [spec()] * 2 + [spec(ANY)],
        out_specs=(spec(HBM),) * 6,
        scratch_shapes=[block(CX) for _ in range(5)]
        + [VMEM((CX, CY, NZ), F32), VMEM((CX, CY, NZ), F32), VMEM((CX - 2 * HALO, CY, NZ), F32), DMA((10,)), DMA((5, 6))],
        compiler_params=pltpu.CompilerParams(vmem_limit_bytes=24 << 20),
        cost_estimate=pl.CostEstimate(flops=40_000_000, bytes_accessed=12_000_000, transcendentals=0),
        name="inner",
    )(far(p), far(k), y_up, y_down, token)


def outer_kernel(
    field, s_edge, q_edge, a_edge, q1_edge, q2_edge, x_up, x_down, cells, out, answers, s, q, a, q1, q2, full, asked, sems, edge_sems
):
    del field
    loads = [[], []]
    for side in range(2):
        for n, (edge, target) in enumerate(zip((s_edge, q_edge, a_edge, q1_edge, q2_edge), (s, q, a, q1, q2))):
            count, depth = EDGES[n]
            loads[side] += started(
                pltpu.make_async_copy(
                    edge.at[side], target.at[side, pl.ds(depth * CHUNKS, count * CHUNKS)], edge_sems.at[side, n]
                )
            )
    ask = pltpu.make_async_copy(cells, asked, sems.at[0])
    ask.start()
    fill = pltpu.make_async_copy(
        out.at[pl.ds(HALO, CX - 2 * HALO)], full.at[pl.ds(HALO, CX - 2 * HALO)], sems.at[1]
    )
    fill.start()
    lane = lax.broadcasted_iota(jnp.int32, (8, LANES), 1)
    row = lax.broadcasted_iota(jnp.int32, (8, LANES), 0)
    zero = jnp.zeros((8, LANES), F32)
    stores = []
    both = (s, q, a, q1, q2)
    for side, wide in enumerate((x_up, x_down)):
        s, q, a, q1, q2 = (ref.at[side] for ref in both)
        for d in range(HALO):
            plane = d if side == 0 else HALO - 1 - d
            for i in range(CHUNKS):
                lanes = pl.ds(LANES * i, LANES)
                n = d * CHUNKS + i
                for t in range(CY // 8 + 1):
                    root = jnp.sqrt(wide[HALO + plane, 8 * t : 8 * t + 8, lanes])
                    scaled = root * wide[plane, 8 * t : 8 * t + 8, lanes]
                    for place in (8 * t + 8,) if t < CY // 8 else (0, CY + 8):
                        s[n, place : place + 8, :] = root
                        q[n, place : place + 8, :] = scaled
        waited(loads[side])

        def first(x, carry):
            for r in stretch(6, 74):
                root, sums = around(s, x, x - 1, x + 1, r, lane)
                centre, total = around(q, x, x - 1, x + 1, r, lane)
                for i in range(CHUNKS):
                    scaled = conductance * root[i]
                    keep = 1.0 - scaled * sums[i]
                    a[x * CHUNKS + i, pl.ds(r, 8), :] = keep
                    q1[x * CHUNKS + i, pl.ds(r, 8), :] = keep * centre[i] + (scaled * root[i]) * total[i]
            return carry

        lax.fori_loop(1, 4, first, 0)

        def second(x, carry):
            for r in stretch(7, 73):
                centre, total = around(q1, x, x - 1, x + 1, r, lane)
                for i in range(CHUNKS):
                    root = s[x * CHUNKS + i, pl.ds(r, 8), :]
                    keep = a[x * CHUNKS + i, pl.ds(r, 8), :]
                    q2[x * CHUNKS + i, pl.ds(r, 8), :] = keep * centre[i] + (conductance * root * root) * total[i]
            return carry

        lax.fori_loop(2, 5, second, 0)

        def third(x, carry):
            position = x - 3 if side == 0 else CX + 2 - x
            for r in stretch(8, 72):
                centre, total = around(q2, x, x - 1, x + 1, r, lane)
                for i in range(CHUNKS):
                    root = s[x * CHUNKS + i, pl.ds(r, 8), :]
                    keep = a[x * CHUNKS + i, pl.ds(r, 8), :]
                    full[position, pl.ds(r - 8, 8), pl.ds(LANES * i, LANES)] = (
                        keep * centre[i] / root + (conductance * root) * total[i]
                    )
            return carry

        lax.fori_loop(3, 6, third, 0)
        planes = pl.ds(0 if side == 0 else CX - HALO, HALO)
        store = pltpu.make_async_copy(full.at[planes], out.at[planes], sems.at[2 + side])
        store.start()
        stores.append(store)
    ask.wait()
    fill.wait()

    def answer(d, carry):
        value = zero
        for c in range(3):
            cell = asked[d, c]
            x, y, z = cell >> 15, (cell >> 9) & 63, cell & 511
            lanes = pl.ds(pl.multiple_of((z >> 7) * LANES, LANES), LANES)
            tile = full[x, pl.ds(pl.multiple_of((y >> 3) * 8, 8), 8), lanes]
            tile = pltpu.roll(tile, (LANES + c - (z & 127)) & 127, 1)
            value = jnp.where(jnp.logical_and(row == (y & 7), lane == c), tile, value)
        answers[pl.ds(d, 1), :] = jnp.sum(value, axis=0, keepdims=True)
        return carry

    lax.fori_loop(0, NGX, answer, 0, unroll=4)
    for store in stores:
        store.wait()


def outer(field, edges, x_up, x_down, cells):
    return pl.pallas_call(
        outer_kernel,
        out_shape=(shape(CX, CY, NZ), shape(NGX, LANES)),
        in_specs=[spec(HBM)] * 6 + [spec()] * 2 + [spec(ANY)],
        out_specs=(spec(pltpu.HBM), spec()),
        scratch_shapes=[VMEM((2, n * CHUNKS, ROWS, LANES), F32) for n in (6, 5, 6, 6, 7)]
        + [
            VMEM((CX, CY, NZ), F32),
            pltpu.SMEM((NGX, LANES), jnp.int32),
            DMA((4,)),
            DMA((2, 5)),
        ],
        input_output_aliases={0: 0},
        compiler_params=pltpu.CompilerParams(vmem_limit_bytes=20 << 20),
        name="outer",
    )(field, *edges, x_up, x_down, cells)


def friction_kernel(rates, answers, terms, state_out, rate_out):
    known = terms[...]
    state, aged, normal, shear, direct, owners, rank = (known[i : i + 1, 0:TRI] for i in range(7))
    got = answers[...]
    named = lax.broadcasted_iota(jnp.int32, (NGX, TRI), 0).astype(F32) == owners
    held = jnp.zeros((NGX, TRI), F32)
    for c in range(3):
        held = jnp.where(jnp.logical_and(named, rank == float(c)), got[:, c : c + 1], held)
    pressure = jnp.sum(held, axis=0, keepdims=True)
    both = jnp.sum(rates[...], axis=0, keepdims=True)
    first, second = both[:, 0:TRI], both[:, TRI : 2 * TRI]
    effective = normal + step_time * second - pressure
    state_out[...] = state
    rate_out[...] = ((shear + step_time * first) / effective - friction_ref - aged) / direct


def friction(*values):
    return pl.pallas_call(
        friction_kernel,
        out_shape=(shape(1, TRI), shape(1, TRI)),
        in_specs=[spec()] * len(values),
        out_specs=(spec(), spec()),
        compiler_params=pltpu.CompilerParams(vmem_limit_bytes=4 << 20),
        name="friction",
    )(*values)


def exchanged(value, axis):
    return lax.all_to_all(value, axis, split_axis=0, concat_axis=0, tiled=True)


def local(
    pressure,
    permeability,
    kernel,
    slip_rate,
    aging_state,
    normal_stress,
    shear_stress,
    direct_effect,
    evolution_effect,
    slip_distance,
    tri_owner,
    tri_cell,
):
    moved = lax.ppermute(slip_rate, ("gx", "gy"), SLIP_MOVES)
    rows = (
        tri_owner,
        tri_cell,
        slip_rate,
        aging_state,
        normal_stress,
        shear_stress,
        direct_effect,
        evolution_effect,
        slip_distance,
    )
    y_up, y_down, wanted, terms = prepare(pressure, permeability, *[v.reshape(1, TRI) for v in rows])
    y_up, y_down = lax.ppermute(y_up, "gy", Y_UP), lax.ppermute(y_down, "gy", Y_DOWN)
    lane = lax.broadcasted_iota(jnp.int32, (NGX, LANES), 1)
    row = jnp.pad(moved, (0, LANES - TRI)).reshape(1, LANES)
    leaving = jnp.where(lane < TRI, row, wanted)
    arrived = exchanged(leaving, "gx")
    x_up, x_down = sides(pressure, permeability, y_up, y_down, leaving)
    field, *edges = inner(pressure, permeability, y_up, y_down, x_up)
    x_up, x_down = lax.ppermute(x_up, "gx", X_UP), lax.ppermute(x_down, "gx", X_DOWN)
    partial_sums, cells = partial_rates(arrived, kernel, edges[1])
    rates = exchanged(partial_sums, "gy")
    field, answers = outer(field, edges, x_up, x_down, cells)
    answers = exchanged(answers, "gx")
    state_next, log_rate = friction(rates, answers, terms)
    return field, state_next.reshape(TRI), log_rate.reshape(TRI)


def solution(mesh):
    both = P(("gx", "gy"))
    placed = (
        P("gx", "gy", None),
        P("gx", "gy", None),
        P(None, "gx", "gy"),
        *([both] * 7),
        P(("gx", "gy"), None),
        both,
    )
    return jax.shard_map(
        local,
        mesh=mesh,
        in_specs=placed,
        out_specs=(P("gx", "gy", None), both, both),
        check_vma=False,
    )
```

time: 90.3 us -> 90 us (level)
  blocking collectives: 28.6 us -> 14.4 us
  Pallas kernels: 20.1 us -> 30.2 us
  waiting for transfers between devices: 0.02 us -> 6.52 us
  local copies, waits for them, and re-layouts: 8.42 us -> 5.77 us
  starting transfers between devices: 29.7 us -> 31.1 us
  other arithmetic: 1.99 us -> 0.61 us
    all_to_all x2 -> x1, blocking collectives: 28.6 us -> 14.4 us  [exchanged(): return lax.all_to_all(value, axis, split_axis=0, concat_axis=0, tiled=True)]
    all_to_all x1 -> x2, starting transfers between devices: 7.45 us -> 15.7 us  [exchanged(): return lax.all_to_all(value, axis, split_axis=0, concat_axis=0, tiled=True)]
    pallas_call x1, Pallas kernels: 8.22 us -> 14.5 us  [inner(): pl.pallas_call(inner_kernel, out_shape=(shape(CX, CY, NZ),) + tuple((shap...]
    ppermute x2 -> x0, starting transfers between devices: 5.76 us -> none  [the longest x1 3.85 us: local(): lax.ppermute(jnp.concatenate([y_up[CX - 2:], y_down[CX - 2:]]), 'gx', X_UP)]
    ppermute x1, waiting for transfers between devices: 0.01 us -> 3.83 us  [local(): lax.ppermute(y_down, 'gy', Y_DOWN)]
    ppermute x1, starting transfers between devices: 4.39 us -> 1.57 us  [local(): lax.ppermute(y_up, 'gy', Y_UP)]
    ppermute x1, waiting for transfers between devices: 0.01 us -> 2.68 us  [local(): lax.ppermute(y_up, 'gy', Y_UP)]
    unnamed x17 -> x12, local copies, waits for them, and re-layouts: 8.4 us -> 5.77 us
  transfers between devices with their start and end apart: 8 -> 7, of which waited for: 0 -> 2; matrix products, arithmetic and copies ran while one was open for 3% -> 1% of each run, Pallas kernels for 19% -> 30%
where the time goes in v2:
time: 90 us; the launch traced here: 89.4 us
  starting transfers between devices  31.1 us (35%)
  Pallas kernels  30.2 us (34%)
  blocking collectives  14.4 us (16%)
  waiting for transfers between devices  6.52 us (7%)
  local copies, waits for them, and re-layouts  5.77 us (6%)
    all_to_all x2, starting transfers between devices, exchanged(): return lax.all_to_all(value, axis, split_axis=0, concat_axis=0, tiled=True)  15.7 us
    pallas_call x1, Pallas kernels, inner(): pl.pallas_call(inner_kernel, out_shape=(shape(CX, CY, NZ),) + tuple((shap...  14.5 us
    all_to_all x1, blocking collectives, exchanged(): return lax.all_to_all(value, axis, split_axis=0, concat_axis=0, tiled=True)  14.4 us
    pallas_call x1, Pallas kernels, outer(): pl.pallas_call(outer_kernel, out_shape=(shape(CX, CY, NZ), shape(NGX, LAN...  7.21 us
    ppermute x1, starting transfers between devices, local(): moved = lax.ppermute(slip_rate, ('gx', 'gy'), SLIP_MOVES)  6.28 us
    unnamed x12, local copies, waits for them, and re-layouts  5.77 us
    ppermute x1, starting transfers between devices, local(): lax.ppermute(x_down, 'gx', X_DOWN)  4.07 us
    ppermute x1, waiting for transfers between devices, local(): lax.ppermute(y_down, 'gy', Y_DOWN)  3.83 us
  transfers between devices with their start and end apart: 7, of which 2 were waited for; matrix products, arithmetic and copies ran while one was open for 1% of the time, Pallas kernels for 30%

profile of v2, /device:TPU:1, one launch (start us, length us, event | category | flops | bytes accessed | tf_op | source)
XLA Modules:
  0.0 89.4 jit_solution(1226795282291877203)
XLA Ops:
  0.6 6.3 %collective-permute-start.2 = (f32[48]{0:T(128)}, f32[48]{0:T(128)S(1)}, u32[]{:S(2)}, u32[]{:S(2)}) collective-permute-start(f32[48]{0:T(128)} %param.15), channel_id=1, source_target_pairs={{0,160},{1,96},{2,128},{3,64},{4,0},{5,192},{6,32},{7,224},{8,168}... | collective-permute-start | bytes 584 | tf_op jit(solution)/shard_map/ppermute | solution.py:550
  6.9 1.5 %prepare.1 = (f32[16,8,512]{2,1,0:T(8,128)S(1)}, f32[16,8,512]{2,1,0:T(8,128)S(1)}, f32[32,128]{1,0:T(8,128)S(1)}, f32[8,128]{1,0:T(8,128)S(1)}) custom-call(f32[16,64,512]{2,1,0:T(8,128)} %p_far.1, f32[16,64,512]{2,1,0:T(8,128)} %k_far.1, s32[1,48]{1,0:T(1,128)} %bitcast.27, s32[1,48]{1,0:T(1,128)} %bitcast.28, f32[1,48]{1,0:T(1,128)} %bitcast.35, ...), custom_call_target="tpu_custom_call" | custom-call | tf_op jit(solution)/shard_map/prepare/pallas_call | solution.py:127
  8.4 1.6 %collective-permute-start = (f32[16,8,512]{2,1,0:T(8,128)S(1)}, f32[16,8,512]{2,1,0:T(8,128)S(1)}, u32[]{:S(2)}, u32[]{:S(2)}) collective-permute-start(f32[16,8,512]{2,1,0:T(8,128)S(1)} %get-tuple-element.21), channel_id=1, source_target_pairs={{0,1},{1,2},{2,3},{3,4},{4,5},{5,6},{6,7},{8,9},{9,10},{10,11},{11... | collective-permute-start | bytes 786440 | tf_op jit(solution)/shard_map/ppermute | solution.py:563
  10.0 1.3 %collective-permute-start.1 = (f32[16,8,512]{2,1,0:T(8,128)S(1)}, f32[16,8,512]{2,1,0:T(8,128)S(1)}, u32[]{:S(2)}, u32[]{:S(2)}) collective-permute-start(f32[16,8,512]{2,1,0:T(8,128)S(1)} %get-tuple-element.22), channel_id=1, source_target_pairs={{1,0},{2,1},{3,2},{4,3},{5,4},{6,5},{7,6},{9,8},{10,9},{11,10},{12... | collective-permute-start | bytes 786440 | tf_op jit(solution)/shard_map/ppermute | solution.py:563
  11.3 0.0 collective-permute-done.2
  11.3 0.6 broadcast_select_fusion.token
  11.9 2.7 %collective-permute-done.y_up = f32[16,8,512]{2,1,0:T(8,128)S(1)} collective-permute-done((f32[16,8,512]{2,1,0:T(8,128)S(1)}, f32[16,8,512]{2,1,0:T(8,128)S(1)}, u32[]{:S(2)}, u32[]{:S(2)}) %collective-permute-start) | collective-permute-done | bytes 262176 | tf_op jit(solution)/shard_map/ppermute | solution.py:563
  14.6 3.8 %collective-permute-done.1.y_down = f32[16,8,512]{2,1,0:T(8,128)S(1)} collective-permute-done((f32[16,8,512]{2,1,0:T(8,128)S(1)}, f32[16,8,512]{2,1,0:T(8,128)S(1)}, u32[]{:S(2)}, u32[]{:S(2)}) %collective-permute-start.1) | collective-permute-done | bytes 262176 | tf_op jit(solution)/shard_map/ppermute | solution.py:563
  18.4 2.6 %sides.1 = (f32[6,72,512]{2,1,0:T(8,128)}, f32[6,72,512]{2,1,0:T(8,128)}) custom-call(f32[16,64,512]{2,1,0:T(8,128)} %p_far.1, f32[16,64,512]{2,1,0:T(8,128)} %k_far.1, f32[16,8,512]{2,1,0:T(8,128)S(1)} %collective-permute-done.y_up, f32[16,8,512]{2,1,0:T(8,128)S(1)} %collective-permute-done.1.y_down, f32[32,128]{1,0:T(8,128)} %broadcast_select_fusion.token), custom_call_target="tpu_custom_call" | custom-call | tf_op jit(solution)/shard_map/sides/pallas_call | solution.py:170
  21.0 4.1 %collective-permute-start.4 = (f32[6,72,512]{2,1,0:T(8,128)}, f32[6,72,512]{2,1,0:T(8,128)S(1)}, u32[]{:S(2)}, u32[]{:S(2)}) collective-permute-start(f32[6,72,512]{2,1,0:T(8,128)} %get-tuple-element.31), channel_id=1, source_target_pairs={{8,0},{16,8},{24,16},{32,24},{40,32},{48,40},{56,48},{64,56},{72,6... | collective-permute-start | bytes 2654216 | tf_op jit(solution)/shard_map/ppermute | solution.py:570
  25.1 2.2 %collective-permute-start.3 = (f32[6,72,512]{2,1,0:T(8,128)}, f32[6,72,512]{2,1,0:T(8,128)}, u32[]{:S(2)}, u32[]{:S(2)}) collective-permute-start(f32[6,72,512]{2,1,0:T(8,128)} %get-tuple-element.24.token), channel_id=1, source_target_pairs={{0,8},{8,16},{16,24},{24,32},{32,40},{40,48},{48,56},{56,64},{64,7... | collective-permute-start | bytes 2654216 | tf_op jit(solution)/shard_map/ppermute | solution.py:570
  27.3 11.1 %all-to-all-start = ((f32[32,1,128]{2,1,0:T(1,128)}), f32[32,1,128]{2,1,0:T(1,128)S(1)}, u32[]{:S(2)}, u32[]{:S(2)}) async-start(f32[32,1,128]{2,1,0:T(1,128)} %bitcast.10), calls=%async_computation | async-start | bytes 32768 | tf_op jit(solution)/shard_map/all_to_all | solution.py:533
  38.4 14.5 %inner.1 = (f32[16,64,512]{2,1,0:T(8,128)}, f32[2,12,80,128]{3,2,1,0:T(8,128)S(1)}, f32[2,8,80,128]{3,2,1,0:T(8,128)S(1)}, f32[2,8,80,128]{3,2,1,0:T(8,128)S(1)}...) custom-call(f32[16,64,512]{2,1,0:T(8,128)} %p_far.1, f32[16,64,512]{2,1,0:T(8,128)} %k_far.1, ...), custom_call_target="tpu_custom_call" | custom-call | flops 40000000 | bytes 12000000 | tf_op jit(solution)/shard_map/inner/pallas_call | solution.py:373
  52.9 0.0 copy-start
  52.9 0.8 copy-done
  53.7 0.0 copy-start.2
  53.7 0.8 copy-done.2
  54.6 0.0 copy-start.4
  54.6 0.8 copy-done.4
  55.4 0.0 all-to-all-done
  55.4 3.8 %rates.1 = (f32[8,128]{1,0:T(8,128)}, s32[32,128]{1,0:T(8,128)S(1)}) custom-call(f32[32,128]{1,0:T(8,128)S(1)} %bitcast.23, f32[2,384,1536]{2,1,0:T(8,128)} %kernel_far.1, f32[2,8,80,128]{3,2,1,0:T(8,128)S(1)} %get-tuple-element.27.token.q_edge), custom_call_target="tpu_custom_call" | custom-call | tf_op jit(solution)/shard_map/rates/pallas_call | solution.py:236
  59.2 4.6 %all-to-all-start.1 = ((f32[8,1,128]{2,1,0:T(1,128)}), f32[8,1,128]{2,1,0:T(1,128)S(1)}, u32[]{:S(2)}, u32[]{:S(2)}) async-start(f32[8,1,128]{2,1,0:T(1,128)} %bitcast.13), calls=%async_computation.1 | async-start | bytes 8192 | tf_op jit(solution)/shard_map/all_to_all | solution.py:533
  63.9 0.0 collective-permute-done.4.x_down
  63.9 0.0 collective-permute-done.3.x_up
  63.9 0.0 copy-start.1
  63.9 1.1 %copy-done.1 = f32[2,8,80,128]{3,2,1,0:T(8,128)S(1)} copy-done((f32[2,8,80,128]{3,2,1,0:T(8,128)S(1)}, f32[2,8,80,128]{3,2,1,0:T(8,128)}, u32[]{:S(2)}) %copy-start.1) | copy-done | bytes 655384
  65.0 0.0 copy-start.3
  65.0 1.1 %copy-done.3 = f32[2,8,80,128]{3,2,1,0:T(8,128)S(1)} copy-done((f32[2,8,80,128]{3,2,1,0:T(8,128)S(1)}, f32[2,8,80,128]{3,2,1,0:T(8,128)}, u32[]{:S(2)}) %copy-start.3) | copy-done | bytes 655384
  66.1 0.0 copy-start.5
  66.1 1.1 %copy-done.5 = f32[2,8,80,128]{3,2,1,0:T(8,128)S(1)} copy-done((f32[2,8,80,128]{3,2,1,0:T(8,128)S(1)}, f32[2,8,80,128]{3,2,1,0:T(8,128)}, u32[]{:S(2)}) %copy-start.5) | copy-done | bytes 655384
  67.2 7.2 %outer.1 = (f32[16,64,512]{2,1,0:T(8,128)}, f32[32,128]{1,0:T(8,128)S(1)}) custom-call(f32[16,64,512]{2,1,0:T(8,128)} %get-tuple-element.25.field, f32[2,12,80,128]{3,2,1,0:T(8,128)S(1)} %get-tuple-element.26.s_edge, f32[2,8,80,128]{3,2,1,0:T(8,128)S(1)} %get-tuple-element.27.token.q_edge, ...), custom_call_target="tpu_custom_call", output_to_operand_aliasing={{0}: (0, {})} | custom-call | tf_op jit(solution)/shard_map/outer/pallas_call | solution.py:487
  74.4 0.0 all-to-all-done.1
  74.4 14.4 %all_to_all.33 = f32[32,1,128]{2,1,0:T(1,128)S(1)} all-to-all(f32[32,1,128]{2,1,0:T(1,128)S(1)} %bitcast.25), channel_id=1, replica_groups=mesh['gx'=32,'gy'=8] {'gx'}, dimensions={0} | all-to-all | bytes 32768 | tf_op jit(solution)/shard_map/all_to_all | solution.py:533
  88.8 0.6 friction.1
  (2 shorter events, 0.0 us)
Async XLA Ops:
  0.6 10.6 %collective-permute-start.2 = (f32[48]{0:T(128)}, f32[48]{0:T(128)S(1)}, u32[]{:S(2)}, u32[]{:S(2)}) collective-permute-start(f32[48]{0:T(128)} %param.15), channel_id=1, source_target_pairs={{0,160},{1,96},{2,128},{3,64},{4,0},{5,192},{6,32},{7,224},{8,168}... | collective-permute-start | bytes 584 | tf_op jit(solution)/shard_map/ppermute | solution.py:550
  8.4 6.2 %collective-permute-start = (f32[16,8,512]{2,1,0:T(8,128)S(1)}, f32[16,8,512]{2,1,0:T(8,128)S(1)}, u32[]{:S(2)}, u32[]{:S(2)}) collective-permute-start(f32[16,8,512]{2,1,0:T(8,128)S(1)} %get-tuple-element.21), channel_id=1, source_target_pairs={{0,1},{1,2},{2,3},{3,4},{4,5},{5,6},{6,7},{8,9},{9,10},{10,11},{11... | collective-permute-start | bytes 786440 | tf_op jit(solution)/shard_map/ppermute | solution.py:563
  10.0 8.5 %collective-permute-start.1 = (f32[16,8,512]{2,1,0:T(8,128)S(1)}, f32[16,8,512]{2,1,0:T(8,128)S(1)}, u32[]{:S(2)}, u32[]{:S(2)}) collective-permute-start(f32[16,8,512]{2,1,0:T(8,128)S(1)} %get-tuple-element.22), channel_id=1, source_target_pairs={{1,0},{2,1},{3,2},{4,3},{5,4},{6,5},{7,6},{9,8},{10,9},{11,10},{12... | collective-permute-start | bytes 786440 | tf_op jit(solution)/shard_map/ppermute | solution.py:563
  21.0 42.8 %collective-permute-start.4 = (f32[6,72,512]{2,1,0:T(8,128)}, f32[6,72,512]{2,1,0:T(8,128)S(1)}, u32[]{:S(2)}, u32[]{:S(2)}) collective-permute-start(f32[6,72,512]{2,1,0:T(8,128)} %get-tuple-element.31), channel_id=1, source_target_pairs={{8,0},{16,8},{24,16},{32,24},{40,32},{48,40},{56,48},{64,56},{72,6... | collective-permute-start | bytes 2654216 | tf_op jit(solution)/shard_map/ppermute | solution.py:570
  25.1 38.8 %collective-permute-start.3 = (f32[6,72,512]{2,1,0:T(8,128)}, f32[6,72,512]{2,1,0:T(8,128)}, u32[]{:S(2)}, u32[]{:S(2)}) collective-permute-start(f32[6,72,512]{2,1,0:T(8,128)} %get-tuple-element.24.token), channel_id=1, source_target_pairs={{0,8},{8,16},{16,24},{24,32},{32,40},{40,48},{48,56},{56,64},{64,7... | collective-permute-start | bytes 2654216 | tf_op jit(solution)/shard_map/ppermute | solution.py:570
  27.3 28.1 %all-to-all-start = ((f32[32,1,128]{2,1,0:T(1,128)}), f32[32,1,128]{2,1,0:T(1,128)S(1)}, u32[]{:S(2)}, u32[]{:S(2)}) async-start(f32[32,1,128]{2,1,0:T(1,128)} %bitcast.10), calls=%async_computation | async-start | bytes 32768 | tf_op jit(solution)/shard_map/all_to_all | solution.py:533
  52.9 0.8 copy-start
  53.7 0.8 copy-start.2
  54.6 0.8 copy-start.4
  59.2 15.1 %all-to-all-start.1 = ((f32[8,1,128]{2,1,0:T(1,128)}), f32[8,1,128]{2,1,0:T(1,128)S(1)}, u32[]{:S(2)}, u32[]{:S(2)}) async-start(f32[8,1,128]{2,1,0:T(1,128)} %bitcast.13), calls=%async_computation.1 | async-start | bytes 8192 | tf_op jit(solution)/shard_map/all_to_all | solution.py:533
  63.9 1.1 %copy-start.1 = (f32[2,8,80,128]{3,2,1,0:T(8,128)S(1)}, f32[2,8,80,128]{3,2,1,0:T(8,128)}, u32[]{:S(2)}) copy-start(f32[2,8,80,128]{3,2,1,0:T(8,128)} %copy-done) | copy-start | bytes 1966084
  65.0 1.1 %copy-start.3 = (f32[2,8,80,128]{3,2,1,0:T(8,128)S(1)}, f32[2,8,80,128]{3,2,1,0:T(8,128)}, u32[]{:S(2)}) copy-start(f32[2,8,80,128]{3,2,1,0:T(8,128)} %copy-done.2) | copy-start | bytes 1966084
  66.1 1.1 %copy-start.5 = (f32[2,8,80,128]{3,2,1,0:T(8,128)S(1)}, f32[2,8,80,128]{3,2,1,0:T(8,128)}, u32[]{:S(2)}) copy-start(f32[2,8,80,128]{3,2,1,0:T(8,128)} %copy-done.4) | copy-start | bytes 1966084

commit v3 on v2

v3 whole, which is shorter than its diff:
```python
import jax
import jax.numpy as jnp
from jax import lax
from jax.experimental import pallas as pl
from jax.experimental.pallas import tpu as pltpu
from jax.sharding import PartitionSpec as P

NGX, NGY = 32, 8
CX, CY, NZ, TRI = 16, 64, 512, 48
HALO = 3
ROWS = 80
LANES = 128
CHUNKS = NZ // LANES
conductance = 0.15
step_time = 1.0
heal_time = 0.5
friction_ref = 0.6
F32 = jnp.float32
VMEM = pltpu.VMEM
ANY = pl.ANY

X_MOVE = (2, 1, 2, 1, 0, 3, 0, 3)
Y_MOVE = (1, 1, 0, 0, 0, 0, 1, 1)
X_CODE = sum(v << (2 * i) for i, v in enumerate(X_MOVE))
Y_CODE = sum(v << i for i, v in enumerate(Y_MOVE))


def landing(group, other):
    delta = (other - group) & 7
    x = ((group >> 1) + ((X_CODE >> (2 * delta)) & 3)) & 3
    y = (group & 1) ^ ((Y_CODE >> delta) & 1)
    return 2 * x + y


SLIP_MOVES = [
    ((4 * g + r) * NGY + j, (4 * landing(g, j) + r) * NGY + g) for g in range(8) for r in range(4) for j in range(NGY)
]
X_UP = [(i, i + 1) for i in range(NGX - 1)]
X_DOWN = [(j, i) for i, j in X_UP]
Y_UP = [(i, i + 1) for i in range(NGY - 1)]
Y_DOWN = [(j, i) for i, j in Y_UP]


def spec(space=VMEM):
    return pl.BlockSpec(memory_space=space)


def shape(*dims, dtype=F32):
    return jax.ShapeDtypeStruct(dims, dtype)


def far(value):
    return pltpu.with_memory_space_constraint(value, pltpu.HBM)


def all_far(*values):
    return tuple(far(v) for v in values)


def started(*copies):
    for copy in copies:
        copy.start()
    return copies


def waited(copies):
    for copy in copies:
        copy.wait()


HBM = pltpu.HBM
DMA = pltpu.SemaphoreType.DMA


def turned(row_value):
    row = lax.broadcasted_iota(jnp.int32, (TRI, TRI), 0)
    column = lax.broadcasted_iota(jnp.int32, (TRI, TRI), 1)
    return jnp.sum(jnp.where(row == column, row_value, 0.0), axis=1, keepdims=True)


def pack_kernel(p, k, y_up, y_down, tiles, sems):
    tops = started(
        pltpu.make_async_copy(p.at[:, pl.ds(CY - 8, 8), :], tiles.at[0], sems.at[0]),
        pltpu.make_async_copy(k.at[:, pl.ds(CY - 8, 8), :], tiles.at[1], sems.at[1]),
        pltpu.make_async_copy(p.at[:, pl.ds(0, 8), :], tiles.at[2], sems.at[2]),
        pltpu.make_async_copy(k.at[:, pl.ds(0, 8), :], tiles.at[3], sems.at[3]),
    )
    row = lax.broadcasted_iota(jnp.int32, (8, NZ), 0)
    waited(tops)

    def plane(x, carry):
        y_up[x] = jnp.where(row >= 5, tiles[0, x], pltpu.roll(tiles[1, x], 3, 0))
        y_down[x] = jnp.where(row < 3, tiles[2, x], pltpu.roll(tiles[3, x], 5, 0))
        return carry

    lax.fori_loop(0, CX, plane, 0)


def pack(p, k):
    return pl.pallas_call(
        pack_kernel,
        out_shape=(shape(CX, 8, NZ),) * 2,
        in_specs=[spec(HBM)] * 2,
        out_specs=(spec(),) * 2,
        scratch_shapes=[VMEM((4, CX, 8, NZ), F32), DMA((4,))],
        compiler_params=pltpu.CompilerParams(vmem_limit_bytes=4 << 20),
        name="pack",
    )(far(p), far(k))


def prepare_kernel(owner, cell, *refs):
    floats, (wanted, terms, whole, held, sems) = refs[:7], refs[7:]
    waited(
        started(
            pltpu.make_async_copy(owner, whole.at[0], sems.at[0]),
            pltpu.make_async_copy(cell, whole.at[1], sems.at[1]),
            *[pltpu.make_async_copy(ref, held.at[n], sems.at[2 + n]) for n, ref in enumerate(floats)],
        )
    )
    slip, aging, normal, shear, direct, evolution, distance = (held[n] for n in range(7))
    owners = whole[0].astype(F32)
    first = lax.broadcasted_iota(jnp.int32, (TRI, TRI), 0)
    second = lax.broadcasted_iota(jnp.int32, (TRI, TRI), 1)
    same = jnp.logical_and(turned(owners) == owners, first < second)
    rank = jnp.sum(jnp.where(same, 1.0, 0.0), axis=0, keepdims=True)
    cells = whole[1].astype(F32)
    lane = lax.broadcasted_iota(jnp.int32, (NGX, LANES), 1)
    named = lax.broadcasted_iota(jnp.int32, (NGX, TRI), 0) == whole[0]
    value = jnp.zeros((NGX, LANES), F32)
    for c in range(3):
        asked = jnp.where(jnp.logical_and(named, rank == float(c)), cells, 0.0)
        value = jnp.where(lane == TRI + c, jnp.sum(asked, axis=1, keepdims=True), value)
    wanted[...] = value
    ratio = distance / slip
    state = ratio + (aging - ratio) * jnp.exp(-heal_time / ratio)
    terms[...] = jnp.zeros((8, LANES), F32)
    aged = evolution * jnp.log(state / distance)
    for n, term in enumerate((state, aged, normal, shear, direct, owners, rank)):
        terms[n : n + 1, 0:TRI] = term


def prepare(*values):
    return pl.pallas_call(
        prepare_kernel,
        out_shape=(shape(NGX, LANES), shape(8, LANES)),
        in_specs=[spec(HBM)] * len(values),
        out_specs=(spec(),) * 2,
        scratch_shapes=[VMEM((2, 1, TRI), jnp.int32), VMEM((7, 1, TRI), F32), DMA((9,))],
        compiler_params=pltpu.CompilerParams(vmem_limit_bytes=2 << 20),
        name="prepare",
    )(*all_far(*values))


def halo_rows(low, high, row):
    p = jnp.where(row >= 5, low, jnp.where(row < 3, high, 0.0))
    k = jnp.where(row >= 5, pltpu.roll(low, 5, 0), jnp.where(row < 3, pltpu.roll(high, 3, 0), 0.0))
    return p, k


def sides_kernel(p, k, y_up, y_down, token, x_up, x_down, sems):
    del token
    copies = []
    for side, (target, start) in enumerate(((x_up, CX - HALO), (x_down, 0))):
        for n, source in enumerate((p, k)):
            copies.append(
                pltpu.make_async_copy(
                    source.at[pl.ds(start, HALO)], target.at[pl.ds(HALO * n, HALO), pl.ds(0, CY)], sems.at[2 * side + n]
                )
            )
    started(*copies)
    row = lax.broadcasted_iota(jnp.int32, (8, NZ), 0)
    for target, start in ((x_up, CX - HALO), (x_down, 0)):
        for n in range(HALO):
            halo_p, halo_k = halo_rows(y_up[start + n], y_down[start + n], row)
            target[n, CY : CY + 8, :] = halo_p
            target[HALO + n, CY : CY + 8, :] = halo_k
    waited(copies)


def sides(p, k, y_up, y_down, token):
    return pl.pallas_call(
        sides_kernel,
        out_shape=(shape(2 * HALO, CY + 8, NZ),) * 2,
        in_specs=[spec(HBM)] * 2 + [spec()] * 2 + [spec(ANY)],
        out_specs=(spec(),) * 2,
        scratch_shapes=[DMA((4,))],
        compiler_params=pltpu.CompilerParams(vmem_limit_bytes=4 << 20),
        name="sides",
    )(far(p), far(k), y_up, y_down, token)


def rates_kernel(arrived, kernel_far, out, cells, acc, kernel, sems):
    copies = started(
        *[
            pltpu.make_async_copy(
                kernel_far.at[n // 4, pl.ds(96 * (n % 4), 96)], kernel.at[n // 4, pl.ds(96 * (n % 4), 96)], sems.at[n]
            )
            for n in range(8)
        ]
    )
    gy = lax.axis_index("gy")
    lane = lax.broadcasted_iota(jnp.int32, (1, LANES), 1)
    chunks = [jnp.zeros((1, LANES), F32) for _ in range(12)]
    for j in range(NGY):
        spot = landing(gy, j)
        for r in range(4):
            start = (r * NGY + j) * TRI
            chunk, offset = divmod(start, LANES)
            row = pltpu.roll(arrived[pl.ds(4 * spot + r, 1), :], offset, 1)
            inside = jnp.logical_and(lane >= offset, lane < offset + TRI)
            chunks[chunk] = jnp.where(inside, row, chunks[chunk])
            if offset + TRI > LANES:
                chunks[chunk + 1] = jnp.where(lane < offset + TRI - LANES, row, chunks[chunk + 1])
    cells[...] = pltpu.roll(arrived[...], LANES - TRI, 1).astype(jnp.int32)
    wide = [jnp.broadcast_to(c, (8, LANES)) for c in chunks]

    for n in range(8):
        part = n // 4
        copies[n].wait()

        def tile(t, carry):
            rows = pl.ds(pl.multiple_of(t * 8, 8), 8)
            terms = [kernel[part, rows, pl.ds(LANES * c, LANES)] * wide[c] for c in range(12)]
            while len(terms) > 1:
                terms = [a + b for a, b in zip(terms[::2], terms[1::2])] + terms[len(terms) // 2 * 2 :]
            dest = (t // 6) * 96 + part * TRI + (t % 6) * 8
            acc[pl.ds(pl.multiple_of(dest, 8), 8), :] = terms[0]
            return carry

        lax.fori_loop(12 * (n % 4), 12 * (n % 4) + 12, tile, 0, unroll=4)
    row8 = lax.broadcasted_iota(jnp.int32, (8, LANES), 0)
    total = jnp.zeros((8, 2 * TRI), F32)
    for j in range(NGY):
        total = total + lax.dot_general(
            jnp.where(row8 == j, 1.0, 0.0),
            acc[pl.ds(2 * TRI * j, 2 * TRI), :],
            (((1,), (1,)), ((), ())),
            precision=lax.Precision.HIGHEST,
            preferred_element_type=F32,
        )
    out[...] = jnp.zeros((8, LANES), F32)
    out[:, 0 : 2 * TRI] = total


def partial_rates(arrived, kernel):
    return pl.pallas_call(
        rates_kernel,
        out_shape=(shape(NGY, LANES), shape(NGX, LANES, dtype=jnp.int32)),
        in_specs=[spec(), spec(HBM)],
        out_specs=(spec(), spec()),
        scratch_shapes=[VMEM((768, LANES), F32), VMEM(kernel.shape, F32), DMA((8,))],
        compiler_params=pltpu.CompilerParams(vmem_limit_bytes=8 << 20),
        cost_estimate=pl.CostEstimate(flops=1000000000000, bytes_accessed=6000000000, transcendentals=0),
        name="rates",
    )(arrived, far(kernel))


def around(ref, x, before, after, row, lane):
    rows = pl.ds(row, 8)
    centre = [ref[x * CHUNKS + i, rows, :] for i in range(CHUNKS)]
    left = [pltpu.roll(v, 1, 1) for v in centre]
    right = [pltpu.roll(v, LANES - 1, 1) for v in centre]
    sums = []
    for i in range(CHUNKS):
        below = left[i - 1] if i else 0.0
        above = right[i + 1] if i + 1 < CHUNKS else 0.0
        z = jnp.where(lane == 0, below, left[i]) + jnp.where(lane == LANES - 1, above, right[i])
        y = ref[x * CHUNKS + i, pl.ds(row - 1, 8), :] + ref[x * CHUNKS + i, pl.ds(row + 1, 8), :]
        xs = ref[before * CHUNKS + i, rows, :] + ref[after * CHUNKS + i, rows, :]
        sums.append((xs + y) + z)
    return centre, sums


PLANES = CX + 2 * HALO


def diffusion_kernel(
    p_far, k_far, y_up, y_down, x_up, x_down, cells, out, answers, s, q, a, q1, q2, p, k, full, asked, sems
):
    loads = [
        started(
            pltpu.make_async_copy(p_far.at[pl.ds(4 * n, 4)], p.at[pl.ds(4 * n, 4)], sems.at[2 * n]),
            pltpu.make_async_copy(k_far.at[pl.ds(4 * n, 4)], k.at[pl.ds(4 * n, 4)], sems.at[2 * n + 1]),
        )
        for n in range(4)
    ]
    ask = started(pltpu.make_async_copy(cells, asked, sems.at[8]))
    lane = lax.broadcasted_iota(jnp.int32, (8, LANES), 1)
    row = lax.broadcasted_iota(jnp.int32, (8, LANES), 0)

    def put(n, places, p_tile, k_tile):
        root = jnp.sqrt(k_tile)
        scaled = root * p_tile
        for place in places:
            s[n, place : place + 8, :] = root
            q[n, place : place + 8, :] = scaled

    def outside(wide, base):
        def plane(n, carry):
            for i in range(CHUNKS):
                lanes = pl.ds(LANES * i, LANES)
                for t in range(CY // 8 + 1):
                    places = (8 * t + 8,) if t < CY // 8 else (0, CY + 8)
                    rows = pl.ds(8 * t, 8)
                    put((base + n) * CHUNKS + i, places, wide[n, rows, lanes], wide[HALO + n, rows, lanes])
            return carry

        lax.fori_loop(0, HALO, plane, 0)

    def inside(x, carry):
        for i in range(CHUNKS):
            lanes = pl.ds(LANES * i, LANES)
            n = (x + HALO) * CHUNKS + i
            put(n, (0, CY + 8), *halo_rows(y_up[x, :, lanes], y_down[x, :, lanes], row))
            for t in range(CY // 8):
                rows = pl.ds(8 * t, 8)
                put(n, (8 * t + 8,), p[x, rows, lanes], k[x, rows, lanes])
        return carry

    def first(x, carry):
        for r in range(6, 74, 8):
            root, sums = around(s, x, x - 1, x + 1, r, lane)
            centre, total = around(q, x, x - 1, x + 1, r, lane)
            for i in range(CHUNKS):
                scaled = conductance * root[i]
                keep = 1.0 - scaled * sums[i]
                a[x * CHUNKS + i, pl.ds(r, 8), :] = keep
                q1[x * CHUNKS + i, pl.ds(r, 8), :] = keep * centre[i] + (scaled * root[i]) * total[i]
        return carry

    def second(x, carry):
        for r in range(7, 73, 8):
            centre, total = around(q1, x, x - 1, x + 1, r, lane)
            for i in range(CHUNKS):
                root = s[x * CHUNKS + i, pl.ds(r, 8), :]
                keep = a[x * CHUNKS + i, pl.ds(r, 8), :]
                q2[x * CHUNKS + i, pl.ds(r, 8), :] = keep * centre[i] + (conductance * root * root) * total[i]
        return carry

    def third(x, carry):
        for r in range(8, 72, 8):
            centre, total = around(q2, x, x - 1, x + 1, r, lane)
            for i in range(CHUNKS):
                root = s[x * CHUNKS + i, pl.ds(r, 8), :]
                keep = a[x * CHUNKS + i, pl.ds(r, 8), :]
                full[x - HALO, pl.ds(r - 8, 8), pl.ds(LANES * i, LANES)] = (
                    keep * centre[i] / root + (conductance * root) * total[i]
                )
        return carry

    outside(x_up, 0)
    outside(x_down, PLANES - HALO)
    begin = 1
    for n in range(4):
        waited(loads[n])
        lax.fori_loop(4 * n, 4 * n + 4, inside, 0)
        end = 4 * n + HALO + 3 if n < 3 else PLANES - 1
        lax.fori_loop(begin, end, first, 0)
        begin = end
    lax.fori_loop(2, PLANES - 2, second, 0)
    stores = []
    for n in range(4):
        lax.fori_loop(HALO + 4 * n, HALO + 4 * n + 4, third, 0)
        planes = pl.ds(4 * n, 4)
        stores += started(pltpu.make_async_copy(full.at[planes], out.at[planes], sems.at[9 + n]))
    waited(ask)

    def answer(d, carry):
        value = jnp.zeros((8, LANES), F32)
        for c in range(3):
            cell = asked[d, c]
            x, y, z = cell >> 15, (cell >> 9) & 63, cell & 511
            lanes = pl.ds(pl.multiple_of((z >> 7) * LANES, LANES), LANES)
            tile = full[x, pl.ds(pl.multiple_of((y >> 3) * 8, 8), 8), lanes]
            tile = pltpu.roll(tile, (LANES + c - (z & 127)) & 127, 1)
            value = jnp.where(jnp.logical_and(row == (y & 7), lane == c), tile, value)
        answers[pl.ds(d, 1), :] = jnp.sum(value, axis=0, keepdims=True)
        return carry

    lax.fori_loop(0, NGX, answer, 0, unroll=4)
    waited(stores)


def diffusion(p, k, y_up, y_down, x_up, x_down, cells):
    return pl.pallas_call(
        diffusion_kernel,
        out_shape=(shape(CX, CY, NZ), shape(NGX, LANES)),
        in_specs=[spec(HBM)] * 2 + [spec()] * 4 + [spec(ANY)],
        out_specs=(spec(HBM), spec()),
        scratch_shapes=[VMEM((PLANES * CHUNKS, ROWS, LANES), F32) for _ in range(5)]
        + [VMEM((CX, CY, NZ), F32) for _ in range(3)]
        + [pltpu.SMEM((NGX, LANES), jnp.int32), DMA((13,))],
        compiler_params=pltpu.CompilerParams(vmem_limit_bytes=34 << 20),
        cost_estimate=pl.CostEstimate(flops=60_000_000, bytes_accessed=12_000_000, transcendentals=0),
        name="diffusion",
    )(far(p), far(k), y_up, y_down, x_up, x_down, cells)


def friction_kernel(rates, answers, terms, state_out, rate_out):
    known = terms[...]
    state, aged, normal, shear, direct, owners, rank = (known[i : i + 1, 0:TRI] for i in range(7))
    got = answers[...]
    named = lax.broadcasted_iota(jnp.int32, (NGX, TRI), 0).astype(F32) == owners
    held = jnp.zeros((NGX, TRI), F32)
    for c in range(3):
        held = jnp.where(jnp.logical_and(named, rank == float(c)), got[:, c : c + 1], held)
    pressure = jnp.sum(held, axis=0, keepdims=True)
    both = jnp.sum(rates[...], axis=0, keepdims=True)
    first, second = both[:, 0:TRI], both[:, TRI : 2 * TRI]
    effective = normal + step_time * second - pressure
    state_out[...] = state
    rate_out[...] = ((shear + step_time * first) / effective - friction_ref - aged) / direct


def friction(*values):
    return pl.pallas_call(
        friction_kernel,
        out_shape=(shape(1, TRI), shape(1, TRI)),
        in_specs=[spec()] * len(values),
        out_specs=(spec(), spec()),
        compiler_params=pltpu.CompilerParams(vmem_limit_bytes=4 << 20),
        name="friction",
    )(*values)


def exchanged(value, axis):
    return lax.all_to_all(value, axis, split_axis=0, concat_axis=0, tiled=True)


def local(
    pressure,
    permeability,
    kernel,
    slip_rate,
    aging_state,
    normal_stress,
    shear_stress,
    direct_effect,
    evolution_effect,
    slip_distance,
    tri_owner,
    tri_cell,
):
    rows = (
        tri_owner,
        tri_cell,
        slip_rate,
        aging_state,
        normal_stress,
        shear_stress,
        direct_effect,
        evolution_effect,
        slip_distance,
    )
    y_up, y_down = pack(pressure, permeability)
    wanted, terms = prepare(*[v.reshape(1, TRI) for v in rows])
    y_up, y_down = lax.ppermute(y_up, "gy", Y_UP), lax.ppermute(y_down, "gy", Y_DOWN)
    lane = lax.broadcasted_iota(jnp.int32, (NGX, LANES), 1)
    row = jnp.pad(lax.ppermute(slip_rate, ("gx", "gy"), SLIP_MOVES), (0, LANES - TRI)).reshape(1, LANES)
    leaving = jnp.where(lane < TRI, row, wanted)
    arrived = exchanged(leaving, "gx")
    x_up, x_down = sides(pressure, permeability, y_up, y_down, leaving)
    x_up, x_down = lax.ppermute(x_up, "gx", X_UP), lax.ppermute(x_down, "gx", X_DOWN)
    partial_sums, cells = partial_rates(arrived, kernel)
    rates = exchanged(partial_sums, "gy")
    field, answers = diffusion(pressure, permeability, y_up, y_down, x_up, x_down, cells)
    answers = exchanged(answers, "gx")
    state_next, log_rate = friction(rates, answers, terms)
    return field, state_next.reshape(TRI), log_rate.reshape(TRI)


def solution(mesh):
    both = P(("gx", "gy"))
    placed = (
        P("gx", "gy", None),
        P("gx", "gy", None),
        P(None, "gx", "gy"),
        *([both] * 7),
        P(("gx", "gy"), None),
        both,
    )
    return jax.shard_map(
        local,
        mesh=mesh,
        in_specs=placed,
        out_specs=(P("gx", "gy", None), both, both),
        check_vma=False,
    )
```

time: 90 us -> 75 us (0.83)
  Pallas kernels: 30.2 us -> 23.5 us
  local copies, waits for them, and re-layouts: 5.77 us -> 0.01 us
  waiting for transfers between devices: 6.52 us -> 3.15 us
    pallas_call x3, Pallas kernels: 23.1 us -> 16.5 us  [the longest x1 14.1 us: diffusion(): pl.pallas_call(diffusion_kernel, out_shape=(shape(CX, CY, NZ), shape(NGX,...]
    unnamed x12 -> x0, local copies, waits for them, and re-layouts: 5.77 us -> none
    ppermute x1, waiting for transfers between devices: 3.83 us -> 0.01 us  [local(): lax.ppermute(y_down, 'gy', Y_DOWN)]
    ppermute x1, waiting for transfers between devices: 0.01 us -> 3.13 us  [local(): lax.ppermute(x_down, 'gx', X_DOWN)]
    ppermute x1, waiting for transfers between devices: 2.68 us -> 0.01 us  [local(): lax.ppermute(y_up, 'gy', Y_UP)]
    ppermute x1, starting transfers between devices: 4.07 us -> 1.92 us  [local(): lax.ppermute(x_down, 'gx', X_DOWN)]
    ppermute x1, starting transfers between devices: 2.2 us -> 3.54 us  [local(): lax.ppermute(x_up, 'gx', X_UP)]
    all_to_all x2, starting transfers between devices: 15.7 us -> 16.7 us  [exchanged(): return lax.all_to_all(value, axis, split_axis=0, concat_axis=0, tiled=True)]
  transfers between devices with their start and end apart: 7 -> 7, of which waited for: 2 -> 1; matrix products, arithmetic and copies ran while one was open for 1% -> 1% of each run, Pallas kernels for 30% -> 31%
where the time goes in v3:
time: 75 us; the launch traced here: 74.6 us
  starting transfers between devices  31.3 us (42%)
  Pallas kernels  23.5 us (31%)
  blocking collectives  15.2 us (20%)
  waiting for transfers between devices  3.15 us (4%)
  between operations  0.77 us (1%)
    all_to_all x2, starting transfers between devices, exchanged(): return lax.all_to_all(value, axis, split_axis=0, concat_axis=0, tiled=True)  16.7 us
    all_to_all x1, blocking collectives, exchanged(): return lax.all_to_all(value, axis, split_axis=0, concat_axis=0, tiled=True)  15.2 us
    pallas_call x1, Pallas kernels, diffusion(): pl.pallas_call(diffusion_kernel, out_shape=(shape(CX, CY, NZ), shape(NGX,...  14.1 us
    ppermute x1, starting transfers between devices, local(): lax.ppermute(slip_rate, ('gx', 'gy'), SLIP_MOVES)  6.28 us
    pallas_call x1, Pallas kernels, partial_rates(): pl.pallas_call(rates_kernel, out_shape=(shape(NGY, LANES), shape(NGX, LAN...  3.83 us
    ppermute x1, starting transfers between devices, local(): lax.ppermute(x_up, 'gx', X_UP)  3.54 us
    ppermute x1, waiting for transfers between devices, local(): lax.ppermute(x_down, 'gx', X_DOWN)  3.13 us
    pallas_call x1, Pallas kernels, sides(): pl.pallas_call(sides_kernel, out_shape=(shape(2 * HALO, CY + 8, NZ),) * 2...  2.59 us
  transfers between devices with their start and end apart: 7, of which 1 were waited for; matrix products, arithmetic and copies ran while one was open for 1% of the time, Pallas kernels for 31%

profile of v3, /device:TPU:1, one launch (start us, length us, event | category | flops | bytes accessed | tf_op | source)
XLA Modules:
  0.0 74.6 jit_solution(4278014897495054266)
XLA Ops:
  0.6 6.3 %collective-permute-start.2 = (f32[48]{0:T(128)}, f32[48]{0:T(128)S(1)}, u32[]{:S(2)}, u32[]{:S(2)}) collective-permute-start(f32[48]{0:T(128)} %param.15), channel_id=1, source_target_pairs={{0,160},{1,96},{2,128},{3,64},{4,0},{5,192},{6,32},{7,224},{8,168}... | collective-permute-start | bytes 584 | tf_op jit(solution)/shard_map/ppermute | solution.py:459
  6.9 1.3 %pack.1 = (f32[16,8,512]{2,1,0:T(8,128)S(1)}, f32[16,8,512]{2,1,0:T(8,128)S(1)}) custom-call(f32[16,64,512]{2,1,0:T(8,128)} %p_far.1, f32[16,64,512]{2,1,0:T(8,128)} %k_far.1), custom_call_target="tpu_custom_call" | custom-call | tf_op jit(solution)/shard_map/pack/pallas_call | solution.py:100
  8.2 1.6 %collective-permute-start = (f32[16,8,512]{2,1,0:T(8,128)S(1)}, f32[16,8,512]{2,1,0:T(8,128)S(1)}, u32[]{:S(2)}, u32[]{:S(2)}) collective-permute-start(f32[16,8,512]{2,1,0:T(8,128)S(1)} %get-tuple-element.15), channel_id=1, source_target_pairs={{0,1},{1,2},{2,3},{3,4},{4,5},{5,6},{6,7},{8,9},{9,10},{10,11},{11... | collective-permute-start | bytes 786440 | tf_op jit(solution)/shard_map/ppermute | solution.py:457
  9.8 1.3 %collective-permute-start.1 = (f32[16,8,512]{2,1,0:T(8,128)S(1)}, f32[16,8,512]{2,1,0:T(8,128)S(1)}, u32[]{:S(2)}, u32[]{:S(2)}) collective-permute-start(f32[16,8,512]{2,1,0:T(8,128)S(1)} %get-tuple-element.16), channel_id=1, source_target_pairs={{1,0},{2,1},{3,2},{4,3},{5,4},{6,5},{7,6},{9,8},{10,9},{11,10},{12... | collective-permute-start | bytes 786440 | tf_op jit(solution)/shard_map/ppermute | solution.py:457
  11.1 1.1 %prepare.1 = (f32[32,128]{1,0:T(8,128)S(1)}, f32[8,128]{1,0:T(8,128)S(1)}) custom-call(s32[1,48]{1,0:T(1,128)} %bitcast.27, s32[1,48]{1,0:T(1,128)} %bitcast.28, f32[1,48]{1,0:T(1,128)} %bitcast.35, f32[1,48]{1,0:T(1,128)} %bitcast.29, f32[1,48]{1,0:T(1,128)} %bitcast.30, f32[1,48]{1,0:T(1,128)} %bitcast.31, f32[1,48]{1,0:T(1,128)} %bitcast.32, ...), custom_call_target="tpu_custom_call" | custom-call | tf_op jit(solution)/shard_map/prepare/pallas_call | solution.py:143
  12.2 0.0 collective-permute-done.2
  12.2 0.6 broadcast_select_fusion.token
  12.8 10.9 %all-to-all-start = ((f32[32,1,128]{2,1,0:T(1,128)}), f32[32,1,128]{2,1,0:T(1,128)S(1)}, u32[]{:S(2)}, u32[]{:S(2)}) async-start(f32[32,1,128]{2,1,0:T(1,128)} %bitcast.10), calls=%async_computation | async-start | bytes 32768 | tf_op jit(solution)/shard_map/all_to_all | solution.py:427
  23.8 0.0 collective-permute-done.y_up
  23.8 0.0 collective-permute-done.1.y_down
  23.8 2.6 %sides.1 = (f32[6,72,512]{2,1,0:T(8,128)}, f32[6,72,512]{2,1,0:T(8,128)}) custom-call(f32[16,64,512]{2,1,0:T(8,128)} %p_far.1, f32[16,64,512]{2,1,0:T(8,128)} %k_far.1, f32[16,8,512]{2,1,0:T(8,128)S(1)} %collective-permute-done.y_up, f32[16,8,512]{2,1,0:T(8,128)S(1)} %collective-permute-done.1.y_down, f32[32,128]{1,0:T(8,128)} %broadcast_select_fusion.token), custom_call_target="tpu_custom_call" | custom-call | tf_op jit(solution)/shard_map/sides/pallas_call | solution.py:181
  26.4 3.5 %collective-permute-start.3 = (f32[6,72,512]{2,1,0:T(8,128)}, f32[6,72,512]{2,1,0:T(8,128)}, u32[]{:S(2)}, u32[]{:S(2)}) collective-permute-start(f32[6,72,512]{2,1,0:T(8,128)} %get-tuple-element.18), channel_id=1, source_target_pairs={{0,8},{8,16},{16,24},{24,32},{32,40},{40,48},{48,56},{56,64},{64,7... | collective-permute-start | bytes 2654216 | tf_op jit(solution)/shard_map/ppermute | solution.py:463
  29.9 1.9 %collective-permute-start.4 = (f32[6,72,512]{2,1,0:T(8,128)}, f32[6,72,512]{2,1,0:T(8,128)}, u32[]{:S(2)}, u32[]{:S(2)}) collective-permute-start(f32[6,72,512]{2,1,0:T(8,128)} %get-tuple-element.19), channel_id=1, source_target_pairs={{8,0},{16,8},{24,16},{32,24},{40,32},{48,40},{56,48},{64,56},{72,6... | collective-permute-start | bytes 2654216 | tf_op jit(solution)/shard_map/ppermute | solution.py:463
  31.9 0.0 all-to-all-done
  31.9 3.8 %rates.1 = (f32[8,128]{1,0:T(8,128)}, s32[32,128]{1,0:T(8,128)S(1)}) custom-call(f32[32,128]{1,0:T(8,128)S(1)} %bitcast.24, f32[2,384,1536]{2,1,0:T(8,128)} %kernel_far.1), custom_call_target="tpu_custom_call" | custom-call | flops 999999995904 | bytes 6000000000 | tf_op jit(solution)/shard_map/rates/pallas_call | solution.py:246
  35.7 5.8 %all-to-all-start.1 = ((f32[8,1,128]{2,1,0:T(1,128)}), f32[8,1,128]{2,1,0:T(1,128)S(1)}, u32[]{:S(2)}, u32[]{:S(2)}) async-start(f32[8,1,128]{2,1,0:T(1,128)} %bitcast.13), calls=%async_computation.1 | async-start | bytes 8192 | tf_op jit(solution)/shard_map/all_to_all | solution.py:427
  41.5 0.0 collective-permute-done.3.x_up
  41.5 3.1 %collective-permute-done.4.x_down = f32[6,72,512]{2,1,0:T(8,128)} collective-permute-done((f32[6,72,512]{2,1,0:T(8,128)}, f32[6,72,512]{2,1,0:T(8,128)}, u32[]{:S(2)}, u32[]{:S(2)}) %collective-permute-start.4) | collective-permute-done | bytes 884768 | tf_op jit(solution)/shard_map/ppermute | solution.py:463
  44.6 14.1 %diffusion.1 = (f32[16,64,512]{2,1,0:T(8,128)}, f32[32,128]{1,0:T(8,128)S(1)}) custom-call(f32[16,64,512]{2,1,0:T(8,128)} %p_far.1, f32[16,64,512]{2,1,0:T(8,128)} %k_far.1, f32[16,8,512]{2,1,0:T(8,128)S(1)} %collective-permute-done.y_up, f32[16,8,512]{2,1,0:T(8,128)S(1)} %collective-permute-done.1.y_down, f32[6,72,512]{2,1,0:T(8,128)} %collective-permute-done.3.x_up, ...), custom_call_target="tpu_custom_call" | custom-call | flops 60000000 | bytes 12000000 | tf_op jit(solution)/shard_map/diffusion/pallas_call | solution.py:385
  58.7 0.0 all-to-all-done.1
  58.8 15.2 %all_to_all.33 = f32[32,1,128]{2,1,0:T(1,128)S(1)} all-to-all(f32[32,1,128]{2,1,0:T(1,128)S(1)} %bitcast.25), channel_id=1, replica_groups=mesh['gx'=32,'gy'=8] {'gx'}, dimensions={0} | all-to-all | bytes 32768 | tf_op jit(solution)/shard_map/all_to_all | solution.py:427
  74.0 0.6 friction.1
  (2 shorter events, 0.0 us)
Async XLA Ops:
  0.6 11.6 %collective-permute-start.2 = (f32[48]{0:T(128)}, f32[48]{0:T(128)S(1)}, u32[]{:S(2)}, u32[]{:S(2)}) collective-permute-start(f32[48]{0:T(128)} %param.15), channel_id=1, source_target_pairs={{0,160},{1,96},{2,128},{3,64},{4,0},{5,192},{6,32},{7,224},{8,168}... | collective-permute-start | bytes 584 | tf_op jit(solution)/shard_map/ppermute | solution.py:459
  8.2 15.5 %collective-permute-start = (f32[16,8,512]{2,1,0:T(8,128)S(1)}, f32[16,8,512]{2,1,0:T(8,128)S(1)}, u32[]{:S(2)}, u32[]{:S(2)}) collective-permute-start(f32[16,8,512]{2,1,0:T(8,128)S(1)} %get-tuple-element.15), channel_id=1, source_target_pairs={{0,1},{1,2},{2,3},{3,4},{4,5},{5,6},{6,7},{8,9},{9,10},{10,11},{11... | collective-permute-start | bytes 786440 | tf_op jit(solution)/shard_map/ppermute | solution.py:457
  9.8 14.0 %collective-permute-start.1 = (f32[16,8,512]{2,1,0:T(8,128)S(1)}, f32[16,8,512]{2,1,0:T(8,128)S(1)}, u32[]{:S(2)}, u32[]{:S(2)}) collective-permute-start(f32[16,8,512]{2,1,0:T(8,128)S(1)} %get-tuple-element.16), channel_id=1, source_target_pairs={{1,0},{2,1},{3,2},{4,3},{5,4},{6,5},{7,6},{9,8},{10,9},{11,10},{12... | collective-permute-start | bytes 786440 | tf_op jit(solution)/shard_map/ppermute | solution.py:457
  12.8 19.1 %all-to-all-start = ((f32[32,1,128]{2,1,0:T(1,128)}), f32[32,1,128]{2,1,0:T(1,128)S(1)}, u32[]{:S(2)}, u32[]{:S(2)}) async-start(f32[32,1,128]{2,1,0:T(1,128)} %bitcast.10), calls=%async_computation | async-start | bytes 32768 | tf_op jit(solution)/shard_map/all_to_all | solution.py:427
  26.4 15.1 %collective-permute-start.3 = (f32[6,72,512]{2,1,0:T(8,128)}, f32[6,72,512]{2,1,0:T(8,128)}, u32[]{:S(2)}, u32[]{:S(2)}) collective-permute-start(f32[6,72,512]{2,1,0:T(8,128)} %get-tuple-element.18), channel_id=1, source_target_pairs={{0,8},{8,16},{16,24},{24,32},{32,40},{40,48},{48,56},{56,64},{64,7... | collective-permute-start | bytes 2654216 | tf_op jit(solution)/shard_map/ppermute | solution.py:463
  29.9 14.7 %collective-permute-start.4 = (f32[6,72,512]{2,1,0:T(8,128)}, f32[6,72,512]{2,1,0:T(8,128)}, u32[]{:S(2)}, u32[]{:S(2)}) collective-permute-start(f32[6,72,512]{2,1,0:T(8,128)} %get-tuple-element.19), channel_id=1, source_target_pairs={{8,0},{16,8},{24,16},{32,24},{40,32},{48,40},{56,48},{64,56},{72,6... | collective-permute-start | bytes 2654216 | tf_op jit(solution)/shard_map/ppermute | solution.py:463
  35.7 23.0 %all-to-all-start.1 = ((f32[8,1,128]{2,1,0:T(1,128)}), f32[8,1,128]{2,1,0:T(1,128)S(1)}, u32[]{:S(2)}, u32[]{:S(2)}) async-start(f32[8,1,128]{2,1,0:T(1,128)} %bitcast.13), calls=%async_computation.1 | async-start | bytes 8192 | tf_op jit(solution)/shard_map/all_to_all | solution.py:427

commit v4 on v3

--- a/solution.py
+++ b/solution.py
@@ -78,13 +78,24 @@
     return jnp.sum(jnp.where(row == column, row_value, 0.0), axis=1, keepdims=True)
 
 
-def pack_kernel(p, k, y_up, y_down, tiles, sems):
+def pack_kernel(p, k, y_up, y_down, x_up, x_down, tiles, sems):
     tops = started(
         pltpu.make_async_copy(p.at[:, pl.ds(CY - 8, 8), :], tiles.at[0], sems.at[0]),
         pltpu.make_async_copy(k.at[:, pl.ds(CY - 8, 8), :], tiles.at[1], sems.at[1]),
         pltpu.make_async_copy(p.at[:, pl.ds(0, 8), :], tiles.at[2], sems.at[2]),
         pltpu.make_async_copy(k.at[:, pl.ds(0, 8), :], tiles.at[3], sems.at[3]),
     )
+    copies = []
+    for side, (target, start) in enumerate(((x_up, CX - HALO), (x_down, 0))):
+        for n, source in enumerate((p, k)):
+            copies.append(
+                pltpu.make_async_copy(
+                    source.at[pl.ds(start, HALO)],
+                    target.at[pl.ds(HALO * n, HALO), pl.ds(0, CY)],
+                    sems.at[4 + 2 * side + n],
+                )
+            )
+    started(*copies)
     row = lax.broadcasted_iota(jnp.int32, (8, NZ), 0)
     waited(tops)
 
@@ -94,15 +105,16 @@
         return carry
 
     lax.fori_loop(0, CX, plane, 0)
+    waited(copies)
 
 
 def pack(p, k):
     return pl.pallas_call(
         pack_kernel,
-        out_shape=(shape(CX, 8, NZ),) * 2,
+        out_shape=(shape(CX, 8, NZ),) * 2 + (HBM((2 * HALO, CY + 8, NZ), F32),) * 2,
         in_specs=[spec(HBM)] * 2,
-        out_specs=(spec(),) * 2,
-        scratch_shapes=[VMEM((4, CX, 8, NZ), F32), DMA((4,))],
+        out_specs=(spec(),) * 2 + (spec(HBM),) * 2,
+        scratch_shapes=[VMEM((4, CX, 8, NZ), F32), DMA((8,))],
         compiler_params=pltpu.CompilerParams(vmem_limit_bytes=4 << 20),
         name="pack",
     )(far(p), far(k))
@@ -157,36 +169,28 @@
     return p, k
 
 
-def sides_kernel(p, k, y_up, y_down, token, x_up, x_down, sems):
-    del token
+def sides_kernel(x_up, x_down, y_up, y_down, token, x_up_out, x_down_out, tiles, sems):
+    del x_up, x_down, token
+    row = lax.broadcasted_iota(jnp.int32, (8, NZ), 0)
     copies = []
-    for side, (target, start) in enumerate(((x_up, CX - HALO), (x_down, 0))):
-        for n, source in enumerate((p, k)):
-            copies.append(
-                pltpu.make_async_copy(
-                    source.at[pl.ds(start, HALO)], target.at[pl.ds(HALO * n, HALO), pl.ds(0, CY)], sems.at[2 * side + n]
-                )
-            )
-    started(*copies)
-    row = lax.broadcasted_iota(jnp.int32, (8, NZ), 0)
-    for target, start in ((x_up, CX - HALO), (x_down, 0)):
+    for side, (target, start) in enumerate(((x_up_out, CX - HALO), (x_down_out, 0))):
         for n in range(HALO):
-            halo_p, halo_k = halo_rows(y_up[start + n], y_down[start + n], row)
-            target[n, CY : CY + 8, :] = halo_p
-            target[HALO + n, CY : CY + 8, :] = halo_k
+            tiles[side, n], tiles[side, HALO + n] = halo_rows(y_up[start + n], y_down[start + n], row)
+        copies += started(pltpu.make_async_copy(tiles.at[side], target.at[:, pl.ds(CY, 8)], sems.at[side]))
     waited(copies)
 
 
-def sides(p, k, y_up, y_down, token):
+def sides(x_up, x_down, y_up, y_down, token):
     return pl.pallas_call(
         sides_kernel,
-        out_shape=(shape(2 * HALO, CY + 8, NZ),) * 2,
+        out_shape=(HBM((2 * HALO, CY + 8, NZ), F32),) * 2,
         in_specs=[spec(HBM)] * 2 + [spec()] * 2 + [spec(ANY)],
-        out_specs=(spec(),) * 2,
-        scratch_shapes=[DMA((4,))],
+        out_specs=(spec(HBM),) * 2,
+        scratch_shapes=[VMEM((2, 2 * HALO, 8, NZ), F32), DMA((2,))],
+        input_output_aliases={0: 0, 1: 1},
         compiler_params=pltpu.CompilerParams(vmem_limit_bytes=4 << 20),
         name="sides",
-    )(far(p), far(k), y_up, y_down, token)
+    )(far(x_up), far(x_down), y_up, y_down, token)
 
 
 def rates_kernel(arrived, kernel_far, out, cells, acc, kernel, sems):
@@ -275,15 +279,19 @@
 
 
 def diffusion_kernel(
-    p_far, k_far, y_up, y_down, x_up, x_down, cells, out, answers, s, q, a, q1, q2, p, k, full, asked, sems
+    p_far, k_far, y_up, y_down, x_up, x_down, cells, out, answers, s, q, a, q1, q2, p, k, full, wide, asked, sems
 ):
-    loads = [
-        started(
-            pltpu.make_async_copy(p_far.at[pl.ds(4 * n, 4)], p.at[pl.ds(4 * n, 4)], sems.at[2 * n]),
-            pltpu.make_async_copy(k_far.at[pl.ds(4 * n, 4)], k.at[pl.ds(4 * n, 4)], sems.at[2 * n + 1]),
+    loads = []
+    low = started(pltpu.make_async_copy(x_up, wide.at[0], sems.at[12]))
+    for n in range(4):
+        planes = pl.ds(4 * n, 4)
+        loads.append(
+            started(
+                pltpu.make_async_copy(p_far.at[planes], p.at[planes], sems.at[2 * n]),
+                pltpu.make_async_copy(k_far.at[planes], k.at[planes], sems.at[2 * n + 1]),
+            )
         )
-        for n in range(4)
-    ]
+    high = started(pltpu.make_async_copy(x_down, wide.at[1], sems.at[13]))
     ask = started(pltpu.make_async_copy(cells, asked, sems.at[8]))
     lane = lax.broadcasted_iota(jnp.int32, (8, LANES), 1)
     row = lax.broadcasted_iota(jnp.int32, (8, LANES), 0)
@@ -295,14 +303,14 @@
             s[n, place : place + 8, :] = root
             q[n, place : place + 8, :] = scaled
 
-    def outside(wide, base):
+    def outside(side, base):
         def plane(n, carry):
             for i in range(CHUNKS):
                 lanes = pl.ds(LANES * i, LANES)
                 for t in range(CY // 8 + 1):
                     places = (8 * t + 8,) if t < CY // 8 else (0, CY + 8)
                     rows = pl.ds(8 * t, 8)
-                    put((base + n) * CHUNKS + i, places, wide[n, rows, lanes], wide[HALO + n, rows, lanes])
+                    put((base + n) * CHUNKS + i, places, wide[side, n, rows, lanes], wide[side, HALO + n, rows, lanes])
             return carry
 
         lax.fori_loop(0, HALO, plane, 0)
@@ -348,21 +356,36 @@
                 )
         return carry
 
-    outside(x_up, 0)
-    outside(x_down, PLANES - HALO)
-    begin = 1
-    for n in range(4):
-        waited(loads[n])
-        lax.fori_loop(4 * n, 4 * n + 4, inside, 0)
-        end = 4 * n + HALO + 3 if n < 3 else PLANES - 1
-        lax.fori_loop(begin, end, first, 0)
-        begin = end
-    lax.fori_loop(2, PLANES - 2, second, 0)
+    waited(low)
+    outside(0, 0)
+
+    def run(begin, end, *stages):
+        def step(x, carry):
+            for stage, shift in stages:
+                stage(x + shift, 0)
+            return carry
+
+        lax.fori_loop(begin, end, step, 0)
+
+    t, u, f, c = (third, -3), (second, -1), (first, 1), (inside, 0)
     stores = []
-    for n in range(4):
-        lax.fori_loop(HALO + 4 * n, HALO + 4 * n + 4, third, 0)
-        planes = pl.ds(4 * n, 4)
-        stores += started(pltpu.make_async_copy(full.at[planes], out.at[planes], sems.at[9 + n]))
+    waited(loads[0])
+    run(0, 3, f, c)
+    run(3, 4, u, f, c)
+    waited(loads[1])
+    run(4, 6, u, f, c)
+    run(6, 8, t, u, f, c)
+    waited(loads[2] + loads[3])
+    run(8, 14, t, u, f, c)
+    stores += started(pltpu.make_async_copy(full.at[pl.ds(0, 8)], out.at[pl.ds(0, 8)], sems.at[9]))
+    run(14, 16, t, u, f, c)
+    waited(high)
+    outside(1, PLANES - HALO)
+    run(16, 20, t, u, f)
+    stores += started(pltpu.make_async_copy(full.at[pl.ds(8, 6)], out.at[pl.ds(8, 6)], sems.at[10]))
+    run(20, 21, t, u)
+    run(21, 22, t)
+    stores += started(pltpu.make_async_copy(full.at[pl.ds(14, 2)], out.at[pl.ds(14, 2)], sems.at[11]))
     waited(ask)
 
     def answer(d, carry):
@@ -385,11 +408,11 @@
     return pl.pallas_call(
         diffusion_kernel,
         out_shape=(shape(CX, CY, NZ), shape(NGX, LANES)),
-        in_specs=[spec(HBM)] * 2 + [spec()] * 4 + [spec(ANY)],
+        in_specs=[spec(HBM)] * 2 + [spec()] * 2 + [spec(ANY)] * 3,
         out_specs=(spec(HBM), spec()),
         scratch_shapes=[VMEM((PLANES * CHUNKS, ROWS, LANES), F32) for _ in range(5)]
         + [VMEM((CX, CY, NZ), F32) for _ in range(3)]
-        + [pltpu.SMEM((NGX, LANES), jnp.int32), DMA((13,))],
+        + [VMEM((2, 2 * HALO, CY + 8, NZ), F32), pltpu.SMEM((NGX, LANES), jnp.int32), DMA((14,))],
         compiler_params=pltpu.CompilerParams(vmem_limit_bytes=34 << 20),
         cost_estimate=pl.CostEstimate(flops=60_000_000, bytes_accessed=12_000_000, transcendentals=0),
         name="diffusion",
@@ -452,14 +475,14 @@
         evolution_effect,
         slip_distance,
     )
-    y_up, y_down = pack(pressure, permeability)
+    y_up, y_down, x_up, x_down = pack(pressure, permeability)
     wanted, terms = prepare(*[v.reshape(1, TRI) for v in rows])
     y_up, y_down = lax.ppermute(y_up, "gy", Y_UP), lax.ppermute(y_down, "gy", Y_DOWN)
     lane = lax.broadcasted_iota(jnp.int32, (NGX, LANES), 1)
     row = jnp.pad(lax.ppermute(slip_rate, ("gx", "gy"), SLIP_MOVES), (0, LANES - TRI)).reshape(1, LANES)
     leaving = jnp.where(lane < TRI, row, wanted)
     arrived = exchanged(leaving, "gx")
-    x_up, x_down = sides(pressure, permeability, y_up, y_down, leaving)
+    x_up, x_down = sides(x_up, x_down, y_up, y_down, leaving)
     x_up, x_down = lax.ppermute(x_up, "gx", X_UP), lax.ppermute(x_down, "gx", X_DOWN)
     partial_sums, cells = partial_rates(arrived, kernel)
     rates = exchanged(partial_sums, "gy")

time: 75 us -> 116 us (1.55)
  Pallas kernels: 23.5 us -> 65 us
    pallas_call x2, Pallas kernels: 3.91 us -> 49.5 us  [the longest x1 48.8 us: pack(): pl.pallas_call(pack_kernel, out_shape=(shape(CX, 8, NZ),) * 2 + (HBM((2 *...]
    pallas_call x1, Pallas kernels: 14.1 us -> 9.95 us  [diffusion(): pl.pallas_call(diffusion_kernel, out_shape=(shape(CX, CY, NZ), shape(NGX,...]
  transfers between devices with their start and end apart: 7 -> 7, of which waited for: 1 -> 2; matrix products, arithmetic and copies ran while one was open for 1% -> 1% of each run, Pallas kernels for 31% -> 55%
where the time goes in v4:
time: 116 us
  Pallas kernels  65 us (56%)
  starting transfers between devices  31.3 us (27%)
  blocking collectives  15.2 us (13%)
  waiting for transfers between devices  3.17 us (3%)
    pallas_call x1, Pallas kernels, pack(): pl.pallas_call(pack_kernel, out_shape=(shape(CX, 8, NZ),) * 2 + (HBM((2 *...  48.8 us
    all_to_all x2, starting transfers between devices, exchanged(): return lax.all_to_all(value, axis, split_axis=0, concat_axis=0, tiled=True)  16.7 us
    all_to_all x1, blocking collectives, exchanged(): return lax.all_to_all(value, axis, split_axis=0, concat_axis=0, tiled=True)  15.2 us
    pallas_call x1, Pallas kernels, diffusion(): pl.pallas_call(diffusion_kernel, out_shape=(shape(CX, CY, NZ), shape(NGX,...  9.95 us
    ppermute x1, starting transfers between devices, local(): lax.ppermute(slip_rate, ('gx', 'gy'), SLIP_MOVES)  6.28 us
    pallas_call x1, Pallas kernels, partial_rates(): pl.pallas_call(rates_kernel, out_shape=(shape(NGY, LANES), shape(NGX, LAN...  3.82 us
    ppermute x1, starting transfers between devices, local(): lax.ppermute(x_up, 'gx', X_UP)  3.54 us
    ppermute x1, waiting for transfers between devices, local(): lax.ppermute(x_down, 'gx', X_DOWN)  2.46 us
  transfers between devices with their start and end apart: 7, of which 2 were waited for; matrix products, arithmetic and copies ran while one was open for 1% of the time, Pallas kernels for 55%

profile of v4, /device:TPU:1, one launch (start us, length us, event | category | flops | bytes accessed | tf_op | source)
XLA Modules:
  0.0 116.1 jit_solution(12447227567433351032)
XLA Ops:
  0.6 6.3 %collective-permute-start.2 = (f32[48]{0:T(128)}, f32[48]{0:T(128)S(1)}, u32[]{:S(2)}, u32[]{:S(2)}) collective-permute-start(f32[48]{0:T(128)} %param.15), channel_id=1, source_target_pairs={{0,160},{1,96},{2,128},{3,64},{4,0},{5,192},{6,32},{7,224},{8,168}... | collective-permute-start | bytes 584 | tf_op jit(solution)/shard_map/ppermute | solution.py:482
  6.9 48.8 %pack.1 = (f32[16,8,512]{2,1,0:T(8,128)S(1)}, f32[16,8,512]{2,1,0:T(8,128)S(1)}, f32[6,72,512]{2,1,0:T(8,128)}, f32[6,72,512]{2,1,0:T(8,128)}) custom-call(f32[16,64,512]{2,1,0:T(8,128)} %p_far.1, f32[16,64,512]{2,1,0:T(8,128)} %k_far.1), custom_call_target="tpu_custom_call" | custom-call | tf_op jit(solution)/shard_map/pack/pallas_call | solution.py:112
  55.7 1.6 %collective-permute-start = (f32[16,8,512]{2,1,0:T(8,128)S(1)}, f32[16,8,512]{2,1,0:T(8,128)S(1)}, u32[]{:S(2)}, u32[]{:S(2)}) collective-permute-start(f32[16,8,512]{2,1,0:T(8,128)S(1)} %get-tuple-element.17), channel_id=1, source_target_pairs={{0,1},{1,2},{2,3},{3,4},{4,5},{5,6},{6,7},{8,9},{9,10},{10,11},{11... | collective-permute-start | bytes 786440 | tf_op jit(solution)/shard_map/ppermute | solution.py:480
  57.3 1.3 %collective-permute-start.1 = (f32[16,8,512]{2,1,0:T(8,128)S(1)}, f32[16,8,512]{2,1,0:T(8,128)S(1)}, u32[]{:S(2)}, u32[]{:S(2)}) collective-permute-start(f32[16,8,512]{2,1,0:T(8,128)S(1)} %get-tuple-element.18), channel_id=1, source_target_pairs={{1,0},{2,1},{3,2},{4,3},{5,4},{6,5},{7,6},{9,8},{10,9},{11,10},{12... | collective-permute-start | bytes 786440 | tf_op jit(solution)/shard_map/ppermute | solution.py:480
  58.6 1.1 prepare.1
  59.7 0.0 collective-permute-done.2
  59.7 0.6 broadcast_select_fusion.token
  60.3 10.9 %all-to-all-start = ((f32[32,1,128]{2,1,0:T(1,128)}), f32[32,1,128]{2,1,0:T(1,128)S(1)}, u32[]{:S(2)}, u32[]{:S(2)}) async-start(f32[32,1,128]{2,1,0:T(1,128)} %bitcast.10), calls=%async_computation | async-start | bytes 32768 | tf_op jit(solution)/shard_map/all_to_all | solution.py:450
  71.3 0.0 collective-permute-done.y_up
  71.3 0.0 collective-permute-done.1.y_down
  71.3 0.7 sides.1
  72.0 3.5 %collective-permute-start.3 = (f32[6,72,512]{2,1,0:T(8,128)}, f32[6,72,512]{2,1,0:T(8,128)}, u32[]{:S(2)}, u32[]{:S(2)}) collective-permute-start(f32[6,72,512]{2,1,0:T(8,128)} %get-tuple-element.22), channel_id=1, source_target_pairs={{0,8},{8,16},{16,24},{24,32},{32,40},{40,48},{48,56},{56,64},{64,7... | collective-permute-start | bytes 2654216 | tf_op jit(solution)/shard_map/ppermute | solution.py:486
  75.6 1.9 %collective-permute-start.4 = (f32[6,72,512]{2,1,0:T(8,128)}, f32[6,72,512]{2,1,0:T(8,128)}, u32[]{:S(2)}, u32[]{:S(2)}) collective-permute-start(f32[6,72,512]{2,1,0:T(8,128)} %get-tuple-element.23), channel_id=1, source_target_pairs={{8,0},{16,8},{24,16},{32,24},{40,32},{48,40},{56,48},{64,56},{72,6... | collective-permute-start | bytes 2654216 | tf_op jit(solution)/shard_map/ppermute | solution.py:486
  77.5 0.7 all-to-all-done
  78.2 3.8 %rates.1 = (f32[8,128]{1,0:T(8,128)}, s32[32,128]{1,0:T(8,128)S(1)}) custom-call(f32[32,128]{1,0:T(8,128)S(1)} %bitcast.24, f32[2,384,1536]{2,1,0:T(8,128)} %kernel_far.1), custom_call_target="tpu_custom_call" | custom-call | flops 999999995904 | bytes 6000000000 | tf_op jit(solution)/shard_map/rates/pallas_call | solution.py:250
  82.0 5.8 %all-to-all-start.1 = ((f32[8,1,128]{2,1,0:T(1,128)}), f32[8,1,128]{2,1,0:T(1,128)S(1)}, u32[]{:S(2)}, u32[]{:S(2)}) async-start(f32[8,1,128]{2,1,0:T(1,128)} %bitcast.13), calls=%async_computation.1 | async-start | bytes 8192 | tf_op jit(solution)/shard_map/all_to_all | solution.py:450
  87.8 0.0 collective-permute-done.3.x_up
  87.8 2.5 %collective-permute-done.4.x_down = f32[6,72,512]{2,1,0:T(8,128)} collective-permute-done((f32[6,72,512]{2,1,0:T(8,128)}, f32[6,72,512]{2,1,0:T(8,128)}, u32[]{:S(2)}, u32[]{:S(2)}) %collective-permute-start.4) | collective-permute-done | bytes 884768 | tf_op jit(solution)/shard_map/ppermute | solution.py:486
  90.2 10.0 %diffusion.1 = (f32[16,64,512]{2,1,0:T(8,128)}, f32[32,128]{1,0:T(8,128)S(1)}) custom-call(f32[16,64,512]{2,1,0:T(8,128)} %p_far.1, f32[16,64,512]{2,1,0:T(8,128)} %k_far.1, f32[16,8,512]{2,1,0:T(8,128)S(1)} %collective-permute-done.y_up, f32[16,8,512]{2,1,0:T(8,128)S(1)} %collective-permute-done.1.y_down, f32[6,72,512]{2,1,0:T(8,128)} %collective-permute-done.3.x_up, ...), custom_call_target="tpu_custom_call" | custom-call | flops 60000000 | bytes 12000000 | tf_op jit(solution)/shard_map/diffusion/pallas_call | solution.py:408
  100.2 0.0 all-to-all-done.1
  100.2 15.2 %all_to_all.33 = f32[32,1,128]{2,1,0:T(1,128)S(1)} all-to-all(f32[32,1,128]{2,1,0:T(1,128)S(1)} %bitcast.25), channel_id=1, replica_groups=mesh['gx'=32,'gy'=8] {'gx'}, dimensions={0} | all-to-all | bytes 32768 | tf_op jit(solution)/shard_map/all_to_all | solution.py:450
  115.4 0.6 friction.1
  (2 shorter events, 0.0 us)
Async XLA Ops:
  0.6 59.1 %collective-permute-start.2 = (f32[48]{0:T(128)}, f32[48]{0:T(128)S(1)}, u32[]{:S(2)}, u32[]{:S(2)}) collective-permute-start(f32[48]{0:T(128)} %param.15), channel_id=1, source_target_pairs={{0,160},{1,96},{2,128},{3,64},{4,0},{5,192},{6,32},{7,224},{8,168}... | collective-permute-start | bytes 584 | tf_op jit(solution)/shard_map/ppermute | solution.py:482
  55.7 15.5 %collective-permute-start = (f32[16,8,512]{2,1,0:T(8,128)S(1)}, f32[16,8,512]{2,1,0:T(8,128)S(1)}, u32[]{:S(2)}, u32[]{:S(2)}) collective-permute-start(f32[16,8,512]{2,1,0:T(8,128)S(1)} %get-tuple-element.17), channel_id=1, source_target_pairs={{0,1},{1,2},{2,3},{3,4},{4,5},{5,6},{6,7},{8,9},{9,10},{10,11},{11... | collective-permute-start | bytes 786440 | tf_op jit(solution)/shard_map/ppermute | solution.py:480
  57.3 14.0 %collective-permute-start.1 = (f32[16,8,512]{2,1,0:T(8,128)S(1)}, f32[16,8,512]{2,1,0:T(8,128)S(1)}, u32[]{:S(2)}, u32[]{:S(2)}) collective-permute-start(f32[16,8,512]{2,1,0:T(8,128)S(1)} %get-tuple-element.18), channel_id=1, source_target_pairs={{1,0},{2,1},{3,2},{4,3},{5,4},{6,5},{7,6},{9,8},{10,9},{11,10},{12... | collective-permute-start | bytes 786440 | tf_op jit(solution)/shard_map/ppermute | solution.py:480
  60.3 17.9 %all-to-all-start = ((f32[32,1,128]{2,1,0:T(1,128)}), f32[32,1,128]{2,1,0:T(1,128)S(1)}, u32[]{:S(2)}, u32[]{:S(2)}) async-start(f32[32,1,128]{2,1,0:T(1,128)} %bitcast.10), calls=%async_computation | async-start | bytes 32768 | tf_op jit(solution)/shard_map/all_to_all | solution.py:450
  72.0 15.8 %collective-permute-start.3 = (f32[6,72,512]{2,1,0:T(8,128)}, f32[6,72,512]{2,1,0:T(8,128)}, u32[]{:S(2)}, u32[]{:S(2)}) collective-permute-start(f32[6,72,512]{2,1,0:T(8,128)} %get-tuple-element.22), channel_id=1, source_target_pairs={{0,8},{8,16},{16,24},{24,32},{32,40},{40,48},{48,56},{56,64},{64,7... | collective-permute-start | bytes 2654216 | tf_op jit(solution)/shard_map/ppermute | solution.py:486
  75.6 14.7 %collective-permute-start.4 = (f32[6,72,512]{2,1,0:T(8,128)}, f32[6,72,512]{2,1,0:T(8,128)}, u32[]{:S(2)}, u32[]{:S(2)}) collective-permute-start(f32[6,72,512]{2,1,0:T(8,128)} %get-tuple-element.23), channel_id=1, source_target_pairs={{8,0},{16,8},{24,16},{32,24},{40,32},{48,40},{56,48},{64,56},{72,6... | collective-permute-start | bytes 2654216 | tf_op jit(solution)/shard_map/ppermute | solution.py:486
  82.0 18.2 %all-to-all-start.1 = ((f32[8,1,128]{2,1,0:T(1,128)}), f32[8,1,128]{2,1,0:T(1,128)S(1)}, u32[]{:S(2)}, u32[]{:S(2)}) async-start(f32[8,1,128]{2,1,0:T(1,128)} %bitcast.13), calls=%async_computation.1 | async-start | bytes 8192 | tf_op jit(solution)/shard_map/all_to_all | solution.py:450

commit v5 on v4

--- a/solution.py
+++ b/solution.py
@@ -78,24 +78,24 @@
     return jnp.sum(jnp.where(row == column, row_value, 0.0), axis=1, keepdims=True)
 
 
-def pack_kernel(p, k, y_up, y_down, x_up, x_down, tiles, sems):
+def pack_kernel(p, k, y_up, y_down, x_up, x_down, tiles, rows, sems):
     tops = started(
         pltpu.make_async_copy(p.at[:, pl.ds(CY - 8, 8), :], tiles.at[0], sems.at[0]),
         pltpu.make_async_copy(k.at[:, pl.ds(CY - 8, 8), :], tiles.at[1], sems.at[1]),
         pltpu.make_async_copy(p.at[:, pl.ds(0, 8), :], tiles.at[2], sems.at[2]),
         pltpu.make_async_copy(k.at[:, pl.ds(0, 8), :], tiles.at[3], sems.at[3]),
     )
-    copies = []
-    for side, (target, start) in enumerate(((x_up, CX - HALO), (x_down, 0))):
-        for n, source in enumerate((p, k)):
-            copies.append(
+    loads = [
+        started(
+            *[
                 pltpu.make_async_copy(
-                    source.at[pl.ds(start, HALO)],
-                    target.at[pl.ds(HALO * n, HALO), pl.ds(0, CY)],
-                    sems.at[4 + 2 * side + n],
+                    source.at[pl.ds(start, HALO)], rows.at[side, pl.ds(HALO * n, HALO)], sems.at[4 + 2 * side + n]
                 )
-            )
-    started(*copies)
+                for n, source in enumerate((p, k))
+            ]
+        )
+        for side, start in enumerate((CX - HALO, 0))
+    ]
     row = lax.broadcasted_iota(jnp.int32, (8, NZ), 0)
     waited(tops)
 
@@ -105,7 +105,11 @@
         return carry
 
     lax.fori_loop(0, CX, plane, 0)
-    waited(copies)
+    stores = []
+    for side, target in enumerate((x_up, x_down)):
+        waited(loads[side])
+        stores += started(pltpu.make_async_copy(rows.at[side], target.at[:, pl.ds(0, CY)], sems.at[8 + side]))
+    waited(stores)
 
 
 def pack(p, k):
@@ -114,8 +118,8 @@
         out_shape=(shape(CX, 8, NZ),) * 2 + (HBM((2 * HALO, CY + 8, NZ), F32),) * 2,
         in_specs=[spec(HBM)] * 2,
         out_specs=(spec(),) * 2 + (spec(HBM),) * 2,
-        scratch_shapes=[VMEM((4, CX, 8, NZ), F32), DMA((8,))],
-        compiler_params=pltpu.CompilerParams(vmem_limit_bytes=4 << 20),
+        scratch_shapes=[VMEM((4, CX, 8, NZ), F32), VMEM((2, 2 * HALO, CY, NZ), F32), DMA((10,))],
+        compiler_params=pltpu.CompilerParams(vmem_limit_bytes=6 << 20),
         name="pack",
     )(far(p), far(k))
 

time: 116 us -> 70.3 us (0.61)
  Pallas kernels: 65 us -> 18.8 us
    pallas_call x1, Pallas kernels: 48.8 us -> 2.66 us  [pack(): pl.pallas_call(pack_kernel, out_shape=(shape(CX, 8, NZ),) * 2 + (HBM((2 *...]
  transfers between devices with their start and end apart: 7 -> 7, of which waited for: 2 -> 2; matrix products, arithmetic and copies ran while one was open for 1% -> 1% of each run, Pallas kernels for 55% -> 26%
where the time goes in v5:
time: 70.3 us; the launch traced here: 69.9 us
  starting transfers between devices  31.3 us (45%)
  Pallas kernels  18.8 us (27%)
  blocking collectives  15.2 us (22%)
  waiting for transfers between devices  3.17 us (5%)
  between operations  0.76 us (1%)
    all_to_all x2, starting transfers between devices, exchanged(): return lax.all_to_all(value, axis, split_axis=0, concat_axis=0, tiled=True)  16.7 us
    all_to_all x1, blocking collectives, exchanged(): return lax.all_to_all(value, axis, split_axis=0, concat_axis=0, tiled=True)  15.2 us
    pallas_call x1, Pallas kernels, diffusion(): pl.pallas_call(diffusion_kernel, out_shape=(shape(CX, CY, NZ), shape(NGX,...  9.95 us
    ppermute x1, starting transfers between devices, local(): lax.ppermute(slip_rate, ('gx', 'gy'), SLIP_MOVES)  6.28 us
    pallas_call x1, Pallas kernels, partial_rates(): pl.pallas_call(rates_kernel, out_shape=(shape(NGY, LANES), shape(NGX, LAN...  3.82 us
    ppermute x1, starting transfers between devices, local(): lax.ppermute(x_up, 'gx', X_UP)  3.54 us
    pallas_call x1, Pallas kernels, pack(): pl.pallas_call(pack_kernel, out_shape=(shape(CX, 8, NZ),) * 2 + (HBM((2 *...  2.66 us
    ppermute x1, waiting for transfers between devices, local(): lax.ppermute(x_down, 'gx', X_DOWN)  2.46 us
  transfers between devices with their start and end apart: 7, of which 2 were waited for; matrix products, arithmetic and copies ran while one was open for 1% of the time, Pallas kernels for 26%

profile of v5, /device:TPU:1, one launch (start us, length us, event | category | flops | bytes accessed | tf_op | source)
XLA Modules:
  0.0 69.9 jit_solution(15800309894402889875)
XLA Ops:
  0.6 6.3 %collective-permute-start.2 = (f32[48]{0:T(128)}, f32[48]{0:T(128)S(1)}, u32[]{:S(2)}, u32[]{:S(2)}) collective-permute-start(f32[48]{0:T(128)} %param.15), channel_id=1, source_target_pairs={{0,160},{1,96},{2,128},{3,64},{4,0},{5,192},{6,32},{7,224},{8,168}... | collective-permute-start | bytes 584 | tf_op jit(solution)/shard_map/ppermute | solution.py:486
  6.9 2.7 %pack.1 = (f32[16,8,512]{2,1,0:T(8,128)S(1)}, f32[16,8,512]{2,1,0:T(8,128)S(1)}, f32[6,72,512]{2,1,0:T(8,128)}, f32[6,72,512]{2,1,0:T(8,128)}) custom-call(f32[16,64,512]{2,1,0:T(8,128)} %p_far.1, f32[16,64,512]{2,1,0:T(8,128)} %k_far.1), custom_call_target="tpu_custom_call" | custom-call | tf_op jit(solution)/shard_map/pack/pallas_call | solution.py:116
  9.6 1.6 %collective-permute-start = (f32[16,8,512]{2,1,0:T(8,128)S(1)}, f32[16,8,512]{2,1,0:T(8,128)S(1)}, u32[]{:S(2)}, u32[]{:S(2)}) collective-permute-start(f32[16,8,512]{2,1,0:T(8,128)S(1)} %get-tuple-element.17), channel_id=1, source_target_pairs={{0,1},{1,2},{2,3},{3,4},{4,5},{5,6},{6,7},{8,9},{9,10},{10,11},{11... | collective-permute-start | bytes 786440 | tf_op jit(solution)/shard_map/ppermute | solution.py:484
  11.2 1.3 %collective-permute-start.1 = (f32[16,8,512]{2,1,0:T(8,128)S(1)}, f32[16,8,512]{2,1,0:T(8,128)S(1)}, u32[]{:S(2)}, u32[]{:S(2)}) collective-permute-start(f32[16,8,512]{2,1,0:T(8,128)S(1)} %get-tuple-element.18), channel_id=1, source_target_pairs={{1,0},{2,1},{3,2},{4,3},{5,4},{6,5},{7,6},{9,8},{10,9},{11,10},{12... | collective-permute-start | bytes 786440 | tf_op jit(solution)/shard_map/ppermute | solution.py:484
  12.5 1.1 %prepare.1 = (f32[32,128]{1,0:T(8,128)S(1)}, f32[8,128]{1,0:T(8,128)S(1)}) custom-call(s32[1,48]{1,0:T(1,128)} %bitcast.27, s32[1,48]{1,0:T(1,128)} %bitcast.28, f32[1,48]{1,0:T(1,128)} %bitcast.35, f32[1,48]{1,0:T(1,128)} %bitcast.29, f32[1,48]{1,0:T(1,128)} %bitcast.30, f32[1,48]{1,0:T(1,128)} %bitcast.31, f32[1,48]{1,0:T(1,128)} %bitcast.32, ...), custom_call_target="tpu_custom_call" | custom-call | tf_op jit(solution)/shard_map/prepare/pallas_call | solution.py:159
  13.5 0.0 collective-permute-done.2
  13.6 0.6 broadcast_select_fusion.token
  14.2 10.9 %all-to-all-start = ((f32[32,1,128]{2,1,0:T(1,128)}), f32[32,1,128]{2,1,0:T(1,128)S(1)}, u32[]{:S(2)}, u32[]{:S(2)}) async-start(f32[32,1,128]{2,1,0:T(1,128)} %bitcast.10), calls=%async_computation | async-start | bytes 32768 | tf_op jit(solution)/shard_map/all_to_all | solution.py:454
  25.1 0.0 collective-permute-done.y_up
  25.1 0.0 collective-permute-done.1.y_down
  25.1 0.7 %sides.1 = (f32[6,72,512]{2,1,0:T(8,128)}, f32[6,72,512]{2,1,0:T(8,128)}) custom-call(f32[6,72,512]{2,1,0:T(8,128)} %get-tuple-element.19.x_up, f32[6,72,512]{2,1,0:T(8,128)} %get-tuple-element.20.x_down, f32[16,8,512]{2,1,0:T(8,128)S(1)} %collective-permute-done.y_up, ...), custom_call_target="tpu_custom_call", output_to_operand_aliasing={{0}: (0, {}), {1}: (1, {})} | custom-call | tf_op jit(solution)/shard_map/sides/pallas_call | solution.py:188
  25.9 3.5 %collective-permute-start.3 = (f32[6,72,512]{2,1,0:T(8,128)}, f32[6,72,512]{2,1,0:T(8,128)}, u32[]{:S(2)}, u32[]{:S(2)}) collective-permute-start(f32[6,72,512]{2,1,0:T(8,128)} %get-tuple-element.22), channel_id=1, source_target_pairs={{0,8},{8,16},{16,24},{24,32},{32,40},{40,48},{48,56},{56,64},{64,7... | collective-permute-start | bytes 2654216 | tf_op jit(solution)/shard_map/ppermute | solution.py:490
  29.4 1.9 %collective-permute-start.4 = (f32[6,72,512]{2,1,0:T(8,128)}, f32[6,72,512]{2,1,0:T(8,128)}, u32[]{:S(2)}, u32[]{:S(2)}) collective-permute-start(f32[6,72,512]{2,1,0:T(8,128)} %get-tuple-element.23), channel_id=1, source_target_pairs={{8,0},{16,8},{24,16},{32,24},{40,32},{48,40},{56,48},{64,56},{72,6... | collective-permute-start | bytes 2654216 | tf_op jit(solution)/shard_map/ppermute | solution.py:490
  31.3 0.7 all-to-all-done
  32.0 3.8 %rates.1 = (f32[8,128]{1,0:T(8,128)}, s32[32,128]{1,0:T(8,128)S(1)}) custom-call(f32[32,128]{1,0:T(8,128)S(1)} %bitcast.24, f32[2,384,1536]{2,1,0:T(8,128)} %kernel_far.1), custom_call_target="tpu_custom_call" | custom-call | flops 999999995904 | bytes 6000000000 | tf_op jit(solution)/shard_map/rates/pallas_call | solution.py:254
  35.9 5.8 %all-to-all-start.1 = ((f32[8,1,128]{2,1,0:T(1,128)}), f32[8,1,128]{2,1,0:T(1,128)S(1)}, u32[]{:S(2)}, u32[]{:S(2)}) async-start(f32[8,1,128]{2,1,0:T(1,128)} %bitcast.13), calls=%async_computation.1 | async-start | bytes 8192 | tf_op jit(solution)/shard_map/all_to_all | solution.py:454
  41.6 0.0 collective-permute-done.3.x_up
  41.6 2.5 %collective-permute-done.4.x_down = f32[6,72,512]{2,1,0:T(8,128)} collective-permute-done((f32[6,72,512]{2,1,0:T(8,128)}, f32[6,72,512]{2,1,0:T(8,128)}, u32[]{:S(2)}, u32[]{:S(2)}) %collective-permute-start.4) | collective-permute-done | bytes 884768 | tf_op jit(solution)/shard_map/ppermute | solution.py:490
  44.1 10.0 %diffusion.1 = (f32[16,64,512]{2,1,0:T(8,128)}, f32[32,128]{1,0:T(8,128)S(1)}) custom-call(f32[16,64,512]{2,1,0:T(8,128)} %p_far.1, f32[16,64,512]{2,1,0:T(8,128)} %k_far.1, f32[16,8,512]{2,1,0:T(8,128)S(1)} %collective-permute-done.y_up, f32[16,8,512]{2,1,0:T(8,128)S(1)} %collective-permute-done.1.y_down, f32[6,72,512]{2,1,0:T(8,128)} %collective-permute-done.3.x_up, ...), custom_call_target="tpu_custom_call" | custom-call | flops 60000000 | bytes 12000000 | tf_op jit(solution)/shard_map/diffusion/pallas_call | solution.py:412
  54.0 0.0 all-to-all-done.1
  54.1 15.2 %all_to_all.33 = f32[32,1,128]{2,1,0:T(1,128)S(1)} all-to-all(f32[32,1,128]{2,1,0:T(1,128)S(1)} %bitcast.25), channel_id=1, replica_groups=mesh['gx'=32,'gy'=8] {'gx'}, dimensions={0} | all-to-all | bytes 32768 | tf_op jit(solution)/shard_map/all_to_all | solution.py:454
  69.3 0.6 friction.1
  (2 shorter events, 0.0 us)
Async XLA Ops:
  0.6 12.9 %collective-permute-start.2 = (f32[48]{0:T(128)}, f32[48]{0:T(128)S(1)}, u32[]{:S(2)}, u32[]{:S(2)}) collective-permute-start(f32[48]{0:T(128)} %param.15), channel_id=1, source_target_pairs={{0,160},{1,96},{2,128},{3,64},{4,0},{5,192},{6,32},{7,224},{8,168}... | collective-permute-start | bytes 584 | tf_op jit(solution)/shard_map/ppermute | solution.py:486
  9.6 15.5 %collective-permute-start = (f32[16,8,512]{2,1,0:T(8,128)S(1)}, f32[16,8,512]{2,1,0:T(8,128)S(1)}, u32[]{:S(2)}, u32[]{:S(2)}) collective-permute-start(f32[16,8,512]{2,1,0:T(8,128)S(1)} %get-tuple-element.17), channel_id=1, source_target_pairs={{0,1},{1,2},{2,3},{3,4},{4,5},{5,6},{6,7},{8,9},{9,10},{10,11},{11... | collective-permute-start | bytes 786440 | tf_op jit(solution)/shard_map/ppermute | solution.py:484
  11.2 14.0 %collective-permute-start.1 = (f32[16,8,512]{2,1,0:T(8,128)S(1)}, f32[16,8,512]{2,1,0:T(8,128)S(1)}, u32[]{:S(2)}, u32[]{:S(2)}) collective-permute-start(f32[16,8,512]{2,1,0:T(8,128)S(1)} %get-tuple-element.18), channel_id=1, source_target_pairs={{1,0},{2,1},{3,2},{4,3},{5,4},{6,5},{7,6},{9,8},{10,9},{11,10},{12... | collective-permute-start | bytes 786440 | tf_op jit(solution)/shard_map/ppermute | solution.py:484
  14.2 17.9 %all-to-all-start = ((f32[32,1,128]{2,1,0:T(1,128)}), f32[32,1,128]{2,1,0:T(1,128)S(1)}, u32[]{:S(2)}, u32[]{:S(2)}) async-start(f32[32,1,128]{2,1,0:T(1,128)} %bitcast.10), calls=%async_computation | async-start | bytes 32768 | tf_op jit(solution)/shard_map/all_to_all | solution.py:454
  25.9 15.8 %collective-permute-start.3 = (f32[6,72,512]{2,1,0:T(8,128)}, f32[6,72,512]{2,1,0:T(8,128)}, u32[]{:S(2)}, u32[]{:S(2)}) collective-permute-start(f32[6,72,512]{2,1,0:T(8,128)} %get-tuple-element.22), channel_id=1, source_target_pairs={{0,8},{8,16},{16,24},{24,32},{32,40},{40,48},{48,56},{56,64},{64,7... | collective-permute-start | bytes 2654216 | tf_op jit(solution)/shard_map/ppermute | solution.py:490
  29.4 14.7 %collective-permute-start.4 = (f32[6,72,512]{2,1,0:T(8,128)}, f32[6,72,512]{2,1,0:T(8,128)}, u32[]{:S(2)}, u32[]{:S(2)}) collective-permute-start(f32[6,72,512]{2,1,0:T(8,128)} %get-tuple-element.23), channel_id=1, source_target_pairs={{8,0},{16,8},{24,16},{32,24},{40,32},{48,40},{56,48},{64,56},{72,6... | collective-permute-start | bytes 2654216 | tf_op jit(solution)/shard_map/ppermute | solution.py:490
  35.9 18.2 %all-to-all-start.1 = ((f32[8,1,128]{2,1,0:T(1,128)}), f32[8,1,128]{2,1,0:T(1,128)S(1)}, u32[]{:S(2)}, u32[]{:S(2)}) async-start(f32[8,1,128]{2,1,0:T(1,128)} %bitcast.13), calls=%async_computation.1 | async-start | bytes 8192 | tf_op jit(solution)/shard_map/all_to_all | solution.py:454

commit v6 on v5

--- a/solution.py
+++ b/solution.py
@@ -124,8 +124,8 @@
     )(far(p), far(k))
 
 
-def prepare_kernel(owner, cell, *refs):
-    floats, (wanted, terms, whole, held, sems) = refs[:7], refs[7:]
+def prepare_kernel(moved, owner, cell, *refs):
+    floats, (leaving, terms, whole, held, sems) = refs[:7], refs[7:]
     waited(
         started(
             pltpu.make_async_copy(owner, whole.at[0], sems.at[0]),
@@ -146,7 +146,8 @@
     for c in range(3):
         asked = jnp.where(jnp.logical_and(named, rank == float(c)), cells, 0.0)
         value = jnp.where(lane == TRI + c, jnp.sum(asked, axis=1, keepdims=True), value)
-    wanted[...] = value
+    leaving[...] = value
+    leaving[:, 0:TRI] = jnp.broadcast_to(moved[...], (NGX, TRI))
     ratio = distance / slip
     state = ratio + (aging - ratio) * jnp.exp(-heal_time / ratio)
     terms[...] = jnp.zeros((8, LANES), F32)
@@ -155,16 +156,17 @@
         terms[n : n + 1, 0:TRI] = term
 
 
-def prepare(*values):
+def prepare(moved, *values):
     return pl.pallas_call(
         prepare_kernel,
         out_shape=(shape(NGX, LANES), shape(8, LANES)),
-        in_specs=[spec(HBM)] * len(values),
+        in_specs=[spec()] + [spec(HBM)] * len(values),
         out_specs=(spec(),) * 2,
         scratch_shapes=[VMEM((2, 1, TRI), jnp.int32), VMEM((7, 1, TRI), F32), DMA((9,))],
         compiler_params=pltpu.CompilerParams(vmem_limit_bytes=2 << 20),
+        cost_estimate=pl.CostEstimate(flops=10**12, bytes_accessed=0, transcendentals=0),
         name="prepare",
-    )(*all_far(*values))
+    )(moved, *all_far(*values))
 
 
 def halo_rows(low, high, row):
@@ -480,11 +482,9 @@
         slip_distance,
     )
     y_up, y_down, x_up, x_down = pack(pressure, permeability)
-    wanted, terms = prepare(*[v.reshape(1, TRI) for v in rows])
+    moved = lax.ppermute(slip_rate, ("gx", "gy"), SLIP_MOVES).reshape(1, TRI)
+    leaving, terms = prepare(moved, *[v.reshape(1, TRI) for v in rows])
     y_up, y_down = lax.ppermute(y_up, "gy", Y_UP), lax.ppermute(y_down, "gy", Y_DOWN)
-    lane = lax.broadcasted_iota(jnp.int32, (NGX, LANES), 1)
-    row = jnp.pad(lax.ppermute(slip_rate, ("gx", "gy"), SLIP_MOVES), (0, LANES - TRI)).reshape(1, LANES)
-    leaving = jnp.where(lane < TRI, row, wanted)
     arrived = exchanged(leaving, "gx")
     x_up, x_down = sides(x_up, x_down, y_up, y_down, leaving)
     x_up, x_down = lax.ppermute(x_up, "gx", X_UP), lax.ppermute(x_down, "gx", X_DOWN)

time: 70.3 us -> 73.9 us (1.051)
  Pallas kernels: 18.8 us -> 22.3 us
    ppermute x1, waiting for transfers between devices: 2.46 us -> 3.84 us  [local(): lax.ppermute(x_down, 'gx', X_DOWN)]
    pallas_call x1, Pallas kernels: 9.95 us -> 11 us  [diffusion(): pl.pallas_call(diffusion_kernel, out_shape=(shape(CX, CY, NZ), shape(NGX,...]
    pallas_call x1, Pallas kernels: 0.73 us -> 1.75 us  [sides(): pl.pallas_call(sides_kernel, out_shape=(HBM((2 * HALO, CY + 8, NZ), F32),...]
    pallas_call x1, Pallas kernels: 2.66 us -> 3.46 us  [pack(): pl.pallas_call(pack_kernel, out_shape=(shape(CX, 8, NZ),) * 2 + (HBM((2 *...]
  transfers between devices with their start and end apart: 7 -> 7, of which waited for: 2 -> 1; matrix products, arithmetic and copies ran while one was open for 1% -> 0% of each run, Pallas kernels for 26% -> 30%
where the time goes in v6:
time: 73.9 us; the launch traced here: 73.4 us
  starting transfers between devices  31.3 us (42%)
  Pallas kernels  22.3 us (30%)
  blocking collectives  15.2 us (21%)
  waiting for transfers between devices  3.85 us (5%)
  between operations  0.75 us (1%)
    all_to_all x2, starting transfers between devices, exchanged(): return lax.all_to_all(value, axis, split_axis=0, concat_axis=0, tiled=True)  16 us
    all_to_all x1, blocking collectives, exchanged(): return lax.all_to_all(value, axis, split_axis=0, concat_axis=0, tiled=True)  15.2 us
    pallas_call x1, Pallas kernels, diffusion(): pl.pallas_call(diffusion_kernel, out_shape=(shape(CX, CY, NZ), shape(NGX,...  11 us
    ppermute x1, starting transfers between devices, local(): moved = lax.ppermute(slip_rate, ('gx', 'gy'), SLIP_MOVES).reshape(1, TRI)  6.28 us
    ppermute x1, waiting for transfers between devices, local(): lax.ppermute(x_down, 'gx', X_DOWN)  3.84 us
    pallas_call x1, Pallas kernels, partial_rates(): pl.pallas_call(rates_kernel, out_shape=(shape(NGY, LANES), shape(NGX, LAN...  3.83 us
    ppermute x1, starting transfers between devices, local(): lax.ppermute(x_up, 'gx', X_UP)  3.54 us
    pallas_call x1, Pallas kernels, pack(): pl.pallas_call(pack_kernel, out_shape=(shape(CX, 8, NZ),) * 2 + (HBM((2 *...  3.46 us
  transfers between devices with their start and end apart: 7, of which 1 were waited for; matrix products, arithmetic and copies ran while one was open for 0% of the time, Pallas kernels for 30%

profile of v6, /device:TPU:1, one launch (start us, length us, event | category | flops | bytes accessed | tf_op | source)
XLA Modules:
  0.0 73.4 jit_solution(5007608928905894697)
XLA Ops:
  0.6 6.3 %collective-permute-start.2 = (f32[48]{0:T(128)}, f32[48]{0:T(128)S(1)}, u32[]{:S(2)}, u32[]{:S(2)}) collective-permute-start(f32[48]{0:T(128)} %param.15), channel_id=1, source_target_pairs={{0,160},{1,96},{2,128},{3,64},{4,0},{5,192},{6,32},{7,224},{8,168}... | collective-permute-start | bytes 584 | tf_op jit(solution)/shard_map/ppermute | solution.py:485
  6.9 3.5 %pack.1 = (f32[16,8,512]{2,1,0:T(8,128)}, f32[16,8,512]{2,1,0:T(8,128)}, f32[6,72,512]{2,1,0:T(8,128)}, f32[6,72,512]{2,1,0:T(8,128)}) custom-call(f32[16,64,512]{2,1,0:T(8,128)} %p_far.1, f32[16,64,512]{2,1,0:T(8,128)} %k_far.1), custom_call_target="tpu_custom_call" | custom-call | tf_op jit(solution)/shard_map/pack/pallas_call | solution.py:116
  10.4 2.3 %collective-permute-start = (f32[16,8,512]{2,1,0:T(8,128)}, f32[16,8,512]{2,1,0:T(8,128)}, u32[]{:S(2)}, u32[]{:S(2)}) collective-permute-start(f32[16,8,512]{2,1,0:T(8,128)} %get-tuple-element.17), channel_id=1, source_target_pairs={{0,1},{1,2},{2,3},{3,4},{4,5},{5,6},{6,7},{8,9},{9,10},{10,11},{11... | collective-permute-start | bytes 786440 | tf_op jit(solution)/shard_map/ppermute | solution.py:487
  12.7 1.3 %collective-permute-start.1 = (f32[16,8,512]{2,1,0:T(8,128)}, f32[16,8,512]{2,1,0:T(8,128)}, u32[]{:S(2)}, u32[]{:S(2)}) collective-permute-start(f32[16,8,512]{2,1,0:T(8,128)} %get-tuple-element.18), channel_id=1, source_target_pairs={{1,0},{2,1},{3,2},{4,3},{5,4},{6,5},{7,6},{9,8},{10,9},{11,10},{12... | collective-permute-start | bytes 786440 | tf_op jit(solution)/shard_map/ppermute | solution.py:487
  14.0 0.0 collective-permute-done.2
  14.0 1.6 %prepare.1 = (f32[32,128]{1,0:T(8,128)}, f32[8,128]{1,0:T(8,128)S(1)}) custom-call(f32[1,48]{1,0:T(1,128)S(1)} %bitcast.28, s32[1,48]{1,0:T(1,128)} %bitcast.30, s32[1,48]{1,0:T(1,128)} %bitcast.31, f32[1,48]{1,0:T(1,128)} %bitcast.29, f32[1,48]{1,0:T(1,128)} %bitcast.32, f32[1,48]{1,0:T(1,128)} %bitcast.33, f32[1,48]{1,0:T(1,128)} %bitcast.34, ...), custom_call_target="tpu_custom_call" | custom-call | flops 999999995904 | tf_op jit(solution)/shard_map/prepare/pallas_call | solution.py:160
  15.6 11.0 %all-to-all-start = ((f32[32,1,128]{2,1,0:T(1,128)}), f32[32,1,128]{2,1,0:T(1,128)S(1)}, u32[]{:S(2)}, u32[]{:S(2)}) async-start(f32[32,1,128]{2,1,0:T(1,128)} %bitcast.11), calls=%async_computation | async-start | bytes 32768 | tf_op jit(solution)/shard_map/all_to_all | solution.py:456
  26.6 0.0 collective-permute-done.y_up
  26.6 0.0 collective-permute-done.1.y_down
  26.6 1.7 %sides.1 = (f32[6,72,512]{2,1,0:T(8,128)}, f32[6,72,512]{2,1,0:T(8,128)}) custom-call(f32[6,72,512]{2,1,0:T(8,128)} %get-tuple-element.19.x_up, f32[6,72,512]{2,1,0:T(8,128)} %get-tuple-element.20.x_down, f32[16,8,512]{2,1,0:T(8,128)} %collective-permute-done.y_up, ...), custom_call_target="tpu_custom_call", output_to_operand_aliasing={{0}: (0, {}), {1}: (1, {})} | custom-call | tf_op jit(solution)/shard_map/sides/pallas_call | solution.py:190
  28.4 3.5 %collective-permute-start.3 = (f32[6,72,512]{2,1,0:T(8,128)}, f32[6,72,512]{2,1,0:T(8,128)}, u32[]{:S(2)}, u32[]{:S(2)}) collective-permute-start(f32[6,72,512]{2,1,0:T(8,128)} %get-tuple-element.22), channel_id=1, source_target_pairs={{0,8},{8,16},{16,24},{24,32},{32,40},{40,48},{48,56},{56,64},{64,7... | collective-permute-start | bytes 2654216 | tf_op jit(solution)/shard_map/ppermute | solution.py:490
  31.9 1.9 %collective-permute-start.4 = (f32[6,72,512]{2,1,0:T(8,128)}, f32[6,72,512]{2,1,0:T(8,128)}, u32[]{:S(2)}, u32[]{:S(2)}) collective-permute-start(f32[6,72,512]{2,1,0:T(8,128)} %get-tuple-element.23), channel_id=1, source_target_pairs={{8,0},{16,8},{24,16},{32,24},{40,32},{48,40},{56,48},{64,56},{72,6... | collective-permute-start | bytes 2654216 | tf_op jit(solution)/shard_map/ppermute | solution.py:490
  33.8 0.0 all-to-all-done
  33.9 3.8 %rates.1 = (f32[8,128]{1,0:T(8,128)}, s32[32,128]{1,0:T(8,128)S(1)}) custom-call(f32[32,128]{1,0:T(8,128)S(1)} %bitcast.25, f32[2,384,1536]{2,1,0:T(8,128)} %kernel_far.1), custom_call_target="tpu_custom_call" | custom-call | flops 999999995904 | bytes 6000000000 | tf_op jit(solution)/shard_map/rates/pallas_call | solution.py:256
  37.7 5.1 %all-to-all-start.1 = ((f32[8,1,128]{2,1,0:T(1,128)}), f32[8,1,128]{2,1,0:T(1,128)S(1)}, u32[]{:S(2)}, u32[]{:S(2)}) async-start(f32[8,1,128]{2,1,0:T(1,128)} %bitcast.14), calls=%async_computation.1 | async-start | bytes 8192 | tf_op jit(solution)/shard_map/all_to_all | solution.py:456
  42.8 0.0 collective-permute-done.3.x_up
  42.8 3.8 %collective-permute-done.4.x_down = f32[6,72,512]{2,1,0:T(8,128)} collective-permute-done((f32[6,72,512]{2,1,0:T(8,128)}, f32[6,72,512]{2,1,0:T(8,128)}, u32[]{:S(2)}, u32[]{:S(2)}) %collective-permute-start.4) | collective-permute-done | bytes 884768 | tf_op jit(solution)/shard_map/ppermute | solution.py:490
  46.6 11.0 %diffusion.1 = (f32[16,64,512]{2,1,0:T(8,128)}, f32[32,128]{1,0:T(8,128)S(1)}) custom-call(f32[16,64,512]{2,1,0:T(8,128)} %p_far.1, f32[16,64,512]{2,1,0:T(8,128)} %k_far.1, f32[16,8,512]{2,1,0:T(8,128)} %collective-permute-done.y_up, f32[16,8,512]{2,1,0:T(8,128)} %collective-permute-done.1.y_down, f32[6,72,512]{2,1,0:T(8,128)} %collective-permute-done.3.x_up, ...), custom_call_target="tpu_custom_call" | custom-call | flops 60000000 | bytes 12000000 | tf_op jit(solution)/shard_map/diffusion/pallas_call | solution.py:414
  57.6 0.0 all-to-all-done.1
  57.6 15.2 %all_to_all.33 = f32[32,1,128]{2,1,0:T(1,128)S(1)} all-to-all(f32[32,1,128]{2,1,0:T(1,128)S(1)} %bitcast.26), channel_id=1, replica_groups=mesh['gx'=32,'gy'=8] {'gx'}, dimensions={0} | all-to-all | bytes 32768 | tf_op jit(solution)/shard_map/all_to_all | solution.py:456
  72.8 0.6 friction.1
Async XLA Ops:
  0.6 13.3 %collective-permute-start.2 = (f32[48]{0:T(128)}, f32[48]{0:T(128)S(1)}, u32[]{:S(2)}, u32[]{:S(2)}) collective-permute-start(f32[48]{0:T(128)} %param.15), channel_id=1, source_target_pairs={{0,160},{1,96},{2,128},{3,64},{4,0},{5,192},{6,32},{7,224},{8,168}... | collective-permute-start | bytes 584 | tf_op jit(solution)/shard_map/ppermute | solution.py:485
  10.4 16.2 %collective-permute-start = (f32[16,8,512]{2,1,0:T(8,128)}, f32[16,8,512]{2,1,0:T(8,128)}, u32[]{:S(2)}, u32[]{:S(2)}) collective-permute-start(f32[16,8,512]{2,1,0:T(8,128)} %get-tuple-element.17), channel_id=1, source_target_pairs={{0,1},{1,2},{2,3},{3,4},{4,5},{5,6},{6,7},{8,9},{9,10},{10,11},{11... | collective-permute-start | bytes 786440 | tf_op jit(solution)/shard_map/ppermute | solution.py:487
  12.7 13.9 %collective-permute-start.1 = (f32[16,8,512]{2,1,0:T(8,128)}, f32[16,8,512]{2,1,0:T(8,128)}, u32[]{:S(2)}, u32[]{:S(2)}) collective-permute-start(f32[16,8,512]{2,1,0:T(8,128)} %get-tuple-element.18), channel_id=1, source_target_pairs={{1,0},{2,1},{3,2},{4,3},{5,4},{6,5},{7,6},{9,8},{10,9},{11,10},{12... | collective-permute-start | bytes 786440 | tf_op jit(solution)/shard_map/ppermute | solution.py:487
  15.6 18.2 %all-to-all-start = ((f32[32,1,128]{2,1,0:T(1,128)}), f32[32,1,128]{2,1,0:T(1,128)S(1)}, u32[]{:S(2)}, u32[]{:S(2)}) async-start(f32[32,1,128]{2,1,0:T(1,128)} %bitcast.11), calls=%async_computation | async-start | bytes 32768 | tf_op jit(solution)/shard_map/all_to_all | solution.py:456
  28.4 14.4 %collective-permute-start.3 = (f32[6,72,512]{2,1,0:T(8,128)}, f32[6,72,512]{2,1,0:T(8,128)}, u32[]{:S(2)}, u32[]{:S(2)}) collective-permute-start(f32[6,72,512]{2,1,0:T(8,128)} %get-tuple-element.22), channel_id=1, source_target_pairs={{0,8},{8,16},{16,24},{24,32},{32,40},{40,48},{48,56},{56,64},{64,7... | collective-permute-start | bytes 2654216 | tf_op jit(solution)/shard_map/ppermute | solution.py:490
  31.9 14.7 %collective-permute-start.4 = (f32[6,72,512]{2,1,0:T(8,128)}, f32[6,72,512]{2,1,0:T(8,128)}, u32[]{:S(2)}, u32[]{:S(2)}) collective-permute-start(f32[6,72,512]{2,1,0:T(8,128)} %get-tuple-element.23), channel_id=1, source_target_pairs={{8,0},{16,8},{24,16},{32,24},{40,32},{48,40},{56,48},{64,56},{72,6... | collective-permute-start | bytes 2654216 | tf_op jit(solution)/shard_map/ppermute | solution.py:490
  37.7 19.9 %all-to-all-start.1 = ((f32[8,1,128]{2,1,0:T(1,128)}), f32[8,1,128]{2,1,0:T(1,128)S(1)}, u32[]{:S(2)}, u32[]{:S(2)}) async-start(f32[8,1,128]{2,1,0:T(1,128)} %bitcast.14), calls=%async_computation.1 | async-start | bytes 8192 | tf_op jit(solution)/shard_map/all_to_all | solution.py:456

commit v7 on v5

--- a/solution.py
+++ b/solution.py
@@ -35,8 +35,8 @@
 SLIP_MOVES = [
     ((4 * g + r) * NGY + j, (4 * landing(g, j) + r) * NGY + g) for g in range(8) for r in range(4) for j in range(NGY)
 ]
-X_UP = [(i, i + 1) for i in range(NGX - 1)]
-X_DOWN = [(j, i) for i, j in X_UP]
+X_FAR = [pair for i in range(1, NGX - 1, 2) for pair in ((i, i + 1), (i + 1, i))]
+X_NEAR = [pair for i in range(0, NGX, 2) for pair in ((i, i + 1), (i + 1, i))]
 Y_UP = [(i, i + 1) for i in range(NGY - 1)]
 Y_DOWN = [(j, i) for i, j in Y_UP]
 
@@ -55,6 +55,14 @@
 
 def all_far(*values):
     return tuple(far(v) for v in values)
+
+
+def core():
+    return lax.rem(lax.axis_index("gx"), 2)
+
+
+def sent_planes(core_index):
+    return (CX - HALO) * core_index, (CX - HALO) * (1 - core_index)
 
 
 def started(*copies):
@@ -78,7 +86,7 @@
     return jnp.sum(jnp.where(row == column, row_value, 0.0), axis=1, keepdims=True)
 
 
-def pack_kernel(p, k, y_up, y_down, x_up, x_down, tiles, rows, sems):
+def pack_kernel(p, k, y_up, y_down, x_far, x_near, tiles, rows, sems):
     tops = started(
         pltpu.make_async_copy(p.at[:, pl.ds(CY - 8, 8), :], tiles.at[0], sems.at[0]),
         pltpu.make_async_copy(k.at[:, pl.ds(CY - 8, 8), :], tiles.at[1], sems.at[1]),
@@ -94,7 +102,7 @@
                 for n, source in enumerate((p, k))
             ]
         )
-        for side, start in enumerate((CX - HALO, 0))
+        for side, start in enumerate(sent_planes(core()))
     ]
     row = lax.broadcasted_iota(jnp.int32, (8, NZ), 0)
     waited(tops)
@@ -106,7 +114,7 @@
 
     lax.fori_loop(0, CX, plane, 0)
     stores = []
-    for side, target in enumerate((x_up, x_down)):
+    for side, target in enumerate((x_far, x_near)):
         waited(loads[side])
         stores += started(pltpu.make_async_copy(rows.at[side], target.at[:, pl.ds(0, CY)], sems.at[8 + side]))
     waited(stores)
@@ -173,18 +181,18 @@
     return p, k
 
 
-def sides_kernel(x_up, x_down, y_up, y_down, token, x_up_out, x_down_out, tiles, sems):
-    del x_up, x_down, token
+def sides_kernel(x_far, x_near, y_up, y_down, token, x_far_out, x_near_out, tiles, sems):
+    del x_far, x_near, token
     row = lax.broadcasted_iota(jnp.int32, (8, NZ), 0)
     copies = []
-    for side, (target, start) in enumerate(((x_up_out, CX - HALO), (x_down_out, 0))):
+    for side, (target, start) in enumerate(zip((x_far_out, x_near_out), sent_planes(core()))):
         for n in range(HALO):
             tiles[side, n], tiles[side, HALO + n] = halo_rows(y_up[start + n], y_down[start + n], row)
         copies += started(pltpu.make_async_copy(tiles.at[side], target.at[:, pl.ds(CY, 8)], sems.at[side]))
     waited(copies)
 
 
-def sides(x_up, x_down, y_up, y_down, token):
+def sides(x_far, x_near, y_up, y_down, token):
     return pl.pallas_call(
         sides_kernel,
         out_shape=(HBM((2 * HALO, CY + 8, NZ), F32),) * 2,
@@ -194,7 +202,7 @@
         input_output_aliases={0: 0, 1: 1},
         compiler_params=pltpu.CompilerParams(vmem_limit_bytes=4 << 20),
         name="sides",
-    )(far(x_up), far(x_down), y_up, y_down, token)
+    )(far(x_far), far(x_near), y_up, y_down, token)
 
 
 def rates_kernel(arrived, kernel_far, out, cells, acc, kernel, sems):
@@ -283,10 +291,12 @@
 
 
 def diffusion_kernel(
-    p_far, k_far, y_up, y_down, x_up, x_down, cells, out, answers, s, q, a, q1, q2, p, k, full, wide, asked, sems
+    p_far, k_far, y_up, y_down, x_far, x_near, cells, out, answers, s, q, a, q1, q2, p, k, full, wide, asked, sems
 ):
     loads = []
-    low = started(pltpu.make_async_copy(x_up, wide.at[0], sems.at[12]))
+    odd = core()
+    started(pltpu.make_async_copy(x_far, wide.at[odd], sems.at[12 + odd]))
+    started(pltpu.make_async_copy(x_near, wide.at[1 - odd], sems.at[13 - odd]))
     for n in range(4):
         planes = pl.ds(4 * n, 4)
         loads.append(
@@ -295,7 +305,8 @@
                 pltpu.make_async_copy(k_far.at[planes], k.at[planes], sems.at[2 * n + 1]),
             )
         )
-    high = started(pltpu.make_async_copy(x_down, wide.at[1], sems.at[13]))
+    low = [pltpu.make_async_copy(x_far, wide.at[0], sems.at[12])]
+    high = [pltpu.make_async_copy(x_near, wide.at[1], sems.at[13])]
     ask = started(pltpu.make_async_copy(cells, asked, sems.at[8]))
     lane = lax.broadcasted_iota(jnp.int32, (8, LANES), 1)
     row = lax.broadcasted_iota(jnp.int32, (8, LANES), 0)
@@ -408,7 +419,7 @@
     waited(stores)
 
 
-def diffusion(p, k, y_up, y_down, x_up, x_down, cells):
+def diffusion(p, k, y_up, y_down, x_far, x_near, cells):
     return pl.pallas_call(
         diffusion_kernel,
         out_shape=(shape(CX, CY, NZ), shape(NGX, LANES)),
@@ -420,7 +431,7 @@
         compiler_params=pltpu.CompilerParams(vmem_limit_bytes=34 << 20),
         cost_estimate=pl.CostEstimate(flops=60_000_000, bytes_accessed=12_000_000, transcendentals=0),
         name="diffusion",
-    )(far(p), far(k), y_up, y_down, x_up, x_down, cells)
+    )(far(p), far(k), y_up, y_down, x_far, x_near, cells)
 
 
 def friction_kernel(rates, answers, terms, state_out, rate_out):
@@ -479,18 +490,18 @@
         evolution_effect,
         slip_distance,
     )
-    y_up, y_down, x_up, x_down = pack(pressure, permeability)
+    y_up, y_down, x_far, x_near = pack(pressure, permeability)
     wanted, terms = prepare(*[v.reshape(1, TRI) for v in rows])
     y_up, y_down = lax.ppermute(y_up, "gy", Y_UP), lax.ppermute(y_down, "gy", Y_DOWN)
     lane = lax.broadcasted_iota(jnp.int32, (NGX, LANES), 1)
     row = jnp.pad(lax.ppermute(slip_rate, ("gx", "gy"), SLIP_MOVES), (0, LANES - TRI)).reshape(1, LANES)
     leaving = jnp.where(lane < TRI, row, wanted)
     arrived = exchanged(leaving, "gx")
-    x_up, x_down = sides(x_up, x_down, y_up, y_down, leaving)
-    x_up, x_down = lax.ppermute(x_up, "gx", X_UP), lax.ppermute(x_down, "gx", X_DOWN)
+    x_far, x_near = sides(x_far, x_near, y_up, y_down, leaving)
+    x_far, x_near = lax.ppermute(x_far, "gx", X_FAR), lax.ppermute(x_near, "gx", X_NEAR)
     partial_sums, cells = partial_rates(arrived, kernel)
     rates = exchanged(partial_sums, "gy")
-    field, answers = diffusion(pressure, permeability, y_up, y_down, x_up, x_down, cells)
+    field, answers = diffusion(pressure, permeability, y_up, y_down, x_far, x_near, cells)
     answers = exchanged(answers, "gx")
     state_next, log_rate = friction(rates, answers, terms)
     return field, state_next.reshape(TRI), log_rate.reshape(TRI)

time: 70.3 us -> 67.5 us (0.960)
  starting transfers between devices: 31.3 us -> 29.5 us
    ppermute x2, waiting for transfers between devices: 2.46 us -> 0.01 us  [the longest x1 0.01 us: local(): lax.ppermute(x_near, 'gx', X_NEAR)]
    ppermute x2, starting transfers between devices: 5.46 us -> 3.64 us  [the longest x1 3.54 us: local(): lax.ppermute(x_far, 'gx', X_FAR)]
    all_to_all x2, waiting for transfers between devices: 0.7 us -> 2.51 us  [exchanged(): return lax.all_to_all(value, axis, split_axis=0, concat_axis=0, tiled=True)]
  transfers between devices with their start and end apart: 7 -> 7, of which waited for: 2 -> 1; matrix products, arithmetic and copies ran while one was open for 1% -> 1% of each run, Pallas kernels for 26% -> 28%
where the time goes in v7:
time: 67.5 us; the launch traced here: 67.1 us
  starting transfers between devices  29.5 us (44%)
  Pallas kernels  19.1 us (28%)
  blocking collectives  14.6 us (22%)
  waiting for transfers between devices  2.53 us (4%)
  between operations  0.77 us (1%)
    all_to_all x2, starting transfers between devices, exchanged(): return lax.all_to_all(value, axis, split_axis=0, concat_axis=0, tiled=True)  16.7 us
    all_to_all x1, blocking collectives, exchanged(): return lax.all_to_all(value, axis, split_axis=0, concat_axis=0, tiled=True)  14.6 us
    pallas_call x1, Pallas kernels, diffusion(): pl.pallas_call(diffusion_kernel, out_shape=(shape(CX, CY, NZ), shape(NGX,...  10.2 us
    ppermute x1, starting transfers between devices, local(): lax.ppermute(slip_rate, ('gx', 'gy'), SLIP_MOVES)  6.28 us
    pallas_call x1, Pallas kernels, partial_rates(): pl.pallas_call(rates_kernel, out_shape=(shape(NGY, LANES), shape(NGX, LAN...  3.82 us
    ppermute x1, starting transfers between devices, local(): lax.ppermute(x_far, 'gx', X_FAR)  3.54 us
    pallas_call x1, Pallas kernels, pack(): pl.pallas_call(pack_kernel, out_shape=(shape(CX, 8, NZ),) * 2 + (HBM((2 *...  2.66 us
    all_to_all x2, waiting for transfers between devices, exchanged(): return lax.all_to_all(value, axis, split_axis=0, concat_axis=0, tiled=True)  2.51 us
  transfers between devices with their start and end apart: 7, of which 1 were waited for; matrix products, arithmetic and copies ran while one was open for 1% of the time, Pallas kernels for 28%

profile of v7, /device:TPU:1, one launch (start us, length us, event | category | flops | bytes accessed | tf_op | source)
XLA Modules:
  0.0 67.1 jit_solution(7241179764970449091)
XLA Ops:
  0.6 6.3 %collective-permute-start.2 = (f32[48]{0:T(128)}, f32[48]{0:T(128)S(1)}, u32[]{:S(2)}, u32[]{:S(2)}) collective-permute-start(f32[48]{0:T(128)} %param.15), channel_id=1, source_target_pairs={{0,160},{1,96},{2,128},{3,64},{4,0},{5,192},{6,32},{7,224},{8,168}... | collective-permute-start | bytes 584 | tf_op jit(solution)/shard_map/ppermute | solution.py:497
  6.9 2.7 %pack.1 = (f32[16,8,512]{2,1,0:T(8,128)S(1)}, f32[16,8,512]{2,1,0:T(8,128)S(1)}, f32[6,72,512]{2,1,0:T(8,128)}, f32[6,72,512]{2,1,0:T(8,128)}) custom-call(f32[16,64,512]{2,1,0:T(8,128)} %p_far.1, f32[16,64,512]{2,1,0:T(8,128)} %k_far.1), custom_call_target="tpu_custom_call" | custom-call | tf_op jit(solution)/shard_map/pack/pallas_call | solution.py:124
  9.6 1.6 %collective-permute-start = (f32[16,8,512]{2,1,0:T(8,128)S(1)}, f32[16,8,512]{2,1,0:T(8,128)S(1)}, u32[]{:S(2)}, u32[]{:S(2)}) collective-permute-start(f32[16,8,512]{2,1,0:T(8,128)S(1)} %get-tuple-element.17), channel_id=1, source_target_pairs={{0,1},{1,2},{2,3},{3,4},{4,5},{5,6},{6,7},{8,9},{9,10},{10,11},{11... | collective-permute-start | bytes 786440 | tf_op jit(solution)/shard_map/ppermute | solution.py:495
  11.2 1.3 %collective-permute-start.1 = (f32[16,8,512]{2,1,0:T(8,128)S(1)}, f32[16,8,512]{2,1,0:T(8,128)S(1)}, u32[]{:S(2)}, u32[]{:S(2)}) collective-permute-start(f32[16,8,512]{2,1,0:T(8,128)S(1)} %get-tuple-element.18), channel_id=1, source_target_pairs={{1,0},{2,1},{3,2},{4,3},{5,4},{6,5},{7,6},{9,8},{10,9},{11,10},{12... | collective-permute-start | bytes 786440 | tf_op jit(solution)/shard_map/ppermute | solution.py:495
  12.5 1.1 %prepare.1 = (f32[32,128]{1,0:T(8,128)S(1)}, f32[8,128]{1,0:T(8,128)S(1)}) custom-call(s32[1,48]{1,0:T(1,128)} %bitcast.27, s32[1,48]{1,0:T(1,128)} %bitcast.28, f32[1,48]{1,0:T(1,128)} %bitcast.35, f32[1,48]{1,0:T(1,128)} %bitcast.29, f32[1,48]{1,0:T(1,128)} %bitcast.30, f32[1,48]{1,0:T(1,128)} %bitcast.31, f32[1,48]{1,0:T(1,128)} %bitcast.32, ...), custom_call_target="tpu_custom_call" | custom-call | tf_op jit(solution)/shard_map/prepare/pallas_call | solution.py:167
  13.5 0.0 collective-permute-done.2
  13.6 0.6 broadcast_select_fusion.token
  14.2 10.9 %all-to-all-start = ((f32[32,1,128]{2,1,0:T(1,128)}), f32[32,1,128]{2,1,0:T(1,128)S(1)}, u32[]{:S(2)}, u32[]{:S(2)}) async-start(f32[32,1,128]{2,1,0:T(1,128)} %bitcast.10), calls=%async_computation | async-start | bytes 32768 | tf_op jit(solution)/shard_map/all_to_all | solution.py:465
  25.1 0.0 collective-permute-done.y_up
  25.1 0.0 collective-permute-done.1.y_down
  25.1 0.7 %sides.1 = (f32[6,72,512]{2,1,0:T(8,128)}, f32[6,72,512]{2,1,0:T(8,128)}) custom-call(f32[6,72,512]{2,1,0:T(8,128)} %get-tuple-element.19.x_far, f32[6,72,512]{2,1,0:T(8,128)} %get-tuple-element.20.x_near, f32[16,8,512]{2,1,0:T(8,128)S(1)} %collective-permute-done.y_up, ...), custom_call_target="tpu_custom_call", output_to_operand_aliasing={{0}: (0, {}), {1}: (1, {})} | custom-call | tf_op jit(solution)/shard_map/sides/pallas_call | solution.py:196
  25.9 3.5 %collective-permute-start.3 = (f32[6,72,512]{2,1,0:T(8,128)}, f32[6,72,512]{2,1,0:T(8,128)}, u32[]{:S(2)}, u32[]{:S(2)}) collective-permute-start(f32[6,72,512]{2,1,0:T(8,128)} %get-tuple-element.22), channel_id=1, source_target_pairs={{8,16},{16,8},{24,32},{32,24},{40,48},{48,40},{56,64},{64,56},{72,... | collective-permute-start | bytes 2654216 | tf_op jit(solution)/shard_map/ppermute | solution.py:501
  29.4 0.1 collective-permute-start.4
  29.5 2.5 %all-to-all-done = f32[32,1,128]{2,1,0:T(1,128)S(1)} async-done(((f32[32,1,128]{2,1,0:T(1,128)}), f32[32,1,128]{2,1,0:T(1,128)S(1)}, u32[]{:S(2)}, u32[]{:S(2)}) %all-to-all-start) | async-done | bytes 16416 | tf_op jit(solution)/shard_map/all_to_all | solution.py:465
  32.0 3.8 %rates.1 = (f32[8,128]{1,0:T(8,128)}, s32[32,128]{1,0:T(8,128)S(1)}) custom-call(f32[32,128]{1,0:T(8,128)S(1)} %bitcast.24, f32[2,384,1536]{2,1,0:T(8,128)} %kernel_far.1), custom_call_target="tpu_custom_call" | custom-call | flops 999999995904 | bytes 6000000000 | tf_op jit(solution)/shard_map/rates/pallas_call | solution.py:262
  35.9 5.8 %all-to-all-start.1 = ((f32[8,1,128]{2,1,0:T(1,128)}), f32[8,1,128]{2,1,0:T(1,128)S(1)}, u32[]{:S(2)}, u32[]{:S(2)}) async-start(f32[8,1,128]{2,1,0:T(1,128)} %bitcast.13), calls=%async_computation.1 | async-start | bytes 8192 | tf_op jit(solution)/shard_map/all_to_all | solution.py:465
  41.6 0.0 collective-permute-done.3.x_far
  41.6 0.0 collective-permute-done.4.x_near
  41.6 10.2 %diffusion.1 = (f32[16,64,512]{2,1,0:T(8,128)}, f32[32,128]{1,0:T(8,128)S(1)}) custom-call(f32[16,64,512]{2,1,0:T(8,128)} %p_far.1, f32[16,64,512]{2,1,0:T(8,128)} %k_far.1, f32[16,8,512]{2,1,0:T(8,128)S(1)} %collective-permute-done.y_up, f32[16,8,512]{2,1,0:T(8,128)S(1)} %collective-permute-done.1.y_down, f32[6,72,512]{2,1,0:T(8,128)} %collective-permute-done.3.x_far, ...), custom_call_target="tpu_custom_call" | custom-call | flops 60000000 | bytes 12000000 | tf_op jit(solution)/shard_map/diffusion/pallas_call | solution.py:423
  51.9 0.0 all-to-all-done.1
  51.9 14.6 %all_to_all.33 = f32[32,1,128]{2,1,0:T(1,128)S(1)} all-to-all(f32[32,1,128]{2,1,0:T(1,128)S(1)} %bitcast.25), channel_id=1, replica_groups=mesh['gx'=32,'gy'=8] {'gx'}, dimensions={0} | all-to-all | bytes 32768 | tf_op jit(solution)/shard_map/all_to_all | solution.py:465
  66.5 0.6 friction.1
  (2 shorter events, 0.0 us)
Async XLA Ops:
  0.6 12.9 %collective-permute-start.2 = (f32[48]{0:T(128)}, f32[48]{0:T(128)S(1)}, u32[]{:S(2)}, u32[]{:S(2)}) collective-permute-start(f32[48]{0:T(128)} %param.15), channel_id=1, source_target_pairs={{0,160},{1,96},{2,128},{3,64},{4,0},{5,192},{6,32},{7,224},{8,168}... | collective-permute-start | bytes 584 | tf_op jit(solution)/shard_map/ppermute | solution.py:497
  9.6 15.5 %collective-permute-start = (f32[16,8,512]{2,1,0:T(8,128)S(1)}, f32[16,8,512]{2,1,0:T(8,128)S(1)}, u32[]{:S(2)}, u32[]{:S(2)}) collective-permute-start(f32[16,8,512]{2,1,0:T(8,128)S(1)} %get-tuple-element.17), channel_id=1, source_target_pairs={{0,1},{1,2},{2,3},{3,4},{4,5},{5,6},{6,7},{8,9},{9,10},{10,11},{11... | collective-permute-start | bytes 786440 | tf_op jit(solution)/shard_map/ppermute | solution.py:495
  11.2 14.0 %collective-permute-start.1 = (f32[16,8,512]{2,1,0:T(8,128)S(1)}, f32[16,8,512]{2,1,0:T(8,128)S(1)}, u32[]{:S(2)}, u32[]{:S(2)}) collective-permute-start(f32[16,8,512]{2,1,0:T(8,128)S(1)} %get-tuple-element.18), channel_id=1, source_target_pairs={{1,0},{2,1},{3,2},{4,3},{5,4},{6,5},{7,6},{9,8},{10,9},{11,10},{12... | collective-permute-start | bytes 786440 | tf_op jit(solution)/shard_map/ppermute | solution.py:495
  14.2 17.9 %all-to-all-start = ((f32[32,1,128]{2,1,0:T(1,128)}), f32[32,1,128]{2,1,0:T(1,128)S(1)}, u32[]{:S(2)}, u32[]{:S(2)}) async-start(f32[32,1,128]{2,1,0:T(1,128)} %bitcast.10), calls=%async_computation | async-start | bytes 32768 | tf_op jit(solution)/shard_map/all_to_all | solution.py:465
  25.9 15.8 %collective-permute-start.3 = (f32[6,72,512]{2,1,0:T(8,128)}, f32[6,72,512]{2,1,0:T(8,128)}, u32[]{:S(2)}, u32[]{:S(2)}) collective-permute-start(f32[6,72,512]{2,1,0:T(8,128)} %get-tuple-element.22), channel_id=1, source_target_pairs={{8,16},{16,8},{24,32},{32,24},{40,48},{48,40},{56,64},{64,56},{72,... | collective-permute-start | bytes 2654216 | tf_op jit(solution)/shard_map/ppermute | solution.py:501
  29.4 12.2 %collective-permute-start.4 = (f32[6,72,512]{2,1,0:T(8,128)}, f32[6,72,512]{2,1,0:T(8,128)}, u32[]{:S(2)}, u32[]{:S(2)}) collective-permute-start(f32[6,72,512]{2,1,0:T(8,128)} %get-tuple-element.23), channel_id=1, source_target_pairs={{0,8},{8,0},{16,24},{24,16},{32,40},{40,32},{48,56},{56,48},{64,72... | collective-permute-start | bytes 2654216 | tf_op jit(solution)/shard_map/ppermute | solution.py:501
  35.9 16.0 %all-to-all-start.1 = ((f32[8,1,128]{2,1,0:T(1,128)}), f32[8,1,128]{2,1,0:T(1,128)S(1)}, u32[]{:S(2)}, u32[]{:S(2)}) async-start(f32[8,1,128]{2,1,0:T(1,128)} %bitcast.13), calls=%async_computation.1 | async-start | bytes 8192 | tf_op jit(solution)/shard_map/all_to_all | solution.py:465

commit v8 on v7

--- a/solution.py
+++ b/solution.py
@@ -37,8 +37,8 @@
 ]
 X_FAR = [pair for i in range(1, NGX - 1, 2) for pair in ((i, i + 1), (i + 1, i))]
 X_NEAR = [pair for i in range(0, NGX, 2) for pair in ((i, i + 1), (i + 1, i))]
-Y_UP = [(i, i + 1) for i in range(NGY - 1)]
-Y_DOWN = [(j, i) for i, j in Y_UP]
+Y_FAR = [pair for i in range(1, NGY - 1, 2) for pair in ((i, i + 1), (i + 1, i))]
+Y_NEAR = [pair for i in range(0, NGY, 2) for pair in ((i, i + 1), (i + 1, i))]
 
 
 def spec(space=VMEM):
@@ -63,6 +63,11 @@
 
 def sent_planes(core_index):
     return (CX - HALO) * core_index, (CX - HALO) * (1 - core_index)
+
+
+def by_turn(first, second):
+    odd = lax.rem(lax.axis_index("gy"), 2) == 1
+    return jnp.where(odd, first, second), jnp.where(odd, second, first)
 
 
 def started(*copies):
@@ -86,7 +91,7 @@
     return jnp.sum(jnp.where(row == column, row_value, 0.0), axis=1, keepdims=True)
 
 
-def pack_kernel(p, k, y_up, y_down, x_far, x_near, tiles, rows, sems):
+def pack_kernel(p, k, y_far, y_near, x_far, x_near, tiles, rows, sems):
     tops = started(
         pltpu.make_async_copy(p.at[:, pl.ds(CY - 8, 8), :], tiles.at[0], sems.at[0]),
         pltpu.make_async_copy(k.at[:, pl.ds(CY - 8, 8), :], tiles.at[1], sems.at[1]),
@@ -108,8 +113,9 @@
     waited(tops)
 
     def plane(x, carry):
-        y_up[x] = jnp.where(row >= 5, tiles[0, x], pltpu.roll(tiles[1, x], 3, 0))
-        y_down[x] = jnp.where(row < 3, tiles[2, x], pltpu.roll(tiles[3, x], 5, 0))
+        top = jnp.where(row >= 5, tiles[0, x], pltpu.roll(tiles[1, x], 3, 0))
+        bottom = jnp.where(row < 3, tiles[2, x], pltpu.roll(tiles[3, x], 5, 0))
+        y_far[x], y_near[x] = by_turn(top, bottom)
         return carry
 
     lax.fori_loop(0, CX, plane, 0)
@@ -181,18 +187,18 @@
     return p, k
 
 
-def sides_kernel(x_far, x_near, y_up, y_down, token, x_far_out, x_near_out, tiles, sems):
+def sides_kernel(x_far, x_near, y_far, y_near, token, x_far_out, x_near_out, tiles, sems):
     del x_far, x_near, token
     row = lax.broadcasted_iota(jnp.int32, (8, NZ), 0)
     copies = []
     for side, (target, start) in enumerate(zip((x_far_out, x_near_out), sent_planes(core()))):
         for n in range(HALO):
-            tiles[side, n], tiles[side, HALO + n] = halo_rows(y_up[start + n], y_down[start + n], row)
+            tiles[side, n], tiles[side, HALO + n] = halo_rows(*by_turn(y_near[start + n], y_far[start + n]), row)
         copies += started(pltpu.make_async_copy(tiles.at[side], target.at[:, pl.ds(CY, 8)], sems.at[side]))
     waited(copies)
 
 
-def sides(x_far, x_near, y_up, y_down, token):
+def sides(x_far, x_near, y_far, y_near, token):
     return pl.pallas_call(
         sides_kernel,
         out_shape=(HBM((2 * HALO, CY + 8, NZ), F32),) * 2,
@@ -202,7 +208,7 @@
         input_output_aliases={0: 0, 1: 1},
         compiler_params=pltpu.CompilerParams(vmem_limit_bytes=4 << 20),
         name="sides",
-    )(far(x_far), far(x_near), y_up, y_down, token)
+    )(far(x_far), far(x_near), y_far, y_near, token)
 
 
 def rates_kernel(arrived, kernel_far, out, cells, acc, kernel, sems):
@@ -291,7 +297,7 @@
 
 
 def diffusion_kernel(
-    p_far, k_far, y_up, y_down, x_far, x_near, cells, out, answers, s, q, a, q1, q2, p, k, full, wide, asked, sems
+    p_far, k_far, y_far, y_near, x_far, x_near, cells, out, answers, s, q, a, q1, q2, p, k, full, wide, asked, sems
 ):
     loads = []
     odd = core()
@@ -334,7 +340,7 @@
         for i in range(CHUNKS):
             lanes = pl.ds(LANES * i, LANES)
             n = (x + HALO) * CHUNKS + i
-            put(n, (0, CY + 8), *halo_rows(y_up[x, :, lanes], y_down[x, :, lanes], row))
+            put(n, (0, CY + 8), *halo_rows(*by_turn(y_near[x, :, lanes], y_far[x, :, lanes]), row))
             for t in range(CY // 8):
                 rows = pl.ds(8 * t, 8)
                 put(n, (8 * t + 8,), p[x, rows, lanes], k[x, rows, lanes])
@@ -419,7 +425,7 @@
     waited(stores)
 
 
-def diffusion(p, k, y_up, y_down, x_far, x_near, cells):
+def diffusion(p, k, y_far, y_near, x_far, x_near, cells):
     return pl.pallas_call(
         diffusion_kernel,
         out_shape=(shape(CX, CY, NZ), shape(NGX, LANES)),
@@ -431,7 +437,7 @@
         compiler_params=pltpu.CompilerParams(vmem_limit_bytes=34 << 20),
         cost_estimate=pl.CostEstimate(flops=60_000_000, bytes_accessed=12_000_000, transcendentals=0),
         name="diffusion",
-    )(far(p), far(k), y_up, y_down, x_far, x_near, cells)
+    )(far(p), far(k), y_far, y_near, x_far, x_near, cells)
 
 
 def friction_kernel(rates, answers, terms, state_out, rate_out):
@@ -490,18 +496,18 @@
         evolution_effect,
         slip_distance,
     )
-    y_up, y_down, x_far, x_near = pack(pressure, permeability)
+    y_far, y_near, x_far, x_near = pack(pressure, permeability)
     wanted, terms = prepare(*[v.reshape(1, TRI) for v in rows])
-    y_up, y_down = lax.ppermute(y_up, "gy", Y_UP), lax.ppermute(y_down, "gy", Y_DOWN)
+    y_far, y_near = lax.ppermute(y_far, "gy", Y_FAR), lax.ppermute(y_near, "gy", Y_NEAR)
     lane = lax.broadcasted_iota(jnp.int32, (NGX, LANES), 1)
     row = jnp.pad(lax.ppermute(slip_rate, ("gx", "gy"), SLIP_MOVES), (0, LANES - TRI)).reshape(1, LANES)
     leaving = jnp.where(lane < TRI, row, wanted)
     arrived = exchanged(leaving, "gx")
-    x_far, x_near = sides(x_far, x_near, y_up, y_down, leaving)
+    x_far, x_near = sides(x_far, x_near, y_far, y_near, leaving)
     x_far, x_near = lax.ppermute(x_far, "gx", X_FAR), lax.ppermute(x_near, "gx", X_NEAR)
     partial_sums, cells = partial_rates(arrived, kernel)
     rates = exchanged(partial_sums, "gy")
-    field, answers = diffusion(pressure, permeability, y_up, y_down, x_far, x_near, cells)
+    field, answers = diffusion(pressure, permeability, y_far, y_near, x_far, x_near, cells)
     answers = exchanged(answers, "gx")
     state_next, log_rate = friction(rates, answers, terms)
     return field, state_next.reshape(TRI), log_rate.reshape(TRI)

time: 67.5 us -> 66.7 us (0.988)
  starting transfers between devices: 29.5 us -> 27.4 us
  blocking collectives: 14.6 us -> 15.7 us
    ppermute x2, starting transfers between devices: 2.86 us -> 1.73 us  [the longest x1 1.05 us: local(): lax.ppermute(y_near, 'gy', Y_NEAR)]
    all_to_all x1, blocking collectives: 14.6 us -> 15.7 us  [exchanged(): return lax.all_to_all(value, axis, split_axis=0, concat_axis=0, tiled=True)]
    all_to_all x2, starting transfers between devices: 16.7 us -> 15.7 us  [exchanged(): return lax.all_to_all(value, axis, split_axis=0, concat_axis=0, tiled=True)]
  transfers between devices with their start and end apart: 7 -> 7, of which waited for: 1 -> 2; matrix products, arithmetic and copies ran while one was open for 1% -> 1% of each run, Pallas kernels for 28% -> 28%
where the time goes in v8:
time: 66.7 us; the launch traced here: 66.4 us
  starting transfers between devices  27.4 us (41%)
  Pallas kernels  19.1 us (29%)
  blocking collectives  15.7 us (24%)
  waiting for transfers between devices  2.86 us (4%)
  between operations  0.74 us (1%)
    all_to_all x2, starting transfers between devices, exchanged(): return lax.all_to_all(value, axis, split_axis=0, concat_axis=0, tiled=True)  15.7 us
    all_to_all x1, blocking collectives, exchanged(): return lax.all_to_all(value, axis, split_axis=0, concat_axis=0, tiled=True)  15.7 us
    pallas_call x1, Pallas kernels, diffusion(): pl.pallas_call(diffusion_kernel, out_shape=(shape(CX, CY, NZ), shape(NGX,...  10.2 us
    ppermute x1, starting transfers between devices, local(): lax.ppermute(slip_rate, ('gx', 'gy'), SLIP_MOVES)  6.28 us
    pallas_call x1, Pallas kernels, partial_rates(): pl.pallas_call(rates_kernel, out_shape=(shape(NGY, LANES), shape(NGX, LAN...  3.82 us
    ppermute x1, starting transfers between devices, local(): lax.ppermute(x_far, 'gx', X_FAR)  3.54 us
    pallas_call x1, Pallas kernels, pack(): pl.pallas_call(pack_kernel, out_shape=(shape(CX, 8, NZ),) * 2 + (HBM((2 *...  2.66 us
    all_to_all x2, waiting for transfers between devices, exchanged(): return lax.all_to_all(value, axis, split_axis=0, concat_axis=0, tiled=True)  2.51 us
  transfers between devices with their start and end apart: 7, of which 2 were waited for; matrix products, arithmetic and copies ran while one was open for 1% of the time, Pallas kernels for 28%

profile of v8, /device:TPU:1, one launch (start us, length us, event | category | flops | bytes accessed | tf_op | source)
XLA Modules:
  0.0 66.4 jit_solution(10312548669311295007)
XLA Ops:
  0.6 6.3 %collective-permute-start.2 = (f32[48]{0:T(128)}, f32[48]{0:T(128)S(1)}, u32[]{:S(2)}, u32[]{:S(2)}) collective-permute-start(f32[48]{0:T(128)} %param.15), channel_id=1, source_target_pairs={{0,160},{1,96},{2,128},{3,64},{4,0},{5,192},{6,32},{7,224},{8,168}... | collective-permute-start | bytes 584 | tf_op jit(solution)/shard_map/ppermute | solution.py:503
  6.9 2.7 %pack.1 = (f32[16,8,512]{2,1,0:T(8,128)S(1)}, f32[16,8,512]{2,1,0:T(8,128)S(1)}, f32[6,72,512]{2,1,0:T(8,128)}, f32[6,72,512]{2,1,0:T(8,128)}) custom-call(f32[16,64,512]{2,1,0:T(8,128)} %p_far.1, f32[16,64,512]{2,1,0:T(8,128)} %k_far.1), custom_call_target="tpu_custom_call" | custom-call | tf_op jit(solution)/shard_map/pack/pallas_call | solution.py:130
  9.6 0.7 %collective-permute-start = (f32[16,8,512]{2,1,0:T(8,128)S(1)}, f32[16,8,512]{2,1,0:T(8,128)S(1)}, u32[]{:S(2)}, u32[]{:S(2)}) collective-permute-start(f32[16,8,512]{2,1,0:T(8,128)S(1)} %get-tuple-element.17), channel_id=1, source_target_pairs={{1,2},{2,1},{3,4},{4,3},{5,6},{6,5},{9,10},{10,9},{11,12},{12,11},... | collective-permute-start | bytes 786440 | tf_op jit(solution)/shard_map/ppermute | solution.py:501
  10.3 1.1 %collective-permute-start.1 = (f32[16,8,512]{2,1,0:T(8,128)S(1)}, f32[16,8,512]{2,1,0:T(8,128)S(1)}, u32[]{:S(2)}, u32[]{:S(2)}) collective-permute-start(f32[16,8,512]{2,1,0:T(8,128)S(1)} %get-tuple-element.18), channel_id=1, source_target_pairs={{0,1},{1,0},{2,3},{3,2},{4,5},{5,4},{6,7},{7,6},{8,9},{9,8},{10,11... | collective-permute-start | bytes 786440 | tf_op jit(solution)/shard_map/ppermute | solution.py:501
  11.3 1.0 %prepare.1 = (f32[32,128]{1,0:T(8,128)S(1)}, f32[8,128]{1,0:T(8,128)S(1)}) custom-call(s32[1,48]{1,0:T(1,128)} %bitcast.27, s32[1,48]{1,0:T(1,128)} %bitcast.28, f32[1,48]{1,0:T(1,128)} %bitcast.35, f32[1,48]{1,0:T(1,128)} %bitcast.29, f32[1,48]{1,0:T(1,128)} %bitcast.30, f32[1,48]{1,0:T(1,128)} %bitcast.31, f32[1,48]{1,0:T(1,128)} %bitcast.32, ...), custom_call_target="tpu_custom_call" | custom-call | tf_op jit(solution)/shard_map/prepare/pallas_call | solution.py:173
  12.4 0.0 collective-permute-done.2
  12.4 0.6 broadcast_select_fusion.token
  13.0 11.4 %all-to-all-start = ((f32[32,1,128]{2,1,0:T(1,128)}), f32[32,1,128]{2,1,0:T(1,128)S(1)}, u32[]{:S(2)}, u32[]{:S(2)}) async-start(f32[32,1,128]{2,1,0:T(1,128)} %bitcast.10), calls=%async_computation | async-start | bytes 32768 | tf_op jit(solution)/shard_map/all_to_all | solution.py:471
  24.4 0.0 collective-permute-done.y_far
  24.4 0.0 collective-permute-done.1.y_near
  24.4 0.7 %sides.1 = (f32[6,72,512]{2,1,0:T(8,128)}, f32[6,72,512]{2,1,0:T(8,128)}) custom-call(f32[6,72,512]{2,1,0:T(8,128)} %get-tuple-element.19.x_far, f32[6,72,512]{2,1,0:T(8,128)} %get-tuple-element.20.x_near, f32[16,8,512]{2,1,0:T(8,128)S(1)} %collective-permute-done.y_far, ...), custom_call_target="tpu_custom_call", output_to_operand_aliasing={{0}: (0, {}), {1}: (1, {})} | custom-call | tf_op jit(solution)/shard_map/sides/pallas_call | solution.py:202
  25.2 3.5 %collective-permute-start.3 = (f32[6,72,512]{2,1,0:T(8,128)}, f32[6,72,512]{2,1,0:T(8,128)}, u32[]{:S(2)}, u32[]{:S(2)}) collective-permute-start(f32[6,72,512]{2,1,0:T(8,128)} %get-tuple-element.22), channel_id=1, source_target_pairs={{8,16},{16,8},{24,32},{32,24},{40,48},{48,40},{56,64},{64,56},{72,... | collective-permute-start | bytes 2654216 | tf_op jit(solution)/shard_map/ppermute | solution.py:507
  28.7 0.1 collective-permute-start.4
  28.8 2.5 %all-to-all-done = f32[32,1,128]{2,1,0:T(1,128)S(1)} async-done(((f32[32,1,128]{2,1,0:T(1,128)}), f32[32,1,128]{2,1,0:T(1,128)S(1)}, u32[]{:S(2)}, u32[]{:S(2)}) %all-to-all-start) | async-done | bytes 16416 | tf_op jit(solution)/shard_map/all_to_all | solution.py:471
  31.3 3.8 %rates.1 = (f32[8,128]{1,0:T(8,128)}, s32[32,128]{1,0:T(8,128)S(1)}) custom-call(f32[32,128]{1,0:T(8,128)S(1)} %bitcast.24, f32[2,384,1536]{2,1,0:T(8,128)} %kernel_far.1), custom_call_target="tpu_custom_call" | custom-call | flops 999999995904 | bytes 6000000000 | tf_op jit(solution)/shard_map/rates/pallas_call | solution.py:268
  35.2 4.4 %all-to-all-start.1 = ((f32[8,1,128]{2,1,0:T(1,128)}), f32[8,1,128]{2,1,0:T(1,128)S(1)}, u32[]{:S(2)}, u32[]{:S(2)}) async-start(f32[8,1,128]{2,1,0:T(1,128)} %bitcast.13), calls=%async_computation.1 | async-start | bytes 8192 | tf_op jit(solution)/shard_map/all_to_all | solution.py:471
  39.5 0.3 collective-permute-done.3.x_far
  39.9 0.0 collective-permute-done.4.x_near
  39.9 10.2 %diffusion.1 = (f32[16,64,512]{2,1,0:T(8,128)}, f32[32,128]{1,0:T(8,128)S(1)}) custom-call(f32[16,64,512]{2,1,0:T(8,128)} %p_far.1, f32[16,64,512]{2,1,0:T(8,128)} %k_far.1, f32[16,8,512]{2,1,0:T(8,128)S(1)} %collective-permute-done.y_far, f32[16,8,512]{2,1,0:T(8,128)S(1)} %collective-permute-done.1.y_near, f32[6,72,512]{2,1,0:T(8,128)} %collective-permute-done.3.x_far, ...), custom_call_target="tpu_custom_call" | custom-call | flops 60000000 | bytes 12000000 | tf_op jit(solution)/shard_map/diffusion/pallas_call | solution.py:429
  50.1 0.0 all-to-all-done.1
  50.1 15.7 %all_to_all.33 = f32[32,1,128]{2,1,0:T(1,128)S(1)} all-to-all(f32[32,1,128]{2,1,0:T(1,128)S(1)} %bitcast.25), channel_id=1, replica_groups=mesh['gx'=32,'gy'=8] {'gx'}, dimensions={0} | all-to-all | bytes 32768 | tf_op jit(solution)/shard_map/all_to_all | solution.py:471
  65.8 0.6 friction.1
  (2 shorter events, 0.0 us)
Async XLA Ops:
  0.6 11.7 %collective-permute-start.2 = (f32[48]{0:T(128)}, f32[48]{0:T(128)S(1)}, u32[]{:S(2)}, u32[]{:S(2)}) collective-permute-start(f32[48]{0:T(128)} %param.15), channel_id=1, source_target_pairs={{0,160},{1,96},{2,128},{3,64},{4,0},{5,192},{6,32},{7,224},{8,168}... | collective-permute-start | bytes 584 | tf_op jit(solution)/shard_map/ppermute | solution.py:503
  9.6 14.8 %collective-permute-start = (f32[16,8,512]{2,1,0:T(8,128)S(1)}, f32[16,8,512]{2,1,0:T(8,128)S(1)}, u32[]{:S(2)}, u32[]{:S(2)}) collective-permute-start(f32[16,8,512]{2,1,0:T(8,128)S(1)} %get-tuple-element.17), channel_id=1, source_target_pairs={{1,2},{2,1},{3,4},{4,3},{5,6},{6,5},{9,10},{10,9},{11,12},{12,11},... | collective-permute-start | bytes 786440 | tf_op jit(solution)/shard_map/ppermute | solution.py:501
  10.3 14.1 %collective-permute-start.1 = (f32[16,8,512]{2,1,0:T(8,128)S(1)}, f32[16,8,512]{2,1,0:T(8,128)S(1)}, u32[]{:S(2)}, u32[]{:S(2)}) collective-permute-start(f32[16,8,512]{2,1,0:T(8,128)S(1)} %get-tuple-element.18), channel_id=1, source_target_pairs={{0,1},{1,0},{2,3},{3,2},{4,5},{5,4},{6,7},{7,6},{8,9},{9,8},{10,11... | collective-permute-start | bytes 786440 | tf_op jit(solution)/shard_map/ppermute | solution.py:501
  13.0 18.3 %all-to-all-start = ((f32[32,1,128]{2,1,0:T(1,128)}), f32[32,1,128]{2,1,0:T(1,128)S(1)}, u32[]{:S(2)}, u32[]{:S(2)}) async-start(f32[32,1,128]{2,1,0:T(1,128)} %bitcast.10), calls=%async_computation | async-start | bytes 32768 | tf_op jit(solution)/shard_map/all_to_all | solution.py:471
  25.2 14.7 %collective-permute-start.3 = (f32[6,72,512]{2,1,0:T(8,128)}, f32[6,72,512]{2,1,0:T(8,128)}, u32[]{:S(2)}, u32[]{:S(2)}) collective-permute-start(f32[6,72,512]{2,1,0:T(8,128)} %get-tuple-element.22), channel_id=1, source_target_pairs={{8,16},{16,8},{24,32},{32,24},{40,48},{48,40},{56,64},{64,56},{72,... | collective-permute-start | bytes 2654216 | tf_op jit(solution)/shard_map/ppermute | solution.py:507
  28.7 11.1 %collective-permute-start.4 = (f32[6,72,512]{2,1,0:T(8,128)}, f32[6,72,512]{2,1,0:T(8,128)}, u32[]{:S(2)}, u32[]{:S(2)}) collective-permute-start(f32[6,72,512]{2,1,0:T(8,128)} %get-tuple-element.23), channel_id=1, source_target_pairs={{0,8},{8,0},{16,24},{24,16},{32,40},{40,32},{48,56},{56,48},{64,72... | collective-permute-start | bytes 2654216 | tf_op jit(solution)/shard_map/ppermute | solution.py:507
  35.2 14.9 %all-to-all-start.1 = ((f32[8,1,128]{2,1,0:T(1,128)}), f32[8,1,128]{2,1,0:T(1,128)S(1)}, u32[]{:S(2)}, u32[]{:S(2)}) async-start(f32[8,1,128]{2,1,0:T(1,128)} %bitcast.13), calls=%async_computation.1 | async-start | bytes 8192 | tf_op jit(solution)/shard_map/all_to_all | solution.py:471
